TPU v7x, 32 devices: a whole 2x2x4 slice. The times are simulated.
32 devices in a mesh: section: 2 (over core), seq: 8 (over z, x), head: 2 (over y).
Axes of the slice: x: 2, y: 2, z: 4, core: 2. Of those that a mesh axis runs over, the one named last changes fastest.
Arguments:
- hidden_in: bfloat16 [4, 2048, 1024], P(None, 'seq'), may hold values from -6 to 6
- order: int32 [4], replicated, may hold values from 0 to 3, each once
- cotangent: bfloat16 [4, 2048, 1024], P(None, 'seq'), may hold values from -6 to 6
- norm_gain: float32 [2, 1024], P('section'), may hold values from 0.25 to 1.75
- w_z: bfloat16 [2, 1024, 2048], P('section', None, 'head'), may hold values from -0.1875 to 0.1875
- w_x: bfloat16 [2, 1024, 2048], P('section', None, 'head'), may hold values from -0.1875 to 0.1875
- w_bc: bfloat16 [2, 1024, 256], P('section'), may hold values from -0.1875 to 0.1875
- w_dt: bfloat16 [2, 1024, 32], P('section', None, 'head'), may hold values from -0.1875 to 0.1875
- dt_bias: float32 [2, 32], P('section', 'head'), may hold values from -12 to -3
- a_log: float32 [2, 32], P('section', 'head'), may hold values from -1 to 1
- d_skip: float32 [2, 32], P('section', 'head'), may hold values from 0.5 to 1.5
- conv_x: float32 [2, 4, 2048], P('section', None, 'head'), may hold values from -3 to 3
- conv_bias_x: float32 [2, 2048], P('section', 'head'), may hold values from -3 to 3
- conv_bc: float32 [2, 4, 256], P('section'), may hold values from -3 to 3
- conv_bias_bc: float32 [2, 256], P('section'), may hold values from -3 to 3
- mix_gain: float32 [2, 2048], P('section', 'head'), may hold values from 0.25 to 1.75
- w_out: bfloat16 [2, 2048, 1024], P('section', 'head'), may hold values from -0.125 to 0.125
Outputs:
- activations: bfloat16 [2, 4, 2048, 1024], P('section', None, 'seq')
- grads: float32 [2, 4, 2048, 1024], P('section', None, 'seq')
- grad_norm_gain: float32 [2, 1024], P('section')
- grad_w_z: float32 [2, 1024, 2048], P('section', None, 'head')
- grad_w_x: float32 [2, 1024, 2048], P('section', None, 'head')
- grad_w_bc: float32 [2, 1024, 256], P('section')
- grad_w_dt: float32 [2, 1024, 32], P('section', None, 'head')
- grad_dt_bias: float32 [2, 32], P('section', 'head')
- grad_a_log: float32 [2, 32], P('section', 'head')
- grad_d_skip: float32 [2, 32], P('section', 'head')
- grad_conv_x: float32 [2, 4, 2048], P('section', None, 'head')
- grad_conv_bias_x: float32 [2, 2048], P('section', 'head')
- grad_conv_bc: float32 [2, 4, 256], P('section')
- grad_conv_bias_bc: float32 [2, 256], P('section')
- grad_mix_gain: float32 [2, 2048], P('section', 'head')
- grad_w_out: float32 [2, 2048, 1024], P('section', 'head')
Inputs may be any that keep to these rules, and one draw needn't show every extreme that they name: `order`: each micro-batch takes a different sequence.
All inputs are finite; a program needn't handle non-finite values.
Results may differ from a plain program's by a relative error of at most 0.019.
Values may be sent and summed in bfloat16 or wider, within the bound.
No kernel may reach another device: no remote copies, remote signals or barrier semaphores. Data moves between devices by JAX's collectives and lax.ppermute only.
A program may use at most 192 MiB of HBM per device.

v0:
```python
import jax
import jax.numpy as jnp
from jax import lax
from jax.sharding import PartitionSpec as P

EPS = 1e-05
HIGH = lax.Precision.HIGHEST


def from_behind(block, axis, distance):
    devices = range(lax.axis_size(axis))
    route = [(i - distance, i) for i in devices if i - distance in devices]
    return lax.ppermute(block, axis, route)


def entering(part, axis, combine, identity, reverse):
    count = lax.axis_size(axis)
    place = lax.axis_index(axis)
    ahead = count - 1 - place if reverse else place
    gathered = jax.tree.map(lambda a: lax.all_gather(a, axis), part)
    state = jax.tree.map(lambda a, e: jnp.zeros_like(a) + jnp.asarray(e, a.dtype), part, identity)

    def one(hop, state):
        source = count - 1 - hop if reverse else hop
        return combine(
            state, jax.tree.map(lambda a: lax.dynamic_index_in_dim(a, source, 0, False), gathered)
        )

    return lax.fori_loop(0, ahead, one, state)


def shortened(array):
    return jax.tree.map(lambda a: a.astype(jnp.bfloat16) if a.dtype == jnp.float32 else a, array)


def matmul(left, right):
    return jnp.dot(left, right, preferred_element_type=jnp.float32)


def exact(left, right):
    return jnp.dot(left, right, precision=HIGH, preferred_element_type=jnp.float32)


def lead_dot(left, right):
    return lax.dot_general(
        left, right, (((0,), (0,)), ((), ())), preferred_element_type=jnp.float32
    )


def tail_dot(left, right):
    return lax.dot_general(
        left, right, (((1,), (1,)), ((), ())), preferred_element_type=jnp.float32
    )


def chain_join(earlier, later):
    return (earlier[0] * later[0], later[0][:, None, None] * earlier[1] + later[1])


def silu_slope(value):
    sigma = jax.nn.sigmoid(value)
    return sigma * (1.0 + value * (1.0 - sigma))


def conv_inputs(layer_weights, padded):
    kernel = jnp.concatenate([layer_weights[8], layer_weights[10]], 1)
    kernel_bias = jnp.concatenate([layer_weights[9], layer_weights[11]], 0)
    taps = kernel.shape[0]
    length = padded.shape[0] - taps + 1
    preact = kernel_bias + sum(
        (kernel[offset] * padded[offset : offset + length] for offset in range(taps))
    )
    return (kernel, preact)


def ssd_parts(layer_weights, activated, step_raw):
    inner = layer_weights[1].shape[1]
    heads = layer_weights[4].shape[1]
    state = layer_weights[3].shape[1] // 2
    length = activated.shape[0]
    signal = activated[:, :inner].reshape(length, heads, inner // heads)
    write_key = activated[:, inner : inner + state]
    read_key = activated[:, inner + state :]
    step = jax.nn.softplus(step_raw + layer_weights[5])
    rate = -jnp.exp(layer_weights[6])
    decay_sum = jnp.cumsum(rate * step, 0)
    index = jnp.arange(length)
    lower = (index[:, None] >= index[None, :])[None]
    diff = decay_sum.T[:, :, None] - decay_sum.T[:, None, :]
    decay = jnp.where(lower, jnp.exp(jnp.where(lower, diff, 0.0)), 0.0)
    gram = exact(read_key, write_key.T)
    return (signal, write_key, read_key, step, rate, decay_sum, decay, gram)


def layer_forward(entry, layer_weights):
    (
        gain,
        w_gate,
        w_signal,
        w_keys,
        w_step,
        step_bias,
        log_rate,
        skip,
        conv_signal,
        bias_signal,
        conv_keys,
        bias_keys,
        mix_gain,
        w_out,
    ) = layer_weights
    length = entry.shape[0]
    wide_in = entry.astype(jnp.float32)
    inverse_rms = lax.rsqrt(jnp.mean(wide_in * wide_in, -1, keepdims=True) + EPS)
    normed = (wide_in * inverse_rms * gain).astype(jnp.bfloat16)
    gate_in = matmul(normed, w_gate)
    joined = jnp.concatenate([matmul(normed, w_signal), matmul(normed, w_keys)], 1)
    step_raw = matmul(normed, w_step)
    taps = conv_signal.shape[0]
    before = from_behind(joined[length - taps + 1 :], "seq", 1)
    padded = jnp.concatenate([before, joined], 0)
    kernel, preact = conv_inputs(layer_weights, padded)
    activated = jax.nn.silu(preact)
    signal, write_key, read_key, step, rate, decay_sum, decay, gram = ssd_parts(
        layer_weights, activated, step_raw
    )
    mixing = gram[None] * decay * step.T[:, None, :]
    intra = jnp.einsum("hts,shp->thp", mixing, signal, precision=HIGH)
    tail = jnp.exp(decay_sum[-1][None, :] - decay_sum) * step
    local = jnp.einsum("sh,shp,sn->hpn", tail, signal, write_key, precision=HIGH)
    fade = jnp.exp(decay_sum[-1])
    start = entering(
        (fade, local), "seq", chain_join, (jnp.ones_like(fade), jnp.zeros_like(local)), False
    )[1]
    inter = jnp.exp(decay_sum)[:, :, None] * jnp.einsum(
        "tn,hpn->thp", read_key, start, precision=HIGH
    )
    ssd_out = (intra + inter + skip[None, :, None] * signal).reshape(length, -1)
    gated = ssd_out * jax.nn.silu(gate_in)
    total_inner = gated.shape[1] * lax.axis_size("head")
    squares = lax.psum(jnp.sum(gated * gated, -1), "head")
    mix_scale = lax.rsqrt(squares / total_inner + EPS)[:, None]
    mixed = (gated * mix_scale * mix_gain).astype(jnp.bfloat16)
    partial_value = matmul(mixed, w_out)
    output = (wide_in + lax.psum(partial_value, "head")).astype(jnp.bfloat16)
    kept = (
        entry,
        inverse_rms,
        normed,
        gate_in,
        padded,
        step_raw,
        start,
        ssd_out,
        gated,
        mix_scale,
        mixed,
    )
    return (output, kept)


def layer_backward(grad_out, kept, layer_weights):
    (
        gain,
        w_gate,
        w_signal,
        w_keys,
        w_step,
        step_bias,
        log_rate,
        skip,
        conv_signal,
        bias_signal,
        conv_keys,
        bias_keys,
        mix_gain,
        w_out,
    ) = layer_weights
    (
        entry,
        inverse_rms,
        normed,
        gate_in,
        padded,
        step_raw,
        start,
        ssd_out,
        gated,
        mix_scale,
        mixed,
    ) = kept
    length = entry.shape[0]
    grad_out_low = grad_out.astype(jnp.bfloat16)
    grad_w_out = lead_dot(mixed, grad_out_low)
    grad_mixed = tail_dot(grad_out_low, w_out)
    grad_mix_gain = jnp.sum(grad_mixed * gated * mix_scale, 0)
    weighted = grad_mixed * mix_gain
    total_inner = gated.shape[1] * lax.axis_size("head")
    along = lax.psum(jnp.sum(weighted * gated, -1), "head")
    grad_gated = mix_scale * weighted - gated * mix_scale**3 * (along / total_inner)[:, None]
    grad_y = grad_gated * jax.nn.silu(gate_in)
    grad_gate = grad_gated * ssd_out * silu_slope(gate_in)
    kernel, preact = conv_inputs(layer_weights, padded)
    activated = jax.nn.silu(preact)
    signal, write_key, read_key, step, rate, decay_sum, decay, gram = ssd_parts(
        layer_weights, activated, step_raw
    )
    grad_heads = grad_y.reshape(signal.shape)
    grad_skip = jnp.sum(grad_heads * signal, (0, 2))
    base = decay * step.T[:, None, :]
    mixing = gram[None] * base
    grad_signal = skip[None, :, None] * grad_heads + jnp.einsum(
        "hts,thp->shp", mixing, grad_heads, precision=HIGH
    )
    grad_mixing = jnp.einsum("thp,shp->hts", grad_heads, signal, precision=HIGH)
    grad_gram = jnp.sum(grad_mixing * base, 0)
    grad_read = exact(grad_gram, write_key)
    grad_write = exact(grad_gram.T, read_key)
    grad_log = grad_mixing * mixing
    grad_decay_sum = (jnp.sum(grad_log, 2) - jnp.sum(grad_log, 1)).T
    grad_step = jnp.sum(grad_mixing * gram[None] * decay, 1).T
    rise = jnp.exp(decay_sum)
    reach = jnp.einsum("tn,hpn->thp", read_key, start, precision=HIGH)
    grad_reach = grad_heads * rise[:, :, None]
    grad_read = grad_read + jnp.einsum("thp,hpn->tn", grad_reach, start, precision=HIGH)
    grad_start = jnp.einsum("thp,tn->hpn", grad_reach, read_key, precision=HIGH)
    grad_decay_sum = grad_decay_sum + jnp.sum(grad_heads * reach, 2) * rise
    fade = rise[-1]
    grad_local = entering(
        (fade, grad_start),
        "seq",
        chain_join,
        (jnp.ones_like(fade), jnp.zeros_like(grad_start)),
        True,
    )[1]
    last_row = (jnp.arange(length) == length - 1)[:, None]
    grad_decay_sum = grad_decay_sum + jnp.where(
        last_row, (jnp.sum(grad_local * start, (1, 2)) * fade)[None, :], 0.0
    )
    keep = jnp.exp(decay_sum[-1][None, :] - decay_sum)
    tail = keep * step
    spread = jnp.einsum("hpn,sn->shp", grad_local, write_key, precision=HIGH)
    grad_signal = grad_signal + tail[:, :, None] * spread
    grad_write = grad_write + jnp.einsum("sh,shp,hpn->sn", tail, signal, grad_local, precision=HIGH)
    grad_tail = jnp.sum(signal * spread, 2)
    grad_step = grad_step + grad_tail * keep
    grad_tail_log = grad_tail * tail
    grad_decay_sum = (
        grad_decay_sum
        - grad_tail_log
        + jnp.where(last_row, jnp.sum(grad_tail_log, 0)[None, :], 0.0)
    )
    grad_log_step = jnp.flip(jnp.cumsum(jnp.flip(grad_decay_sum, 0), 0), 0)
    grad_log_rate = jnp.sum(grad_log_step * step, 0) * rate
    grad_step = grad_step + grad_log_step * rate
    grad_step_raw = grad_step * jax.nn.sigmoid(step_raw + step_bias)
    grad_step_bias = jnp.sum(grad_step_raw, 0)
    grad_shared = lax.psum(
        jnp.concatenate([grad_write, grad_read], 1).astype(jnp.bfloat16), "head"
    ).astype(jnp.float32)
    grad_activated = jnp.concatenate([grad_signal.reshape(length, -1), grad_shared], 1)
    grad_pre = grad_activated * silu_slope(preact)
    taps = kernel.shape[0]
    grad_kernel = jnp.stack(
        [jnp.sum(grad_pre * padded[offset : offset + length], 0) for offset in range(taps)]
    )
    grad_kernel_bias = jnp.sum(grad_pre, 0)
    grad_padded = sum(
        (
            jnp.pad(kernel[offset] * grad_pre, ((offset, taps - 1 - offset), (0, 0)))
            for offset in range(taps)
        )
    )
    returned_rim = from_behind(grad_padded[: taps - 1], "seq", -1)
    grad_joined = grad_padded[taps - 1 :] + jnp.pad(returned_rim, ((length - taps + 1, 0), (0, 0)))
    inner = w_signal.shape[1]
    gate_low = grad_gate.astype(jnp.bfloat16)
    signal_low = grad_joined[:, :inner].astype(jnp.bfloat16)
    keys_low = grad_joined[:, inner:].astype(jnp.bfloat16)
    step_low = grad_step_raw.astype(jnp.bfloat16)
    own_terms = (
        tail_dot(gate_low, w_gate) + tail_dot(signal_low, w_signal) + tail_dot(step_low, w_step)
    )
    grad_normed = lax.psum(own_terms.astype(jnp.bfloat16), "head").astype(jnp.float32) + tail_dot(
        keys_low, w_keys
    )
    wide_in = entry.astype(jnp.float32)
    grad_gain = jnp.sum(grad_normed * wide_in * inverse_rms, 0)
    scaled = grad_normed * gain
    grad_in = inverse_rms * scaled - wide_in * inverse_rms**3 * jnp.mean(
        scaled * wide_in, -1, keepdims=True
    )
    terms = (
        grad_gain,
        lead_dot(normed, gate_low),
        lead_dot(normed, signal_low),
        lead_dot(normed, keys_low),
        lead_dot(normed, step_low),
        grad_step_bias,
        grad_log_rate,
        grad_skip,
        grad_kernel[:, :inner],
        grad_kernel_bias[:inner],
        grad_kernel[:, inner:],
        grad_kernel_bias[inner:],
        grad_mix_gain,
        grad_w_out,
    )
    return (grad_out + grad_in, terms)


def shards(
    hidden_in,
    order,
    cotangent,
    norm_gain,
    w_z,
    w_x,
    w_bc,
    w_dt,
    dt_bias,
    a_log,
    d_skip,
    conv_x,
    conv_bias_x,
    conv_bc,
    conv_bias_bc,
    mix_gain,
    w_out,
):
    layer_weights = tuple(
        (
            weight[0]
            for weight in (
                norm_gain,
                w_z,
                w_x,
                w_bc,
                w_dt,
                dt_bias,
                a_log,
                d_skip,
                conv_x,
                conv_bias_x,
                conv_bc,
                conv_bias_bc,
                mix_gain,
                w_out,
            )
        )
    )
    count = order.shape[0]
    first_section = lax.axis_index("section") == 0
    length = hidden_in.shape[1]
    features = hidden_in.shape[2]
    arrived = jnp.zeros((length, features), jnp.bfloat16)
    kept_list = []
    output_list = []
    for tick in range(count + 1):
        picked = lax.dynamic_index_in_dim(hidden_in, order[min(tick, count - 1)], 0, keepdims=False)
        entry = jnp.where(first_section, picked, arrived)
        output, kept = layer_forward(entry, layer_weights)
        kept_list.append(kept)
        output_list.append(output)
        if tick < count:
            arrived = from_behind(output, "section", 1)
    activations = jnp.stack(
        [
            jnp.where(first_section, output_list[index], output_list[index + 1])
            for index in range(count)
        ]
    )[None]
    returned = jnp.zeros((length, features), jnp.bfloat16)
    totals = None
    grad_list = []
    for tick in range(count + 1):
        later_grad = cotangent[min(tick, count - 1)].astype(jnp.float32)
        incoming = jnp.where(first_section, returned.astype(jnp.float32), later_grad)
        active = jnp.where(first_section, tick >= 1, tick < count)
        incoming = jnp.where(active, incoming, 0.0)
        kept = jax.tree.map(
            lambda early, late: jnp.where(first_section, early, late),
            kept_list[max(tick - 1, 0)],
            kept_list[min(tick + 1, count)],
        )
        grad_in, terms = layer_backward(incoming, kept, layer_weights)
        totals = terms if totals is None else jax.tree.map(jnp.add, totals, terms)
        grad_list.append(grad_in)
        if tick < count:
            returned = from_behind(grad_in.astype(jnp.bfloat16), "section", -1)
    grads = jnp.stack(
        [jnp.where(first_section, grad_list[index + 1], grad_list[index]) for index in range(count)]
    )[None]
    summed = jax.tree.map(lambda part: part.astype(jnp.float32), lax.psum(shortened(totals), "seq"))
    return (activations, grads) + tuple((total[None] for total in summed))


def solution(mesh):
    in_specs = (
        P(None, "seq", None),
        P(),
        P(None, "seq", None),
        P("section", None),
        P("section", None, "head"),
        P("section", None, "head"),
        P("section", None, None),
        P("section", None, "head"),
        P("section", "head"),
        P("section", "head"),
        P("section", "head"),
        P("section", None, "head"),
        P("section", "head"),
        P("section", None, None),
        P("section", None),
        P("section", "head"),
        P("section", "head", None),
    )
    out_specs = (
        P("section", None, "seq", None),
        P("section", None, "seq", None),
        P("section", None),
        P("section", None, "head"),
        P("section", None, "head"),
        P("section", None, None),
        P("section", None, "head"),
        P("section", "head"),
        P("section", "head"),
        P("section", "head"),
        P("section", None, "head"),
        P("section", "head"),
        P("section", None, None),
        P("section", None),
        P("section", "head"),
        P("section", "head", None),
    )
    return jax.shard_map(shards, mesh=mesh, in_specs=in_specs, out_specs=out_specs, check_vma=False)
```

profile of v0, /device:TPU:0, one launch (start us, length us, event | category | flops | bytes accessed | tf_op | source)
XLA Modules:
  0.0 2050.2 jit_solution(7456876298540588762)
XLA Ops:
  35.8 18.7 all-gather.10
  55.9 6.7 fusion.193
  62.6 47.0 %all-gather.31.cloned.1.call-done = f32[128,64,128]{2,1,0:T(8,128)} async-done(((f32[16,64,128]{2,1,0:T(8,128)}), f32[128,64,128]{2,1,0:T(8,128)}) %all-gather.31.cloned.1.call-update) | async-done | bytes 4194320 | tf_op jit(solution)/shard_map/all_gather | solution.py:20
  119.8 4.9 psum.273
  128.7 46.6 %all-reduce.47.cloned.1.call-done = f32[256,1024]{1,0:T(8,128)} async-done(((f32[256,1024]{1,0:T(8,128)}), f32[256,1024]{1,0:T(8,128)}) %all-reduce.47.cloned.1.call-update) | async-done | bytes 1048592 | tf_op jit(solution)/shard_map/psum | solution.py:145
  204.3 18.4 all-gather.11
  224.0 6.8 fusion.196
  230.8 46.1 %all-gather.33.cloned.1.call-done = f32[128,64,128]{2,1,0:T(8,128)} async-done(((f32[16,64,128]{2,1,0:T(8,128)}), f32[128,64,128]{2,1,0:T(8,128)}) %all-gather.33.cloned.1.call-update) | async-done | bytes 4194320 | tf_op jit(solution)/shard_map/all_gather | solution.py:20
  287.8 4.9 psum.275
  300.4 46.6 %all-reduce.49.cloned.1.call-done = f32[256,1024]{1,0:T(8,128)} async-done(((f32[256,1024]{1,0:T(8,128)}), f32[256,1024]{1,0:T(8,128)}) %all-reduce.49.cloned.1.call-update) | async-done | bytes 1048592 | tf_op jit(solution)/shard_map/psum | solution.py:145
  383.2 18.9 all-gather.12
  404.1 7.2 fusion.199
  411.3 40.5 %all-gather.35.cloned.1.call-done = f32[128,64,128]{2,1,0:T(8,128)} async-done(((f32[16,64,128]{2,1,0:T(8,128)}), f32[128,64,128]{2,1,0:T(8,128)}) %all-gather.35.cloned.1.call-update) | async-done | bytes 4194320 | tf_op jit(solution)/shard_map/all_gather | solution.py:20
  463.7 5.8 all-reduce.27
  470.8 6.0 multiply_reduce_fusion.39
  484.0 37.8 %all-gather.15 = f32[8,1,16]{2,1,0:T(1,128)} all-gather(f32[1,1,16]{2,1,0:T(1,128)S(1)} %bitcast.1414), channel_id=1, replica_groups=mesh['section'=2,'seq'=8,'head'=2] {'seq'}, dimensions={0}, use_global_device_ids=true | all-gather | bytes 576 | tf_op jit(solution)/shard_map/all_gather | solution.py:20
  531.0 7.4 fusion.60
  538.4 35.3 %all-gather.41.cloned.1.call-done = f32[128,64,128]{2,1,0:T(8,128)} async-done(((f32[16,64,128]{2,1,0:T(8,128)}), f32[128,64,128]{2,1,0:T(8,128)}) %all-gather.41.cloned.1.call-update) | async-done | bytes 4194320 | tf_op jit(solution)/shard_map/all_gather | solution.py:20
  574.6 19.7 while.135
  613.5 5.9 fusion.275
  636.6 5.5 multiply_reduce_fusion.29
  650.4 18.3 all-reduce.51.cloned.1.call-done
  675.9 24.4 %all-reduce.59.cloned.1.call-done = bf16[256,1024]{1,0:T(8,128)(2,1)} async-done(((bf16[256,1024]{1,0:T(8,128)(2,1)}), bf16[256,1024]{1,0:T(8,128)(2,1)}) %all-reduce.59.cloned.1.call-update) | async-done | bytes 524304 | tf_op jit(solution)/shard_map/psum | solution.py:284
  740.0 18.6 all-gather.13
  760.7 7.3 fusion.202
  772.1 30.6 %all-gather.37.cloned.1.call-done = f32[128,64,128]{2,1,0:T(8,128)} async-done(((f32[16,64,128]{2,1,0:T(8,128)}), f32[128,64,128]{2,1,0:T(8,128)}) %all-gather.37.cloned.1.call-update) | async-done | bytes 4194320 | tf_op jit(solution)/shard_map/all_gather | solution.py:20
  814.6 5.6 all-reduce.26
  822.1 5.9 multiply_reduce_fusion.38
  836.6 38.0 %all-gather.16 = f32[8,1,16]{2,1,0:T(1,128)} all-gather(f32[1,1,16]{2,1,0:T(1,128)S(1)} %bitcast.1415), channel_id=1, replica_groups=mesh['section'=2,'seq'=8,'head'=2] {'seq'}, dimensions={0}, use_global_device_ids=true | all-gather | bytes 576 | tf_op jit(solution)/shard_map/all_gather | solution.py:20
  882.9 7.4 fusion.62
  890.3 34.8 %all-gather.43.cloned.1.call-done = f32[128,64,128]{2,1,0:T(8,128)} async-done(((f32[16,64,128]{2,1,0:T(8,128)}), f32[128,64,128]{2,1,0:T(8,128)}) %all-gather.43.cloned.1.call-update) | async-done | bytes 4194320 | tf_op jit(solution)/shard_map/all_gather | solution.py:20
  925.9 19.7 while.136
  965.3 5.9 fusion.269
  1002.9 17.1 all-reduce.53.cloned.1.call-done
  1025.2 26.3 %all-reduce.63.cloned.1.call-done = bf16[256,1024]{1,0:T(8,128)(2,1)} async-done(((bf16[256,1024]{1,0:T(8,128)(2,1)}), bf16[256,1024]{1,0:T(8,128)(2,1)}) %all-reduce.63.cloned.1.call-update) | async-done | bytes 524304 | tf_op jit(solution)/shard_map/psum | solution.py:284
  1091.4 18.0 all-gather.14
  1110.8 7.0 fusion.205
  1121.9 33.0 %all-gather.39.cloned.1.call-done = f32[128,64,128]{2,1,0:T(8,128)} async-done(((f32[16,64,128]{2,1,0:T(8,128)}), f32[128,64,128]{2,1,0:T(8,128)}) %all-gather.39.cloned.1.call-update) | async-done | bytes 4194320 | tf_op jit(solution)/shard_map/all_gather | solution.py:20
  1165.9 5.7 all-reduce.25
  1171.6 5.4 multiply_reduce_fusion.37
  1181.7 26.4 %all-gather.17 = f32[8,1,16]{2,1,0:T(1,128)} all-gather(f32[1,1,16]{2,1,0:T(1,128)S(1)} %bitcast.1416), channel_id=1, replica_groups=mesh['section'=2,'seq'=8,'head'=2] {'seq'}, dimensions={0}, use_global_device_ids=true | all-gather | bytes 576 | tf_op jit(solution)/shard_map/all_gather | solution.py:20
  1219.8 7.4 fusion.64
  1227.2 34.2 %all-gather.45.cloned.1.call-done = f32[128,64,128]{2,1,0:T(8,128)} async-done(((f32[16,64,128]{2,1,0:T(8,128)}), f32[128,64,128]{2,1,0:T(8,128)}) %all-gather.45.cloned.1.call-update) | async-done | bytes 4194320 | tf_op jit(solution)/shard_map/all_gather | solution.py:20
  1262.3 19.7 while.137
  1298.0 6.8 fusion.263
  1324.9 5.3 multiply_reduce_fusion.21
  1341.9 24.6 %all-reduce.67.cloned.1.call-done = bf16[256,1024]{1,0:T(8,128)(2,1)} async-done(((bf16[256,1024]{1,0:T(8,128)(2,1)}), bf16[256,1024]{1,0:T(8,128)(2,1)}) %all-reduce.67.cloned.1.call-update) | async-done | bytes 524304 | tf_op jit(solution)/shard_map/psum | solution.py:284
  1382.2 5.7 psum.292
  1388.6 5.3 multiply_reduce_fusion.36
  1403.7 21.4 %all-gather.18 = f32[8,1,16]{2,1,0:T(1,128)} all-gather(f32[1,1,16]{2,1,0:T(1,128)S(1)} %bitcast.1417), channel_id=1, replica_groups=mesh['section'=2,'seq'=8,'head'=2] {'seq'}, dimensions={0}, use_global_device_ids=true | all-gather | bytes 576 | tf_op jit(solution)/shard_map/all_gather | solution.py:20
  1434.9 7.4 fusion.66
  1442.3 30.8 %all-gather.47.cloned.1.call-done = f32[128,64,128]{2,1,0:T(8,128)} async-done(((f32[16,64,128]{2,1,0:T(8,128)}), f32[128,64,128]{2,1,0:T(8,128)}) %all-gather.47.cloned.1.call-update) | async-done | bytes 4194320 | tf_op jit(solution)/shard_map/all_gather | solution.py:20
  1473.9 19.5 while.138
  1509.1 6.8 fusion.257
  1549.0 17.0 all-gather.19
  1594.4 5.4 multiply_reduce_fusion.35
  1613.8 7.3 fusion.68
  1652.4 49.9 %all-gather.49.cloned.1.call-done = f32[128,64,128]{2,1,0:T(8,128)} async-done(((f32[16,64,128]{2,1,0:T(8,128)}), f32[128,64,128]{2,1,0:T(8,128)}) %all-gather.49.cloned.1.call-update) | async-done | bytes 4194320 | tf_op jit(solution)/shard_map/all_gather | solution.py:20
  1703.1 19.8 while.139
  1738.2 6.0 fusion.251
  1772.6 8.4 fusion.192
  1788.6 9.5 all-reduce.75.cloned.1.call-done
  1801.1 39.9 %all-reduce.28 = (bf16[1,1024]{1,0:T(2,128)(2,1)S(1)}, bf16[1,1024,16]{1,2,0:T(8,128)(2,1)S(1)}, bf16[1,16]{1,0:T(2,128)(2,1)S(1)}, bf16[1,16]{1,0:T(2,128)(2,1)...) all-reduce(bf16[1,1024]{1,0:T(2,128)(2,1)S(1)} %broadcast_in_dim.53, ...), channel_id=1, replica_groups=mesh['section'=2,'seq'=8,'head'=2] {'seq'}, use_global_device_ids=true, to_apply=%region_140.141 | all-reduce | flops 24880 | bytes 99520 | tf_op jit(solution)/shard_map/psum | solution.py:394
  1852.0 180.9 %all-reduce.77.cloned.1.call-done = (bf16[1,1024,1024]{2,1,0:T(8,128)(2,1)}, bf16[1,1024,1024]{2,1,0:T(8,128)(2,1)}, bf16[1,1024,256]{2,1,0:T(8,128)(2,1)}, bf16[1,1024,1024]{2,1,0:T(8,128)(2,1)}) async-done(((bf16[1,1024,1024]{2,1,0:T(8,128)(2,1)}, bf16[1,1024,1024]{2,1,0:T(8,128)(2,1)}, bf16[1,1024,256]{2,1,0:T(8,128)(2,1)}, bf16[1,1024,1024]{2,1,0:T(8,128)(2,1)}), (bf16[1,1024,1024]{2,1,0:T(8,128)(2,1)}, ...) | async-done | bytes 6815760 | tf_op jit(solution)/shard_map/psum | solution.py:394
  (1412 shorter events, 790.4 us)
Async XLA Ops:
  7.2 119.7 %copy-start = (bf16[1,1024,1024]{2,1,0:T(8,128)(2,1)S(1)}, bf16[1,1024,1024]{2,1,0:T(8,128)(2,1)}, u32[]{:S(2)}) copy-start(bf16[1,1024,1024]{2,1,0:T(8,128)(2,1)} %param.53) | copy-start | bytes 6291460
  7.2 102.4 %all-gather.31.cloned.1.call-start = ((), (), s32[]{:S(2)}) async-start(), calls=%async_computation.15 | async-start | bytes 4718592 | tf_op jit(solution)/shard_map/all_gather | solution.py:20
  12.1 103.3 %copy-start.352 = (f32[256]{0:T(256)}, f32[256]{0:T(256)S(1)}, u32[]{:S(2)}) copy-start(f32[256]{0:T(256)S(1)} %add_rsqrt_fusion.9) | copy-start | bytes 3076
  16.8 10.9 collective-permute-start
  21.6 358.1 %copy-start.214 = (f32[16]{0:T(128)}, f32[16]{0:T(128)S(1)}, u32[]{:S(2)}) copy-start(f32[16]{0:T(128)S(1)} %negate_bitcast_fusion) | copy-start | bytes 196
  35.7 139.6 %all-reduce.47.cloned.1.call-start = ((), (), s32[]{:S(2)}) async-start(), calls=%async_computation | async-start | bytes 2097152 | tf_op jit(solution)/shard_map/psum | solution.py:145
  128.6 148.3 %all-gather.33.cloned.1.call-start = ((), (), s32[]{:S(2)}) async-start(), calls=%async_computation.16 | async-start | bytes 4718592 | tf_op jit(solution)/shard_map/all_gather | solution.py:20
  176.8 4.6 collective-permute-start.1
  182.9 100.8 %copy-start.247 = (f32[256]{0:T(256)}, f32[256]{0:T(256)S(1)}, u32[]{:S(2)}) copy-start(f32[256]{0:T(256)S(1)} %add_rsqrt_fusion.7) | copy-start | bytes 3076
  184.5 177.4 %copy-start.177 = (f32[256,16]{0,1:T(8,128)}, f32[256,16]{0,1:T(8,128)S(1)}, u32[]{:S(2)}) copy-start(f32[256,16]{0,1:T(8,128)S(1)} %fusion.629) | copy-start | bytes 49156
  185.2 10.9 collective-permute-start.2
  204.2 142.8 %all-reduce.49.cloned.1.call-start = ((), (), s32[]{:S(2)}) async-start(), calls=%async_computation.1 | async-start | bytes 2097152 | tf_op jit(solution)/shard_map/psum | solution.py:145
  300.4 46.6 %copy-start.158 = (bf16[256,1024]{1,0:T(8,128)(2,1)S(1)}, bf16[256,1024]{1,0:T(8,128)(2,1)}, u32[]{:S(2)}) copy-start(bf16[256,1024]{1,0:T(8,128)(2,1)} %copy-done.157) | copy-start | bytes 1572868
  300.4 151.5 %all-gather.35.cloned.1.call-start = ((), (), s32[]{:S(2)}) async-start(), calls=%async_computation.17 | async-start | bytes 4718592 | tf_op jit(solution)/shard_map/all_gather | solution.py:20
  349.6 3.6 collective-permute-start.3
  355.4 103.6 %copy-start.249 = (f32[256]{0:T(256)}, f32[256]{0:T(256)S(1)}, u32[]{:S(2)}) copy-start(f32[256]{0:T(256)S(1)} %get-tuple-element.1114) | copy-start | bytes 3076
  357.6 7.9 collective-permute-start.4
  379.7 194.0 %all-gather.41.cloned.1.call-start = ((), (), s32[]{:S(2)}) async-start(), calls=%async_computation.20 | async-start | bytes 4718592 | tf_op jit(solution)/shard_map/all_gather | solution.py:20
  383.2 241.1 %copy-start.243 = (f32[16,2]{0,1:T(2,128)}, f32[16,2]{0,1:T(2,128)S(1)}, u32[]{:S(2)}) copy-start(f32[16,2]{0,1:T(2,128)S(1)} %slice.660) | copy-start | bytes 388
  482.5 153.2 %all-reduce.57.cloned.1.call-start = ((), (), s32[]{:S(2)}) async-start(), calls=%async_computation.5 | async-start | bytes 262144 | tf_op jit(solution)/shard_map/psum | solution.py:258
  522.7 78.7 %copy-start.346 = (f32[16]{0:T(128)}, f32[16]{0:T(128)S(1)}, u32[]{:S(2)}) copy-start(f32[16]{0:T(128)S(1)} %slice_reduce_fusion.19) | copy-start | bytes 196
  607.4 61.2 %all-reduce.51.cloned.1.call-start = ((), (), s32[]{:S(2)}) async-start(), calls=%async_computation.2 | async-start | bytes 2097152 | tf_op jit(solution)/shard_map/psum | solution.py:145
  610.2 90.0 %all-reduce.59.cloned.1.call-start = ((), (), s32[]{:S(2)}) async-start(), calls=%async_computation.6 | async-start | bytes 1048576 | tf_op jit(solution)/shard_map/psum | solution.py:284
  642.5 5.7 collective-permute-start.9
  650.3 152.5 %all-gather.37.cloned.1.call-start = ((), (), s32[]{:S(2)}) async-start(), calls=%async_computation.18 | async-start | bytes 4718592 | tf_op jit(solution)/shard_map/all_gather | solution.py:20
  671.4 30.5 %copy-start.316 = (f32[256]{0:T(256)S(1)}, f32[256]{0:T(256)}, u32[]{:S(2)}) copy-start(f32[256]{0:T(256)} %get-tuple-element.1113) | copy-start | bytes 3076
  671.4 30.5 %collective-permute-start.5 = (bf16[256,1024]{1,0:T(8,128)(2,1)}, bf16[256,1024]{1,0:T(8,128)(2,1)}, u32[]{:S(2)}, u32[]{:S(2)}) collective-permute-start(bf16[256,1024]{1,0:T(8,128)(2,1)} %get-tuple-element.940), channel_id=1, source_target_pairs={{0,16},{1,17},{2,18},{3,19},{4,20},{5,21},{6,22},{7,23},{8,24},{9,... | collective-permute-start | bytes 1572872 | tf_op jit(solution)/shard_map/ppermute | solution.py:13
  708.5 12.0 collective-permute-start.6
  730.6 194.4 %all-gather.43.cloned.1.call-start = ((), (), s32[]{:S(2)}) async-start(), calls=%async_computation.21 | async-start | bytes 4718592 | tf_op jit(solution)/shard_map/all_gather | solution.py:20
  734.1 33.9 %collective-permute-start.10 = (bf16[256,1024]{1,0:T(8,128)(2,1)}, bf16[256,1024]{1,0:T(8,128)(2,1)}, u32[]{:S(2)}, u32[]{:S(2)}) collective-permute-start(bf16[256,1024]{1,0:T(8,128)(2,1)} %fusion.762), channel_id=1, source_target_pairs={{16,0},{17,1},{18,2},{19,3},{20,4},{21,5},{22,6},{23,7},{24,8},{25... | collective-permute-start | bytes 1572872 | tf_op jit(solution)/shard_map/ppermute | solution.py:13
  833.6 156.8 %all-reduce.61.cloned.1.call-start = ((), (), s32[]{:S(2)}) async-start(), calls=%async_computation.7 | async-start | bytes 262144 | tf_op jit(solution)/shard_map/psum | solution.py:258
  958.8 61.2 %all-reduce.53.cloned.1.call-start = ((), (), s32[]{:S(2)}) async-start(), calls=%async_computation.3 | async-start | bytes 2097152 | tf_op jit(solution)/shard_map/psum | solution.py:145
  961.6 89.9 %all-reduce.63.cloned.1.call-start = ((), (), s32[]{:S(2)}) async-start(), calls=%async_computation.8 | async-start | bytes 1048576 | tf_op jit(solution)/shard_map/psum | solution.py:284
  995.0 5.7 collective-permute-start.11
  1002.9 48.6 %copy-start.76 = (bf16[1,1024,256]{2,1,0:T(8,128)(2,1)S(1)}, bf16[1,1024,256]{2,1,0:T(8,128)(2,1)}, u32[]{:S(2)}) copy-start(bf16[1,1024,256]{2,1,0:T(8,128)(2,1)} %param.43) | copy-start | bytes 1572868
  1002.9 152.0 %all-gather.39.cloned.1.call-start = ((), (), s32[]{:S(2)}) async-start(), calls=%async_computation.19 | async-start | bytes 4718592 | tf_op jit(solution)/shard_map/all_gather | solution.py:20
  1022.7 30.3 %copy-start.50 = (bf16[256,1024]{1,0:T(8,128)(2,1)S(1)}, bf16[256,1024]{1,0:T(8,128)(2,1)}, u32[]{:S(2)}) copy-start(bf16[256,1024]{1,0:T(8,128)(2,1)} %copy-done.49) | copy-start | bytes 1572868
  1022.7 30.3 %copy-start.342 = (f32[256]{0:T(256)S(1)}, f32[256]{0:T(256)}, u32[]{:S(2)}) copy-start(f32[256]{0:T(256)} %get-tuple-element.945) | copy-start | bytes 3076
  1022.7 30.2 %collective-permute-start.7 = (bf16[256,1024]{1,0:T(8,128)(2,1)}, bf16[256,1024]{1,0:T(8,128)(2,1)}, u32[]{:S(2)}, u32[]{:S(2)}) collective-permute-start(bf16[256,1024]{1,0:T(8,128)(2,1)} %get-tuple-element.942), channel_id=1, source_target_pairs={{0,16},{1,17},{2,18},{3,19},{4,20},{5,21},{6,22},{7,23},{8,24},{9,... | collective-permute-start | bytes 1572872 | tf_op jit(solution)/shard_map/ppermute | solution.py:13
  1057.2 104.7 %copy-start.253 = (f32[256]{0:T(256)}, f32[256]{0:T(256)S(1)}, u32[]{:S(2)}) copy-start(f32[256]{0:T(256)S(1)} %get-tuple-element.1107) | copy-start | bytes 3076
  1060.0 11.1 collective-permute-start.8
  1082.8 178.6 %all-gather.45.cloned.1.call-start = ((), (), s32[]{:S(2)}) async-start(), calls=%async_computation.22 | async-start | bytes 4718592 | tf_op jit(solution)/shard_map/all_gather | solution.py:20
  1088.6 29.2 %collective-permute-start.12 = (bf16[256,1024]{1,0:T(8,128)(2,1)}, bf16[256,1024]{1,0:T(8,128)(2,1)}, u32[]{:S(2)}, u32[]{:S(2)}) collective-permute-start(bf16[256,1024]{1,0:T(8,128)(2,1)} %convert_element_type.377), channel_id=1, source_target_pairs={{16,0},{17,1},{18,2},{19,3},{20,4},{21,5},{22,6},{23,7},{24,8},{25... | collective-permute-start | bytes 1572872 | tf_op jit(solution)/shard_map/ppermute | solution.py:13
  1109.4 72.1 %copy-start.170 = (f32[256,16]{0,1:T(8,128)}, f32[256,16]{0,1:T(8,128)S(1)}, u32[]{:S(2)}) copy-start(f32[256,16]{0,1:T(8,128)S(1)} %bitcast_exponential_fusion.2) | copy-start | bytes 49156
  1178.6 31.0 %copy-start.63 = (f32[256,1024]{0,1:T(8,128)}, f32[256,1024]{0,1:T(8,128)S(1)}, u32[]{:S(2)}) copy-start(f32[256,1024]{0,1:T(8,128)S(1)} %copy.403) | copy-start | bytes 3145732
  1181.5 142.6 %all-reduce.65.cloned.1.call-start = ((), (), s32[]{:S(2)}) async-start(), calls=%async_computation.9 | async-start | bytes 262144 | tf_op jit(solution)/shard_map/psum | solution.py:258
  1297.5 69.0 %all-reduce.67.cloned.1.call-start = ((), (), s32[]{:S(2)}) async-start(), calls=%async_computation.10 | async-start | bytes 1048576 | tf_op jit(solution)/shard_map/psum | solution.py:284
  1332.8 5.7 collective-permute-start.13
  1340.6 132.5 %all-gather.47.cloned.1.call-start = ((), (), s32[]{:S(2)}) async-start(), calls=%async_computation.23 | async-start | bytes 4718592 | tf_op jit(solution)/shard_map/all_gather | solution.py:20
  1373.8 4.1 collective-permute-start.14
  1399.5 131.7 %all-reduce.69.cloned.1.call-start = ((), (), s32[]{:S(2)}) async-start(), calls=%async_computation.11 | async-start | bytes 262144 | tf_op jit(solution)/shard_map/psum | solution.py:258
  1508.8 60.8 %all-reduce.71.cloned.1.call-start = ((), (), s32[]{:S(2)}) async-start(), calls=%async_computation.12 | async-start | bytes 1048576 | tf_op jit(solution)/shard_map/psum | solution.py:284
  1535.8 5.7 collective-permute-start.15
  1543.7 82.2 %all-reduce.55.cloned.1.call-start = ((), (), s32[]{:S(2)}) async-start(), calls=%async_computation.4 | async-start | bytes 2097152 | tf_op jit(solution)/shard_map/psum | solution.py:145
  1548.8 183.4 %copy-start.240 = (f32[16,2]{0,1:T(2,128)}, f32[16,2]{0,1:T(2,128)S(1)}, u32[]{:S(2)}) copy-start(f32[16,2]{0,1:T(2,128)S(1)} %slice.731) | copy-start | bytes 388
  1575.0 4.4 collective-permute-start.16
  1576.6 37.1 %copy-start.302 = (f32[16,256]{1,0:T(8,128)}, f32[16,256]{1,0:T(8,128)S(1)}, u32[]{:S(2)}) copy-start(f32[16,256]{1,0:T(8,128)S(1)} %get-tuple-element.1072) | copy-start | bytes 49156
  1584.8 117.5 %all-gather.49.cloned.1.call-start = ((), (), s32[]{:S(2)}) async-start(), calls=%async_computation.24 | async-start | bytes 4718592 | tf_op jit(solution)/shard_map/all_gather | solution.py:20
  1607.9 149.8 %all-reduce.73.cloned.1.call-start = ((), (), s32[]{:S(2)}) async-start(), calls=%async_computation.13 | async-start | bytes 262144 | tf_op jit(solution)/shard_map/psum | solution.py:258
  1738.1 60.0 %all-reduce.75.cloned.1.call-start = ((), (), s32[]{:S(2)}) async-start(), calls=%async_computation.14 | async-start | bytes 1048576 | tf_op jit(solution)/shard_map/psum | solution.py:284
  1762.4 5.7 collective-permute-start.17
  1770.2 262.8 %all-reduce.77.cloned.1.call-start = ((), (), s32[]{:S(2)}) async-start(), calls=%async_computation.25 | async-start | bytes 13631488 | tf_op jit(solution)/shard_map/psum | solution.py:394
  1798.2 48.6 %copy-start.324 = (f32[256]{0:T(256)S(1)}, f32[256]{0:T(256)}, u32[]{:S(2)}) copy-start(f32[256]{0:T(256)} %get-tuple-element.897) | copy-start | bytes 3076
  1798.2 48.6 %copy-start.349 = (f32[256]{0:T(256)S(1)}, f32[256]{0:T(256)}, u32[]{:S(2)}) copy-start(f32[256]{0:T(256)} %get-tuple-element.896) | copy-start | bytes 3076
  (357 other events, 1558.9 us)
Sparse Core Ops, SparseCore 0:
  35.8 73.7 all-gather.30
  128.7 46.4 all-reduce.46
  204.3 72.5 all-gather.32
  300.5 46.4 all-reduce.48
  379.8 71.9 all-gather.34
  482.7 90.9 all-gather.40
  607.5 18.6 all-reduce.56
  628.6 40.0 all-reduce.50
  671.6 28.5 all-reduce.58
  730.8 71.9 all-gather.36
  833.7 91.3 all-gather.42
  958.9 18.6 all-reduce.60
  979.9 40.0 all-reduce.52
  1022.8 28.5 all-reduce.62
  1082.9 71.9 all-gather.38
  1181.6 79.7 all-gather.44
  1297.6 18.6 all-reduce.64
  1340.7 25.8 all-reduce.66
  1399.6 73.4 all-gather.46
  1508.9 18.7 all-reduce.68
  1543.8 25.8 all-reduce.70
  1584.9 40.9 all-reduce.54
  1628.8 73.3 all-gather.48
  1738.3 18.7 all-reduce.72
  1770.3 27.8 all-reduce.74
  1802.5 230.4 all-reduce.76
where the time goes:
time: 2070 us; the launch traced here: 2050 us
  waiting for transfers between devices  802 us (39%)
  matrix products  379 us (18%)
  other arithmetic  316 us (15%)
  blocking collectives  311 us (15%)
  local copies, waits for them, and re-layouts  169 us (8%)
  starting transfers between devices  45.5 us (2%)
  between operations  26.8 us (1%)
    all_gather x10, waiting for transfers between devices, entering(): gathered = jax.tree.map(lambda a: lax.all_gather(a, axis), part)  382 us
    all_gather x10, blocking collectives, entering(): gathered = jax.tree.map(lambda a: lax.all_gather(a, axis), part)  233 us
    psum x1, waiting for transfers between devices, shards(): lax.psum(shortened(totals), 'seq')  181 us
    psum x5, waiting for transfers between devices, layer_forward(): output = (wide_in + lax.psum(partial_value, 'head')).astype(jnp.bfloat16)  131 us
    psum x5, waiting for transfers between devices, layer_backward(): lax.psum(own_terms.astype(jnp.bfloat16), 'head').astype(jnp.float32)  88.4 us
    add x35, other arithmetic, chain_join(): later[0][:, None, None] * earlier[1] + later[1]  74.1 us
    dot_general x25, matrix products, tail_dot(): lax.dot_general(left, right, (((1,), (1,)), ((), ())), preferred_element_...  58.8 us
    dot_general x25, matrix products, lead_dot(): lax.dot_general(left, right, (((0,), (0,)), ((), ())), preferred_element_...  47.7 us
  transfers between devices with their start and end apart: 44, of which 27 were waited for; matrix products, arithmetic and copies ran while one was open for 21% of the time, Pallas kernels for 0%

commit v1 on v0

v1 whole, which is shorter than its diff:
```python
import jax
import jax.numpy as jnp
from jax import lax
from jax.sharding import PartitionSpec as P

EPS = 1e-05
F32 = jnp.float32
BF16 = jnp.bfloat16


def exchange(block, axis, bit):
    route = [(i, i ^ bit) for i in range(lax.axis_size(axis))]
    return lax.ppermute(block, axis, route)


def shifted(block, axis, distance):
    devices = range(lax.axis_size(axis))
    route = [(i - distance, i) for i in devices if i - distance in devices]
    return lax.ppermute(block, axis, route)


def head_sum(part):
    bit = 1
    total = part.astype(F32)
    while bit < lax.axis_size("head"):
        low = total.astype(BF16)
        total = low.astype(F32) + exchange(low, "head", bit).astype(F32)
        bit *= 2
    return total


def head_sum_wide(total):
    bit = 1
    while bit < lax.axis_size("head"):
        total = total + exchange(total, "head", bit)
        bit *= 2
    return total


def matmul(left, right):
    return jnp.dot(left, right, preferred_element_type=F32)


def lead_dot(left, right):
    return lax.dot_general(
        left, right, (((0,), (0,)), ((), ())), preferred_element_type=F32
    )


def tail_dot(left, right):
    return lax.dot_general(
        left, right, (((1,), (1,)), ((), ())), preferred_element_type=F32
    )


def low(value):
    return value.astype(BF16)


def silu_slope(value):
    sigma = jax.nn.sigmoid(value)
    return sigma * (1.0 + value * (1.0 - sigma))


def send_chunks(chunks):
    me = lax.axis_index("seq")
    pick = lambda d: lax.dynamic_index_in_dim(chunks, me ^ d, 0, False)
    return [pick(0)] + [exchange(pick(d), "seq", d) for d in range(1, chunks.shape[0])]


def scan_states(fade, local, fades):
    blocks = lax.axis_size("seq")
    me = lax.axis_index("seq")
    reverse = fades is not None
    width, state = local.shape
    rows = width // blocks
    message = low(local).reshape(blocks, rows, state)
    if fades is None:
        heads = fade.shape[0]
        per = max(1, heads // blocks)
        spread = jnp.repeat(fade, blocks * per // heads).reshape(blocks, per, 1)
        high = low(spread).astype(F32)
        pair = jnp.concatenate([high, spread - high], 1)
        tail = jnp.pad(low(jnp.broadcast_to(pair, (blocks, 2 * per, state))), ((0, 0), (0, 16 - 2 * per), (0, 0)))
        message = jnp.concatenate([message, tail], 1)
    arrived = jnp.stack(send_chunks(message))
    if fades is None:
        fades = (arrived[:, rows : rows + per].astype(F32) + arrived[:, rows + per : rows + 2 * per].astype(F32))
        arrived = arrived[:, :rows]
    per = fades.shape[1]
    running = jnp.zeros((rows, state), F32)
    entering = []
    order = range(blocks - 1, -1, -1) if reverse else range(blocks)
    for block in order:
        entering.append(low(running))
        one = lax.dynamic_index_in_dim(arrived, me ^ block, 0, False).astype(F32)
        factor = lax.dynamic_index_in_dim(fades, me ^ block, 0, False)
        running = (running.reshape(per, rows // per, state) * factor[:, None, :]).reshape(rows, state) + one
    if reverse:
        entering = entering[::-1]
    returned = send_chunks(jnp.stack(entering))
    returned = jnp.stack(returned)
    ordered = jnp.stack(
        [lax.dynamic_index_in_dim(returned, me ^ block, 0, False) for block in range(blocks)]
    )
    return ordered.reshape(width, state), fades


def by_head(values, width):
    return jnp.repeat(values, width, axis=1)


def of_heads(values, heads):
    return jnp.sum(values.reshape(values.shape[0], heads, -1), 2)


def conv_preact(weights, padded, length):
    kernel = jnp.concatenate([weights["conv_x"], weights["conv_bc"]], 1)
    bias = jnp.concatenate([weights["conv_bias_x"], weights["conv_bias_bc"]], 0)
    taps = kernel.shape[0]
    return kernel, bias + sum(
        kernel[offset] * padded[offset : offset + length] for offset in range(taps)
    )


def ssd_parts(weights, preact, step_raw):
    activated = jax.nn.silu(preact)
    inner = weights["w_x"].shape[1]
    state = weights["w_bc"].shape[1] // 2
    length = preact.shape[0]
    signal = activated[:, :inner]
    write_key = activated[:, inner : inner + state]
    read_key = activated[:, inner + state :]
    step = jax.nn.softplus(step_raw + weights["dt_bias"])
    rate = -jnp.exp(weights["a_log"])
    decay_sum = jnp.cumsum(rate * step, 0)
    index = jnp.arange(length)
    lower = (index[:, None] >= index[None, :])[None]
    diff = decay_sum.T[:, :, None] - decay_sum.T[:, None, :]
    decay = jnp.where(lower, jnp.exp(jnp.where(lower, diff, 0.0)), 0.0)
    gram = tail_dot(low(read_key), low(write_key))
    return signal, write_key, read_key, step, rate, decay_sum, decay, gram


def layer_forward(entry, weights):
    length = entry.shape[0]
    wide = entry.astype(F32)
    inverse_rms = lax.rsqrt(jnp.mean(wide * wide, -1, keepdims=True) + EPS)
    normed = low(wide * inverse_rms * weights["norm_gain"])
    joined = jnp.concatenate([matmul(normed, weights["w_x"]), matmul(normed, weights["w_bc"])], 1)
    step_raw = matmul(normed, weights["w_dt"])
    taps = weights["conv_x"].shape[0]
    before = shifted(joined[length - taps + 1 :], "seq", 1)
    gate_in = matmul(normed, weights["w_z"])
    padded = jnp.concatenate([before, joined], 0)
    _, preact = conv_preact(weights, padded, length)
    signal, write_key, read_key, step, rate, decay_sum, decay, gram = ssd_parts(
        weights, preact, step_raw
    )
    heads = step.shape[1]
    inner = signal.shape[1]
    width = inner // heads
    tail = jnp.exp(decay_sum[-1][None, :] - decay_sum) * step
    local = lead_dot(low(by_head(tail, width) * signal), low(write_key))
    start, fades = scan_states(jnp.exp(decay_sum[-1]), local, None)
    mixing = gram[None] * decay * step.T[:, None, :]
    intra = jnp.einsum(
        "hts,shp->thp", low(mixing), low(signal).reshape(length, heads, width),
        preferred_element_type=F32,
    ).reshape(length, inner)
    inter = by_head(jnp.exp(decay_sum), width) * tail_dot(low(read_key), start)
    ssd_out = intra + inter + jnp.repeat(weights["d_skip"], width) * signal
    gated = ssd_out * jax.nn.silu(gate_in)
    total_inner = inner * lax.axis_size("head")
    squares = head_sum_wide(jnp.sum(gated * gated, -1))
    mix_scale = lax.rsqrt(squares / total_inner + EPS)[:, None]
    branch = mix_scale * head_sum(matmul(low(gated * weights["mix_gain"]), weights["w_out"]))
    kept = (entry, inverse_rms, normed, gate_in, padded, step_raw, start, fades, ssd_out, mix_scale, branch)
    return low(wide + branch), kept


def layer_backward(grad_out, kept, weights):
    entry, inverse_rms, normed, gate_in, padded, step_raw, start, fades, ssd_out, mix_scale, branch = kept
    length = entry.shape[0]
    wide_grad = grad_out.astype(F32)
    grad_low = low(grad_out)
    gated = ssd_out * jax.nn.silu(gate_in)
    mixed = low(gated * mix_scale * weights["mix_gain"])
    grad_mixed = tail_dot(grad_low, weights["w_out"])
    grad_mix_gain = jnp.sum(grad_mixed * gated * mix_scale, 0)
    weighted = grad_mixed * weights["mix_gain"]
    inner = gated.shape[1]
    total_inner = inner * lax.axis_size("head")
    along = jnp.sum(grad_low.astype(F32) * branch, -1, keepdims=True)
    grad_gated = mix_scale * weighted - gated * (mix_scale**2 * along / total_inner)
    grad_y = grad_gated * jax.nn.silu(gate_in)
    gate_low = low(grad_gated * ssd_out * silu_slope(gate_in))
    kernel, preact = conv_preact(weights, padded, length)
    signal, write_key, read_key, step, rate, decay_sum, decay, gram = ssd_parts(
        weights, preact, step_raw
    )
    heads = step.shape[1]
    width = inner // heads
    write_low, read_low = low(write_key), low(read_key)
    rise = jnp.exp(decay_sum)
    grad_reach = low(grad_y * by_head(rise, width))
    grad_start = lead_dot(grad_reach, read_low)
    grad_local, _ = scan_states(None, grad_start, fades)
    grad_skip = jnp.sum(of_heads(grad_y * signal, heads), 0)
    cube = lambda a: low(a).reshape(length, heads, width)
    base = decay * step.T[:, None, :]
    mixing = gram[None] * base
    grad_signal = jnp.repeat(weights["d_skip"], width) * grad_y + jnp.einsum(
        "hts,thp->shp", low(mixing), cube(grad_y), preferred_element_type=F32
    ).reshape(length, inner)
    grad_mixing = jnp.einsum("thp,shp->hts", cube(grad_y), cube(signal), preferred_element_type=F32)
    grad_gram = low(jnp.sum(grad_mixing * base, 0))
    grad_read = matmul(grad_gram, write_low) + matmul(grad_reach, start)
    grad_write = lead_dot(grad_gram, read_low)
    grad_log = grad_mixing * mixing
    grad_decay_sum = (jnp.sum(grad_log, 2) - jnp.sum(grad_log, 1)).T
    grad_step = jnp.sum(grad_mixing * gram[None] * decay, 1).T
    reach = tail_dot(read_low, start)
    grad_decay_sum = grad_decay_sum + of_heads(grad_y * reach, heads) * rise
    fade = rise[-1]
    last_row = (jnp.arange(length) == length - 1)[:, None]
    products = jnp.sum(grad_local.astype(F32) * start.astype(F32), 1).reshape(heads, width)
    grad_decay_sum = grad_decay_sum + jnp.where(last_row, (jnp.sum(products, 1) * fade)[None, :], 0.0)
    keep = jnp.exp(decay_sum[-1][None, :] - decay_sum)
    tail = keep * step
    spread = tail_dot(write_low, grad_local)
    wide_tail = by_head(tail, width)
    grad_signal = grad_signal + wide_tail * spread
    grad_write = grad_write + matmul(low(wide_tail * signal), grad_local)
    grad_tail = of_heads(signal * spread, heads)
    grad_step = grad_step + grad_tail * keep
    grad_tail_log = grad_tail * tail
    grad_decay_sum = (
        grad_decay_sum
        - grad_tail_log
        + jnp.where(last_row, jnp.sum(grad_tail_log, 0)[None, :], 0.0)
    )
    grad_log_step = jnp.flip(jnp.cumsum(jnp.flip(grad_decay_sum, 0), 0), 0)
    grad_log_rate = jnp.sum(grad_log_step * step, 0) * rate
    grad_step = grad_step + grad_log_step * rate
    grad_step_raw = grad_step * jax.nn.sigmoid(step_raw + weights["dt_bias"])
    grad_step_bias = jnp.sum(grad_step_raw, 0)
    grad_pre = jnp.concatenate([grad_signal, grad_write, grad_read], 1) * silu_slope(preact)
    taps = kernel.shape[0]
    grad_kernel = jnp.stack(
        [jnp.sum(grad_pre * padded[offset : offset + length], 0) for offset in range(taps)]
    )
    grad_kernel_bias = jnp.sum(grad_pre, 0)
    after = shifted(grad_pre[: taps - 1], "seq", -1)
    extended = jnp.concatenate([grad_pre, after], 0)
    grad_joined = sum(
        kernel[offset] * extended[taps - 1 - offset : taps - 1 - offset + length]
        for offset in range(taps)
    )
    signal_low = low(grad_joined[:, :inner])
    keys_low = low(grad_joined[:, inner:])
    step_low = low(grad_step_raw)
    grad_normed = head_sum(
        tail_dot(gate_low, weights["w_z"])
        + tail_dot(signal_low, weights["w_x"])
        + tail_dot(keys_low, weights["w_bc"])
        + tail_dot(step_low, weights["w_dt"])
    )
    wide = entry.astype(F32)
    grad_gain = jnp.sum(grad_normed * wide * inverse_rms, 0)
    scaled = grad_normed * weights["norm_gain"]
    grad_in = inverse_rms * scaled - wide * inverse_rms**3 * jnp.mean(
        scaled * wide, -1, keepdims=True
    )
    factors = (mixed, grad_low, normed, gate_low, signal_low, keys_low, step_low)
    vectors = (
        grad_gain,
        grad_step_bias,
        grad_log_rate,
        grad_skip,
        grad_kernel[:, :inner],
        grad_kernel_bias[:inner],
        grad_kernel[:, inner:],
        grad_kernel_bias[inner:],
        grad_mix_gain,
    )
    return wide_grad + grad_in, factors, vectors


NAMES = (
    "norm_gain",
    "w_z",
    "w_x",
    "w_bc",
    "w_dt",
    "dt_bias",
    "a_log",
    "d_skip",
    "conv_x",
    "conv_bias_x",
    "conv_bc",
    "conv_bias_bc",
    "mix_gain",
    "w_out",
)


def both_layers(mine):
    first = lax.axis_index("section") == 0
    other = {}
    for name in ("w_x", "w_bc", "w_dt", "w_z", "w_out"):
        other[name] = exchange(mine[name], "section", 1)
    vectors = [name for name in NAMES if not name.startswith("w_")]
    flat = jnp.concatenate([mine[name].reshape(-1) for name in vectors])
    flat = exchange(flat, "section", 1)
    place = 0
    for name in vectors:
        size = mine[name].size
        other[name] = flat[place : place + size].reshape(mine[name].shape)
        place += size
    layer = lambda flag: {name: jnp.where(flag, mine[name], other[name]) for name in NAMES}
    return layer(first), layer(~first)


def shards(hidden_in, order, cotangent, *params):
    mine = {name: param[0] for name, param in zip(NAMES, params)}
    layers = both_layers(mine)
    sections = lax.axis_size("section")
    section = lax.axis_index("section")
    count = order.shape[0] // sections
    base = section * count
    entries = [
        lax.dynamic_index_in_dim(hidden_in, order[base + index], 0, False) for index in range(count)
    ]
    outputs = []
    kept = []
    for weights in layers:
        done = [layer_forward(entry, weights) for entry in entries]
        entries = [one[0] for one in done]
        outputs.append(jnp.stack(entries))
        kept.append([one[1] for one in done])
    cotangents = lax.dynamic_slice_in_dim(cotangent, base, count, 0)
    incoming = [cotangents[index] for index in range(count)]
    grads = [None, None]
    sums = [None, None]
    for layer in (1, 0):
        done = [layer_backward(incoming[index], kept[layer][index], layers[layer]) for index in range(count)]
        grads[layer] = jnp.stack([one[0] for one in done])
        incoming = [low(one[0]) for one in done]
        mixed, grad_low, normed, gate_low, signal_low, keys_low, step_low = (
            jnp.concatenate(parts, 0) for parts in zip(*(one[1] for one in done))
        )
        vectors = jax.tree.map(lambda *parts: sum(parts), *(one[2] for one in done))
        sums[layer] = {
            "w_out": lead_dot(mixed, grad_low),
            "w_z": lead_dot(normed, gate_low),
            "w_x": lead_dot(normed, signal_low),
            "w_bc": lead_dot(normed, keys_low),
            "w_dt": lead_dot(normed, step_low),
        }
        names = [name for name in NAMES if not name.startswith("w_")]
        sums[layer].update(zip(names, vectors))

    first = section == 0

    def to_owner(early, late):
        own = jnp.where(first, early, late)
        sent = exchange(jnp.where(first, late, early), "section", 1)
        return jnp.concatenate(
            [jnp.where(first, own, sent), jnp.where(first, sent, own)], 0
        )

    activations = to_owner(outputs[0], outputs[1])[None]
    grads = to_owner(grads[0], grads[1])[None]

    def reduced(name):
        own = jnp.where(first, sums[0][name], sums[1][name])
        sent = low(jnp.where(first, sums[1][name], sums[0][name]))
        total = low(own + exchange(sent, "section", 1).astype(F32))
        axes = ("seq", "head") if name in ("w_bc", "conv_bc", "conv_bias_bc") else "seq"
        return lax.psum(total, axes)

    return (activations, grads) + tuple(reduced(name).astype(F32)[None] for name in NAMES)


def solution(mesh):
    in_specs = (
        P(None, "seq", None),
        P(),
        P(None, "seq", None),
        P("section", None),
        P("section", None, "head"),
        P("section", None, "head"),
        P("section", None, None),
        P("section", None, "head"),
        P("section", "head"),
        P("section", "head"),
        P("section", "head"),
        P("section", None, "head"),
        P("section", "head"),
        P("section", None, None),
        P("section", None),
        P("section", "head"),
        P("section", "head", None),
    )
    out_specs = (
        P("section", None, "seq", None),
        P("section", None, "seq", None),
        P("section", None),
        P("section", None, "head"),
        P("section", None, "head"),
        P("section", None, None),
        P("section", None, "head"),
        P("section", "head"),
        P("section", "head"),
        P("section", "head"),
        P("section", None, "head"),
        P("section", "head"),
        P("section", None, None),
        P("section", None),
        P("section", "head"),
        P("section", "head", None),
    )
    return jax.shard_map(shards, mesh=mesh, in_specs=in_specs, out_specs=out_specs, check_vma=False)
```

time: 2070 us -> 1120 us (0.54)
  waiting for transfers between devices: 802 us -> 257 us
  blocking collectives: 311 us -> 75.8 us
  matrix products: 379 us -> 159 us
  starting transfers between devices: 45.5 us -> 221 us
  other arithmetic: 316 us -> 182 us
    all_gather x10 -> x0, waiting for transfers between devices: 382 us -> none  [entering(): gathered = jax.tree.map(lambda a: lax.all_gather(a, axis), part)]
    all_gather x10 -> x0, blocking collectives: 233 us -> none  [entering(): gathered = jax.tree.map(lambda a: lax.all_gather(a, axis), part)]
    psum x16 -> x2, waiting for transfers between devices: 400 us -> 183 us  [reduced(): return lax.psum(total, axes)]
    dot_general x95 -> x44, matrix products: 272 us -> 74.1 us  [the longest x32 30.4 us: matmul(): return jnp.dot(left, right, preferred_element_type=F32)]
    ppermute x18 -> x154, starting transfers between devices: 43 us -> 221 us  [the longest x146 202 us: exchange(): return lax.ppermute(block, axis, route)]
    add x40 -> x4, other arithmetic: 76.1 us -> 3.21 us  [scan_states(): arrived[:, rows:rows + per].astype(F32)]
    ppermute x18 -> x154, waiting for transfers between devices: 19.8 us -> 73.3 us  [the longest x146 73.2 us: exchange(): return lax.ppermute(block, axis, route)]
    unnamed x754 -> x1130, local copies, waits for them, and re-layouts: 22.4 us -> 68.3 us
  transfers between devices with their start and end apart: 44 -> 156, of which waited for: 27 -> 34; matrix products, arithmetic and copies ran while one was open for 21% -> 37% of each run, Pallas kernels for 0% -> 0%
where the time goes in v1:
time: 1120 us; the launch traced here: 1100 us
  waiting for transfers between devices  257 us (23%)
  starting transfers between devices  221 us (20%)
  local copies, waits for them, and re-layouts  185 us (17%)
  other arithmetic  182 us (16%)
  matrix products  159 us (14%)
  blocking collectives  75.8 us (7%)
  between operations  25.5 us (2%)
    ppermute x146, starting transfers between devices, exchange(): return lax.ppermute(block, axis, route)  202 us
    psum x2, waiting for transfers between devices, reduced(): return lax.psum(total, axes)  183 us
    psum x2, blocking collectives, reduced(): return lax.psum(total, axes)  75.8 us
    ppermute x146, waiting for transfers between devices, exchange(): return lax.ppermute(block, axis, route)  73.2 us
    unnamed x1130, local copies, waits for them, and re-layouts  68.3 us
    dot_general x32, matrix products, tail_dot(): lax.dot_general(left, right, (((1,), (1,)), ((), ())), preferred_element_...  48.1 us
    dot_general x22, matrix products, lead_dot(): lax.dot_general(left, right, (((0,), (0,)), ((), ())), preferred_element_...  37.1 us
    broadcast_in_dim x24, other arithmetic, shards(): reduced(name).astype(F32)[None]  34.1 us
  transfers between devices with their start and end apart: 156, of which 34 were waited for; matrix products, arithmetic and copies ran while one was open for 37% of the time, Pallas kernels for 0%

profile of v1, /device:TPU:0, one launch (start us, length us, event | category | flops | bytes accessed | tf_op | source)
XLA Modules:
  0.0 1104.7 jit_solution(15510397267337513820)
XLA Ops:
  41.6 3.5 broadcast_select_fusion.2
  45.9 5.1 collective-permute-start.23
  51.8 3.8 collective-permute-start.3
  55.6 3.5 broadcast_select_fusion.1
  60.8 3.8 broadcast_select_fusion.3
  66.8 2.8 fusion.708
  93.0 3.6 fusion.29
  96.7 2.8 fusion.26
  121.0 3.1 collective-permute-start.9
  141.8 3.2 collective-permute-start.35
  155.1 2.8 collective-permute-start.16
  165.2 3.0 collective-permute-done.18
  170.4 3.1 multiply_reduce_fusion.35
  182.8 9.8 collective-permute-done.20
  199.8 3.1 collective-permute-start.57
  220.1 2.7 fusion.729
  232.1 2.7 fusion.703
  238.1 3.4 collective-permute-start.43
  257.6 3.6 fusion.32
  280.7 3.3 collective-permute-start.60
  291.5 2.8 collective-permute-start.64
  306.0 3.4 collective-permute-start.52
  319.4 3.1 collective-permute-start.69
  336.1 4.4 collective-permute-done.55
  354.3 3.4 collective-permute-start.79
  390.6 3.4 collective-permute-start.86
  412.7 7.0 multiply_add_fusion.3
  439.7 4.2 multiply_reduce_fusion.24
  454.5 6.7 fusion.20
  465.3 3.1 collective-permute-start.109
  478.7 2.8 collective-permute-start.113
  482.5 2.8 collective-permute-done.113
  512.7 3.4 collective-permute-start.120
  528.7 3.6 multiply_add_fusion.1
  564.1 5.6 collective-permute-done.90
  572.0 3.0 fusion.697
  579.6 4.5 multiply_reduce_fusion.31
  588.4 4.1 fusion.736
  595.9 7.8 fusion.16
  608.9 2.8 fusion.24
  617.1 3.2 collective-permute-start.123
  633.4 2.9 fusion.183
  636.4 4.0 select_convert_fusion.2
  641.0 2.9 fusion.199
  644.2 4.1 select_convert_fusion
  650.4 2.9 collective-permute-start.127
  656.5 3.3 collective-permute-start.129
  661.3 3.0 collective-permute-start.93
  664.8 3.0 collective-permute-start.95
  682.3 3.0 collective-permute-start.134
  696.8 2.9 collective-permute-start.100
  710.3 4.1 collective-permute-done.104
  715.1 3.6 multiply_add_fusion.2
  743.0 5.7 fusion.118
  750.5 4.1 select_convert_fusion.1
  761.4 5.6 fusion.38
  767.1 4.4 fusion.36
  771.5 4.2 fusion.37
  787.2 8.6 collective-permute-done.138
  795.7 10.7 collective-permute-done.106
  812.7 41.4 %all-reduce.4 = (bf16[1,4,256]{2,1,0:T(4,128)(2,1)S(1)}, bf16[1,256]{1,0:T(2,128)(2,1)S(1)}) all-reduce(bf16[1,4,256]{2,1,0:T(4,128)(2,1)S(1)} %fusion.584, bf16[1,256]{1,0:T(2,128)(2,1)S(1)} %broadcast_in_dim.592), channel_id=1, replica_groups=mesh['section'=2,'seq'=8,'head'=2] {'seq','head'}, use_global_device_ids=true, to_apply=%region_118.119 | all-reduce | flops 1280 | bytes 5120 | tf_op jit(solution)/shard_map/psum | solution.py:381
  859.0 34.4 %all-reduce.5 = (bf16[1,1024]{1,0:T(2,128)(2,1)S(1)}, bf16[1,1024,16]{1,2,0:T(8,128)(2,1)S(1)}, bf16[1,16]{1,0:T(2,128)(2,1)S(1)}, bf16[1,16]{1,0:T(2,128)(2,1)S...) all-reduce(bf16[1,1024]{1,0:T(2,128)(2,1)S(1)} %broadcast_in_dim.57, ...), channel_id=1, replica_groups=mesh['section'=2,'seq'=8,'head'=2] {'seq'}, use_global_device_ids=true, to_apply=%region_72.73 | all-reduce | flops 23600 | bytes 94400 | tf_op jit(solution)/shard_map/psum | solution.py:381
  905.0 183.5 %all-reduce.12.cloned.1.call-done = (bf16[1,1024,1024]{2,1,0:T(8,128)(2,1)}, bf16[1,1024,1024]{2,1,0:T(8,128)(2,1)}, bf16[1,1024,1024]{2,1,0:T(8,128)(2,1)}) async-done(((bf16[1,1024,1024]{2,1,0:T(8,128)(2,1)}, bf16[1,1024,1024]{2,1,0:T(8,128)(2,1)}, bf16[1,1024,1024]{2,1,0:T(8,128)(2,1)}), (bf16[1,1024,1024]{2,1,0:T(8,128)(2,1)}, bf16[1,1024,1024]{2,1,0:T(8,128)(2,1)}, ...) | async-done | bytes 6291472 | tf_op jit(solution)/shard_map/psum | solution.py:381
  1088.5 4.2 broadcast_in_dim.573
  (1955 shorter events, 574.9 us)
Async XLA Ops:
  7.2 890.7 %all-reduce.10.cloned.1.call-start = ((), (), s32[]{:S(2)}) async-start(), calls=%async_computation | async-start | bytes 1048576 | tf_op jit(solution)/shard_map/psum | solution.py:381
  9.6 14.8 %collective-permute-start = (f32[8496]{0:T(1024)S(1)}, f32[8496]{0:T(1024)S(1)}, u32[]{:S(2)}, u32[]{:S(2)}) collective-permute-start(f32[8496]{0:T(1024)S(1)} %concatenate.151), channel_id=1, source_target_pairs={{0,16},{16,0},{1,17},{17,1},{2,18},{18,2},{3,19},{19,3},{4,20},{20... | collective-permute-start | bytes 101960 | tf_op jit(solution)/shard_map/ppermute | solution.py:13
  10.1 31.5 %collective-permute-start.1 = (bf16[1024,1024]{1,0:T(8,128)(2,1)}, bf16[1024,1024]{1,0:T(8,128)(2,1)}, u32[]{:S(2)}, u32[]{:S(2)}) collective-permute-start(bf16[1024,1024]{1,0:T(8,128)(2,1)} %bitcast.2044), channel_id=1, source_target_pairs={{0,16},{16,0},{1,17},{17,1},{2,18},{18,2},{3,19},{19,3},{4,20},{20... | collective-permute-start | bytes 6291464 | tf_op jit(solution)/shard_map/ppermute | solution.py:13
  10.2 28.7 %collective-permute-start.2 = (bf16[1024,256]{1,0:T(8,128)(2,1)}, bf16[1024,256]{1,0:T(8,128)(2,1)}, u32[]{:S(2)}, u32[]{:S(2)}) collective-permute-start(bf16[1024,256]{1,0:T(8,128)(2,1)} %bitcast.2102), channel_id=1, source_target_pairs={{0,16},{16,0},{1,17},{17,1},{2,18},{18,2},{3,19},{19,3},{4,20},{20... | collective-permute-start | bytes 1572872 | tf_op jit(solution)/shard_map/ppermute | solution.py:13
  10.6 13.0 %collective-permute-start.4 = (bf16[1024,16]{0,1:T(8,128)(2,1)}, bf16[1024,16]{0,1:T(8,128)(2,1)S(1)}, u32[]{:S(2)}, u32[]{:S(2)}) collective-permute-start(bf16[1024,16]{0,1:T(8,128)(2,1)} %bitcast.2109), channel_id=1, source_target_pairs={{0,16},{16,0},{1,17},{17,1},{2,18},{18,2},{3,19},{19,3},{4,20},{20... | collective-permute-start | bytes 98312 | tf_op jit(solution)/shard_map/ppermute | solution.py:13
  10.7 44.9 %collective-permute-start.19 = (bf16[1024,1024]{1,0:T(8,128)(2,1)}, bf16[1024,1024]{1,0:T(8,128)(2,1)}, u32[]{:S(2)}, u32[]{:S(2)}) collective-permute-start(bf16[1024,1024]{1,0:T(8,128)(2,1)} %bitcast.2045), channel_id=1, source_target_pairs={{0,16},{16,0},{1,17},{17,1},{2,18},{18,2},{3,19},{19,3},{4,20},{20... | collective-permute-start | bytes 6291464 | tf_op jit(solution)/shard_map/ppermute | solution.py:13
  23.6 37.1 %collective-permute-start.21 = (bf16[1024,1024]{1,0:T(8,128)(2,1)}, bf16[1024,1024]{1,0:T(8,128)(2,1)}, u32[]{:S(2)}, u32[]{:S(2)}) collective-permute-start(bf16[1024,1024]{1,0:T(8,128)(2,1)} %bitcast.68), channel_id=1, source_target_pairs={{0,16},{16,0},{1,17},{17,1},{2,18},{18,2},{3,19},{19,3},{4,20},{20... | collective-permute-start | bytes 6291464 | tf_op jit(solution)/shard_map/ppermute | solution.py:13
  45.9 20.5 %collective-permute-start.23 = (f32[3,1280]{1,0:T(4,128)S(1)}, f32[3,1280]{1,0:T(4,128)S(1)}, u32[]{:S(2)}, u32[]{:S(2)}) collective-permute-start(f32[3,1280]{1,0:T(4,128)S(1)} %fusion.515), channel_id=1, source_target_pairs={{0,2},{2,4},{4,6},{6,8},{8,10},{10,12},{12,14},{1,3},{3,5},{5,7},{... | collective-permute-start | bytes 46088 | tf_op jit(solution)/shard_map/ppermute | solution.py:19
  51.8 14.8 %collective-permute-start.3 = (f32[3,1280]{1,0:T(4,128)S(1)}, f32[3,1280]{1,0:T(4,128)S(1)}, u32[]{:S(2)}, u32[]{:S(2)}) collective-permute-start(f32[3,1280]{1,0:T(4,128)S(1)} %fusion.516), channel_id=1, source_target_pairs={{0,2},{2,4},{4,6},{6,8},{8,10},{10,12},{12,14},{1,3},{3,5},{5,7},{... | collective-permute-start | bytes 46088 | tf_op jit(solution)/shard_map/ppermute | solution.py:19
  72.9 32.5 %collective-permute-start.24 = (bf16[144,128]{1,0:T(8,128)(2,1)}, bf16[144,128]{1,0:T(8,128)(2,1)}, u32[]{:S(2)}, u32[]{:S(2)}) collective-permute-start(bf16[144,128]{1,0:T(8,128)(2,1)} %get-tuple-element.280), channel_id=1, source_target_pairs={{0,2},{2,0},{4,6},{6,4},{8,10},{10,8},{12,14},{14,12},{1,3},{3,1},... | collective-permute-start | bytes 110600 | tf_op jit(solution)/shard_map/ppermute | solution.py:13
  74.4 34.4 %collective-permute-start.25 = (bf16[144,128]{1,0:T(8,128)(2,1)}, bf16[144,128]{1,0:T(8,128)(2,1)}, u32[]{:S(2)}, u32[]{:S(2)}) collective-permute-start(bf16[144,128]{1,0:T(8,128)(2,1)} %get-tuple-element.279), channel_id=1, source_target_pairs={{0,4},{2,6},{4,0},{6,2},{8,12},{10,14},{12,8},{14,10},{1,5},{3,7},... | collective-permute-start | bytes 110600 | tf_op jit(solution)/shard_map/ppermute | solution.py:13
  76.0 36.0 %collective-permute-start.26 = (bf16[144,128]{1,0:T(8,128)(2,1)}, bf16[144,128]{1,0:T(8,128)(2,1)}, u32[]{:S(2)}, u32[]{:S(2)}) collective-permute-start(bf16[144,128]{1,0:T(8,128)(2,1)} %get-tuple-element.278), channel_id=1, source_target_pairs={{0,6},{2,4},{4,2},{6,0},{8,14},{10,12},{12,10},{14,8},{1,7},{3,5},... | collective-permute-start | bytes 110600 | tf_op jit(solution)/shard_map/ppermute | solution.py:13
  76.4 38.4 %collective-permute-start.27 = (bf16[144,128]{1,0:T(8,128)(2,1)}, bf16[144,128]{1,0:T(8,128)(2,1)}, u32[]{:S(2)}, u32[]{:S(2)}) collective-permute-start(bf16[144,128]{1,0:T(8,128)(2,1)} %get-tuple-element.277), channel_id=1, source_target_pairs={{0,8},{2,10},{4,12},{6,14},{8,0},{10,2},{12,4},{14,6},{1,9},{3,11}... | collective-permute-start | bytes 110600 | tf_op jit(solution)/shard_map/ppermute | solution.py:13
  79.0 37.2 %collective-permute-start.28 = (bf16[144,128]{1,0:T(8,128)(2,1)}, bf16[144,128]{1,0:T(8,128)(2,1)}, u32[]{:S(2)}, u32[]{:S(2)}) collective-permute-start(bf16[144,128]{1,0:T(8,128)(2,1)} %get-tuple-element.276), channel_id=1, source_target_pairs={{0,10},{2,8},{4,14},{6,12},{8,2},{10,0},{12,6},{14,4},{1,11},{3,9}... | collective-permute-start | bytes 110600 | tf_op jit(solution)/shard_map/ppermute | solution.py:13
  105.4 14.2 %collective-permute-start.29 = (bf16[144,128]{1,0:T(8,128)(2,1)}, bf16[144,128]{1,0:T(8,128)(2,1)S(1)}, u32[]{:S(2)}, u32[]{:S(2)}) collective-permute-start(bf16[144,128]{1,0:T(8,128)(2,1)} %get-tuple-element.275), channel_id=1, source_target_pairs={{0,12},{2,14},{4,8},{6,10},{8,4},{10,6},{12,0},{14,2},{1,13},{3,15... | collective-permute-start | bytes 110600 | tf_op jit(solution)/shard_map/ppermute | solution.py:13
  116.2 13.5 %collective-permute-start.7 = (bf16[144,128]{1,0:T(8,128)(2,1)}, bf16[144,128]{1,0:T(8,128)(2,1)S(1)}, u32[]{:S(2)}, u32[]{:S(2)}) collective-permute-start(bf16[144,128]{1,0:T(8,128)(2,1)} %get-tuple-element.262), channel_id=1, source_target_pairs={{0,6},{2,4},{4,2},{6,0},{8,14},{10,12},{12,10},{14,8},{1,7},{3,5},... | collective-permute-start | bytes 110600 | tf_op jit(solution)/shard_map/ppermute | solution.py:13
  176.6 16.0 %collective-permute-start.39 = (bf16[256,1024]{1,0:T(8,128)(2,1)S(1)}, bf16[256,1024]{1,0:T(8,128)(2,1)S(1)}, u32[]{:S(2)}, u32[]{:S(2)}) collective-permute-start(bf16[256,1024]{1,0:T(8,128)(2,1)S(1)} %convolution_convert_fusion.2), channel_id=1, source_target_pairs={{0,1},{1,0},{2,3},{3,2},{4,5},{5,4},{6,7},{7,6},{8,9},{9,8},{10,11... | collective-permute-start | bytes 1572872 | tf_op jit(solution)/shard_map/ppermute | solution.py:13
  179.0 13.6 %collective-permute-start.22 = (bf16[256,1024]{1,0:T(8,128)(2,1)S(1)}, bf16[256,1024]{1,0:T(8,128)(2,1)S(1)}, u32[]{:S(2)}, u32[]{:S(2)}) collective-permute-start(bf16[256,1024]{1,0:T(8,128)(2,1)S(1)} %convolution_convert_fusion.3), channel_id=1, source_target_pairs={{0,1},{1,0},{2,3},{3,2},{4,5},{5,4},{6,7},{7,6},{8,9},{9,8},{10,11... | collective-permute-start | bytes 1572872 | tf_op jit(solution)/shard_map/ppermute | solution.py:13
  199.8 30.1 %collective-permute-start.57 = (f32[3,1280]{1,0:T(4,128)}, f32[3,1280]{1,0:T(4,128)}, u32[]{:S(2)}, u32[]{:S(2)}) collective-permute-start(f32[3,1280]{1,0:T(4,128)} %fusion.513), channel_id=1, source_target_pairs={{0,2},{2,4},{4,6},{6,8},{8,10},{10,12},{12,14},{1,3},{3,5},{5,7},{... | collective-permute-start | bytes 46088 | tf_op jit(solution)/shard_map/ppermute | solution.py:19
  203.4 27.4 %collective-permute-start.40 = (f32[3,1280]{1,0:T(4,128)}, f32[3,1280]{1,0:T(4,128)}, u32[]{:S(2)}, u32[]{:S(2)}) collective-permute-start(f32[3,1280]{1,0:T(4,128)} %fusion.514), channel_id=1, source_target_pairs={{0,2},{2,4},{4,6},{6,8},{8,10},{10,12},{12,14},{1,3},{3,5},{5,7},{... | collective-permute-start | bytes 46088 | tf_op jit(solution)/shard_map/ppermute | solution.py:19
  238.1 31.7 %collective-permute-start.41 = (bf16[144,128]{1,0:T(8,128)(2,1)}, bf16[144,128]{1,0:T(8,128)(2,1)}, u32[]{:S(2)}, u32[]{:S(2)}) collective-permute-start(bf16[144,128]{1,0:T(8,128)(2,1)} %get-tuple-element.256), channel_id=1, source_target_pairs={{0,2},{2,0},{4,6},{6,4},{8,10},{10,8},{12,14},{14,12},{1,3},{3,1},... | collective-permute-start | bytes 110600 | tf_op jit(solution)/shard_map/ppermute | solution.py:13
  238.1 35.5 %collective-permute-start.42 = (bf16[144,128]{1,0:T(8,128)(2,1)}, bf16[144,128]{1,0:T(8,128)(2,1)}, u32[]{:S(2)}, u32[]{:S(2)}) collective-permute-start(bf16[144,128]{1,0:T(8,128)(2,1)} %get-tuple-element.255), channel_id=1, source_target_pairs={{0,4},{2,6},{4,0},{6,2},{8,12},{10,14},{12,8},{14,10},{1,5},{3,7},... | collective-permute-start | bytes 110600 | tf_op jit(solution)/shard_map/ppermute | solution.py:13
  238.1 39.5 %collective-permute-start.43 = (bf16[144,128]{1,0:T(8,128)(2,1)}, bf16[144,128]{1,0:T(8,128)(2,1)}, u32[]{:S(2)}, u32[]{:S(2)}) collective-permute-start(bf16[144,128]{1,0:T(8,128)(2,1)} %get-tuple-element.254), channel_id=1, source_target_pairs={{0,6},{2,4},{4,2},{6,0},{8,14},{10,12},{12,10},{14,8},{1,7},{3,5},... | collective-permute-start | bytes 110600 | tf_op jit(solution)/shard_map/ppermute | solution.py:13
  241.6 37.7 %collective-permute-start.44 = (bf16[144,128]{1,0:T(8,128)(2,1)}, bf16[144,128]{1,0:T(8,128)(2,1)}, u32[]{:S(2)}, u32[]{:S(2)}) collective-permute-start(bf16[144,128]{1,0:T(8,128)(2,1)} %get-tuple-element.253), channel_id=1, source_target_pairs={{0,8},{2,10},{4,12},{6,14},{8,0},{10,2},{12,4},{14,6},{1,9},{3,11}... | collective-permute-start | bytes 110600 | tf_op jit(solution)/shard_map/ppermute | solution.py:13
  244.2 36.5 %collective-permute-start.45 = (bf16[144,128]{1,0:T(8,128)(2,1)}, bf16[144,128]{1,0:T(8,128)(2,1)}, u32[]{:S(2)}, u32[]{:S(2)}) collective-permute-start(bf16[144,128]{1,0:T(8,128)(2,1)} %get-tuple-element.252), channel_id=1, source_target_pairs={{0,10},{2,8},{4,14},{6,12},{8,2},{10,0},{12,6},{14,4},{1,11},{3,9}... | collective-permute-start | bytes 110600 | tf_op jit(solution)/shard_map/ppermute | solution.py:13
  269.8 15.5 %collective-permute-start.46 = (bf16[144,128]{1,0:T(8,128)(2,1)S(1)}, bf16[144,128]{1,0:T(8,128)(2,1)S(1)}, u32[]{:S(2)}, u32[]{:S(2)}) collective-permute-start(bf16[144,128]{1,0:T(8,128)(2,1)S(1)} %copy-done.366), channel_id=1, source_target_pairs={{0,12},{2,14},{4,8},{6,10},{8,4},{10,6},{12,0},{14,2},{1,13},{3,15... | collective-permute-start | bytes 110600 | tf_op jit(solution)/shard_map/ppermute | solution.py:13
  273.6 13.1 %collective-permute-start.47 = (bf16[144,128]{1,0:T(8,128)(2,1)S(1)}, bf16[144,128]{1,0:T(8,128)(2,1)S(1)}, u32[]{:S(2)}, u32[]{:S(2)}) collective-permute-start(bf16[144,128]{1,0:T(8,128)(2,1)S(1)} %copy-done.365), channel_id=1, source_target_pairs={{0,14},{2,12},{4,10},{6,8},{8,6},{10,4},{12,2},{14,0},{1,15},{3,13... | collective-permute-start | bytes 110600 | tf_op jit(solution)/shard_map/ppermute | solution.py:13
  280.7 13.6 %collective-permute-start.60 = (bf16[144,128]{1,0:T(8,128)(2,1)}, bf16[144,128]{1,0:T(8,128)(2,1)S(1)}, u32[]{:S(2)}, u32[]{:S(2)}) collective-permute-start(bf16[144,128]{1,0:T(8,128)(2,1)} %get-tuple-element.270), channel_id=1, source_target_pairs={{0,6},{2,4},{4,2},{6,0},{8,14},{10,12},{12,10},{14,8},{1,7},{3,5},... | collective-permute-start | bytes 110600 | tf_op jit(solution)/shard_map/ppermute | solution.py:13
  316.3 12.9 %collective-permute-start.66 = (bf16[128,128]{1,0:T(8,128)(2,1)S(1)}, bf16[128,128]{1,0:T(8,128)(2,1)S(1)}, u32[]{:S(2)}, u32[]{:S(2)}) collective-permute-start(bf16[128,128]{1,0:T(8,128)(2,1)S(1)} %get-tuple-element.367), channel_id=1, source_target_pairs={{0,4},{2,6},{4,0},{6,2},{8,12},{10,14},{12,8},{14,10},{1,5},{3,7},... | collective-permute-start | bytes 98312 | tf_op jit(solution)/shard_map/ppermute | solution.py:13
  316.4 14.9 %collective-permute-start.67 = (bf16[128,128]{1,0:T(8,128)(2,1)S(1)}, bf16[128,128]{1,0:T(8,128)(2,1)S(1)}, u32[]{:S(2)}, u32[]{:S(2)}) collective-permute-start(bf16[128,128]{1,0:T(8,128)(2,1)S(1)} %get-tuple-element.366), channel_id=1, source_target_pairs={{0,6},{2,4},{4,2},{6,0},{8,14},{10,12},{12,10},{14,8},{1,7},{3,5},... | collective-permute-start | bytes 98312 | tf_op jit(solution)/shard_map/ppermute | solution.py:13
  318.5 13.4 %collective-permute-start.68 = (bf16[128,128]{1,0:T(8,128)(2,1)S(1)}, bf16[128,128]{1,0:T(8,128)(2,1)S(1)}, u32[]{:S(2)}, u32[]{:S(2)}) collective-permute-start(bf16[128,128]{1,0:T(8,128)(2,1)S(1)} %get-tuple-element.365), channel_id=1, source_target_pairs={{0,8},{2,10},{4,12},{6,14},{8,0},{10,2},{12,4},{14,6},{1,9},{3,11}... | collective-permute-start | bytes 98312 | tf_op jit(solution)/shard_map/ppermute | solution.py:13
  319.4 14.1 %collective-permute-start.69 = (bf16[128,128]{1,0:T(8,128)(2,1)S(1)}, bf16[128,128]{1,0:T(8,128)(2,1)S(1)}, u32[]{:S(2)}, u32[]{:S(2)}) collective-permute-start(bf16[128,128]{1,0:T(8,128)(2,1)S(1)} %get-tuple-element.364), channel_id=1, source_target_pairs={{0,10},{2,8},{4,14},{6,12},{8,2},{10,0},{12,6},{14,4},{1,11},{3,9}... | collective-permute-start | bytes 98312 | tf_op jit(solution)/shard_map/ppermute | solution.py:13
  351.9 14.6 %collective-permute-start.77 = (bf16[128,128]{1,0:T(8,128)(2,1)}, bf16[128,128]{1,0:T(8,128)(2,1)}, u32[]{:S(2)}, u32[]{:S(2)}) collective-permute-start(bf16[128,128]{1,0:T(8,128)(2,1)} %get-tuple-element.326), channel_id=1, source_target_pairs={{0,6},{2,4},{4,2},{6,0},{8,14},{10,12},{12,10},{14,8},{1,7},{3,5},... | collective-permute-start | bytes 98312 | tf_op jit(solution)/shard_map/ppermute | solution.py:13
  353.9 14.0 %collective-permute-start.78 = (bf16[128,128]{1,0:T(8,128)(2,1)}, bf16[128,128]{1,0:T(8,128)(2,1)}, u32[]{:S(2)}, u32[]{:S(2)}) collective-permute-start(bf16[128,128]{1,0:T(8,128)(2,1)} %get-tuple-element.325), channel_id=1, source_target_pairs={{0,8},{2,10},{4,12},{6,14},{8,0},{10,2},{12,4},{14,6},{1,9},{3,11}... | collective-permute-start | bytes 98312 | tf_op jit(solution)/shard_map/ppermute | solution.py:13
  354.3 14.9 %collective-permute-start.79 = (bf16[128,128]{1,0:T(8,128)(2,1)}, bf16[128,128]{1,0:T(8,128)(2,1)}, u32[]{:S(2)}, u32[]{:S(2)}) collective-permute-start(bf16[128,128]{1,0:T(8,128)(2,1)} %get-tuple-element.324), channel_id=1, source_target_pairs={{0,10},{2,8},{4,14},{6,12},{8,2},{10,0},{12,6},{14,4},{1,11},{3,9}... | collective-permute-start | bytes 98312 | tf_op jit(solution)/shard_map/ppermute | solution.py:13
  378.9 15.2 %collective-permute-start.82 = (bf16[128,128]{1,0:T(8,128)(2,1)}, bf16[128,128]{1,0:T(8,128)(2,1)}, u32[]{:S(2)}, u32[]{:S(2)}) collective-permute-start(bf16[128,128]{1,0:T(8,128)(2,1)} %get-tuple-element.320), channel_id=1, source_target_pairs={{0,2},{2,0},{4,6},{6,4},{8,10},{10,8},{12,14},{14,12},{1,3},{3,1},... | collective-permute-start | bytes 98312 | tf_op jit(solution)/shard_map/ppermute | solution.py:13
  421.2 18.5 %collective-permute-start.73 = (bf16[256,1024]{1,0:T(8,128)(2,1)}, bf16[256,1024]{1,0:T(8,128)(2,1)}, u32[]{:S(2)}, u32[]{:S(2)}) collective-permute-start(bf16[256,1024]{1,0:T(8,128)(2,1)} %convolution_convert_fusion), channel_id=1, source_target_pairs={{0,1},{1,0},{2,3},{3,2},{4,5},{5,4},{6,7},{7,6},{8,9},{9,8},{10,11... | collective-permute-start | bytes 1572872 | tf_op jit(solution)/shard_map/ppermute | solution.py:13
  421.7 17.2 %collective-permute-start.72 = (f32[256]{0:T(256)}, f32[256]{0:T(256)}, u32[]{:S(2)}, u32[]{:S(2)}) collective-permute-start(f32[256]{0:T(256)} %get-tuple-element.488), channel_id=1, source_target_pairs={{0,1},{1,0},{2,3},{3,2},{4,5},{5,4},{6,7},{7,6},{8,9},{9,8},{10,11... | collective-permute-start | bytes 3080 | tf_op jit(solution)/shard_map/ppermute | solution.py:13
  465.3 13.4 %collective-permute-start.108 = (bf16[128,128]{1,0:T(8,128)(2,1)S(1)}, bf16[128,128]{1,0:T(8,128)(2,1)S(1)}, u32[]{:S(2)}, u32[]{:S(2)}) collective-permute-start(bf16[128,128]{1,0:T(8,128)(2,1)S(1)} %get-tuple-element.343), channel_id=1, source_target_pairs={{0,4},{2,6},{4,0},{6,2},{8,12},{10,14},{12,8},{14,10},{1,5},{3,7},... | collective-permute-start | bytes 98312 | tf_op jit(solution)/shard_map/ppermute | solution.py:13
  465.3 16.2 %collective-permute-start.109 = (bf16[128,128]{1,0:T(8,128)(2,1)S(1)}, bf16[128,128]{1,0:T(8,128)(2,1)S(1)}, u32[]{:S(2)}, u32[]{:S(2)}) collective-permute-start(bf16[128,128]{1,0:T(8,128)(2,1)S(1)} %get-tuple-element.342), channel_id=1, source_target_pairs={{0,6},{2,4},{4,2},{6,0},{8,14},{10,12},{12,10},{14,8},{1,7},{3,5},... | collective-permute-start | bytes 98312 | tf_op jit(solution)/shard_map/ppermute | solution.py:13
  468.4 13.1 %collective-permute-start.110 = (bf16[128,128]{1,0:T(8,128)(2,1)S(1)}, bf16[128,128]{1,0:T(8,128)(2,1)S(1)}, u32[]{:S(2)}, u32[]{:S(2)}) collective-permute-start(bf16[128,128]{1,0:T(8,128)(2,1)S(1)} %get-tuple-element.341), channel_id=1, source_target_pairs={{0,8},{2,10},{4,12},{6,14},{8,0},{10,2},{12,4},{14,6},{1,9},{3,11}... | collective-permute-start | bytes 98312 | tf_op jit(solution)/shard_map/ppermute | solution.py:13
  486.5 21.0 %collective-permute-start.114 = (bf16[128,128]{1,0:T(8,128)(2,1)}, bf16[128,128]{1,0:T(8,128)(2,1)}, u32[]{:S(2)}, u32[]{:S(2)}) collective-permute-start(bf16[128,128]{1,0:T(8,128)(2,1)} %get-tuple-element.336), channel_id=1, source_target_pairs={{0,2},{2,0},{4,6},{6,4},{8,10},{10,8},{12,14},{14,12},{1,3},{3,1},... | collective-permute-start | bytes 98312 | tf_op jit(solution)/shard_map/ppermute | solution.py:13
  494.0 54.5 %collective-permute-start.89 = (f32[3,1280]{1,0:T(4,128)}, f32[3,1280]{1,0:T(4,128)}, u32[]{:S(2)}, u32[]{:S(2)}) collective-permute-start(f32[3,1280]{1,0:T(4,128)} %slice.665), channel_id=1, source_target_pairs={{2,0},{4,2},{6,4},{8,6},{10,8},{12,10},{14,12},{3,1},{5,3},{7,5},{... | collective-permute-start | bytes 46088 | tf_op jit(solution)/shard_map/ppermute | solution.py:19
  533.9 14.6 %collective-permute-start.121 = (f32[3,1280]{1,0:T(4,128)S(1)}, f32[3,1280]{1,0:T(4,128)S(1)}, u32[]{:S(2)}, u32[]{:S(2)}) collective-permute-start(f32[3,1280]{1,0:T(4,128)S(1)} %slice.683), channel_id=1, source_target_pairs={{2,0},{4,2},{6,4},{8,6},{10,8},{12,10},{14,12},{3,1},{5,3},{7,5},{... | collective-permute-start | bytes 46088 | tf_op jit(solution)/shard_map/ppermute | solution.py:19
  556.4 13.2 %collective-permute-start.90 = (bf16[256,1024]{1,0:T(8,128)(2,1)S(1)}, bf16[256,1024]{1,0:T(8,128)(2,1)S(1)}, u32[]{:S(2)}, u32[]{:S(2)}) collective-permute-start(bf16[256,1024]{1,0:T(8,128)(2,1)S(1)} %fusion.137), channel_id=1, source_target_pairs={{0,1},{1,0},{2,3},{3,2},{4,5},{5,4},{6,7},{7,6},{8,9},{9,8},{10,11... | collective-permute-start | bytes 1572872 | tf_op jit(solution)/shard_map/ppermute | solution.py:13
  559.2 296.3 %collective-permute-start.74 = (bf16[2,256,1024]{2,1,0:T(8,128)(2,1)}, bf16[2,256,1024]{2,1,0:T(8,128)(2,1)}, u32[]{:S(2)}, u32[]{:S(2)}) collective-permute-start(bf16[2,256,1024]{2,1,0:T(8,128)(2,1)} %broadcast_select_fusion.10), channel_id=1, source_target_pairs={{0,16},{16,0},{1,17},{17,1},{2,18},{18,2},{3,19},{19,3},{4,20},{20... | collective-permute-start | bytes 3145736 | tf_op jit(solution)/shard_map/ppermute | solution.py:13
  617.1 33.3 %collective-permute-start.123 = (bf16[128,128]{1,0:T(8,128)(2,1)}, bf16[128,128]{1,0:T(8,128)(2,1)}, u32[]{:S(2)}, u32[]{:S(2)}) collective-permute-start(bf16[128,128]{1,0:T(8,128)(2,1)} %get-tuple-element.312), channel_id=1, source_target_pairs={{0,2},{2,0},{4,6},{6,4},{8,10},{10,8},{12,14},{14,12},{1,3},{3,1},... | collective-permute-start | bytes 98312 | tf_op jit(solution)/shard_map/ppermute | solution.py:13
  620.3 33.8 %collective-permute-start.124 = (bf16[128,128]{1,0:T(8,128)(2,1)}, bf16[128,128]{1,0:T(8,128)(2,1)}, u32[]{:S(2)}, u32[]{:S(2)}) collective-permute-start(bf16[128,128]{1,0:T(8,128)(2,1)} %get-tuple-element.311), channel_id=1, source_target_pairs={{0,4},{2,6},{4,0},{6,2},{8,12},{10,14},{12,8},{14,10},{1,5},{3,7},... | collective-permute-start | bytes 98312 | tf_op jit(solution)/shard_map/ppermute | solution.py:13
  621.9 34.6 %collective-permute-start.125 = (bf16[128,128]{1,0:T(8,128)(2,1)}, bf16[128,128]{1,0:T(8,128)(2,1)}, u32[]{:S(2)}, u32[]{:S(2)}) collective-permute-start(bf16[128,128]{1,0:T(8,128)(2,1)} %get-tuple-element.310), channel_id=1, source_target_pairs={{0,6},{2,4},{4,2},{6,0},{8,14},{10,12},{12,10},{14,8},{1,7},{3,5},... | collective-permute-start | bytes 98312 | tf_op jit(solution)/shard_map/ppermute | solution.py:13
  672.7 88.2 %collective-permute-start.153 = (bf16[1024,1024]{1,0:T(8,128)(2,1)}, bf16[1024,1024]{1,0:T(8,128)(2,1)}, u32[]{:S(2)}, u32[]{:S(2)}) collective-permute-start(bf16[1024,1024]{1,0:T(8,128)(2,1)} %get-tuple-element.530), channel_id=1, source_target_pairs={{0,16},{16,0},{1,17},{17,1},{2,18},{18,2},{3,19},{19,3},{4,20},{20... | collective-permute-start | bytes 6291464 | tf_op jit(solution)/shard_map/ppermute | solution.py:13
  672.8 94.2 %collective-permute-start.141 = (bf16[1024,1024]{1,0:T(8,128)(2,1)}, bf16[1024,1024]{1,0:T(8,128)(2,1)}, u32[]{:S(2)}, u32[]{:S(2)}) collective-permute-start(bf16[1024,1024]{1,0:T(8,128)(2,1)} %get-tuple-element.526), channel_id=1, source_target_pairs={{0,16},{16,0},{1,17},{17,1},{2,18},{18,2},{3,19},{19,3},{4,20},{20... | collective-permute-start | bytes 6291464 | tf_op jit(solution)/shard_map/ppermute | solution.py:13
  723.9 19.0 %collective-permute-start.137 = (f32[3,1280]{1,0:T(4,128)S(1)}, f32[3,1280]{1,0:T(4,128)S(1)}, u32[]{:S(2)}, u32[]{:S(2)}) collective-permute-start(f32[3,1280]{1,0:T(4,128)S(1)} %slice.692), channel_id=1, source_target_pairs={{2,0},{4,2},{6,4},{8,6},{10,8},{12,10},{14,12},{3,1},{5,3},{7,5},{... | collective-permute-start | bytes 46088 | tf_op jit(solution)/shard_map/ppermute | solution.py:19
  725.3 17.7 %collective-permute-start.105 = (f32[3,1280]{1,0:T(4,128)S(1)}, f32[3,1280]{1,0:T(4,128)S(1)}, u32[]{:S(2)}, u32[]{:S(2)}) collective-permute-start(f32[3,1280]{1,0:T(4,128)S(1)} %slice.674), channel_id=1, source_target_pairs={{2,0},{4,2},{6,4},{8,6},{10,8},{12,10},{14,12},{3,1},{5,3},{7,5},{... | collective-permute-start | bytes 46088 | tf_op jit(solution)/shard_map/ppermute | solution.py:19
  754.6 16.9 %collective-permute-start.142 = (bf16[1024,1024]{1,0:T(8,128)(2,1)}, bf16[1024,1024]{1,0:T(8,128)(2,1)}, u32[]{:S(2)}, u32[]{:S(2)}) collective-permute-start(bf16[1024,1024]{1,0:T(8,128)(2,1)} %get-tuple-element.528), channel_id=1, source_target_pairs={{0,16},{16,0},{1,17},{17,1},{2,18},{18,2},{3,19},{19,3},{4,20},{20... | collective-permute-start | bytes 6291464 | tf_op jit(solution)/shard_map/ppermute | solution.py:13
  759.5 51.9 %collective-permute-start.151 = (bf16[256]{0:T(256)(128)(2,1)}, bf16[256]{0:T(256)(128)(2,1)}, u32[]{:S(2)}, u32[]{:S(2)}) collective-permute-start(bf16[256]{0:T(256)(128)(2,1)} %select_convert_fusion.10), channel_id=1, source_target_pairs={{0,16},{16,0},{1,17},{17,1},{2,18},{18,2},{3,19},{19,3},{4,20},{20... | collective-permute-start | bytes 1544 | tf_op jit(solution)/shard_map/ppermute | solution.py:13
  760.7 327.8 %all-reduce.12.cloned.1.call-start = ((), (), s32[]{:S(2)}) async-start(), calls=%async_computation.1 | async-start | bytes 12582912 | tf_op jit(solution)/shard_map/psum | solution.py:381
  760.9 25.1 %collective-permute-start.146 = (bf16[16]{0:T(256)(128)(2,1)}, bf16[16]{0:T(256)(128)(2,1)}, u32[]{:S(2)}, u32[]{:S(2)}) collective-permute-start(bf16[16]{0:T(256)(128)(2,1)} %fusion.634), channel_id=1, source_target_pairs={{0,16},{16,0},{1,17},{17,1},{2,18},{18,2},{3,19},{19,3},{4,20},{20... | collective-permute-start | bytes 104 | tf_op jit(solution)/shard_map/ppermute | solution.py:13
  780.2 15.5 %collective-permute-start.138 = (bf16[256,1024]{1,0:T(8,128)(2,1)S(1)}, bf16[256,1024]{1,0:T(8,128)(2,1)S(1)}, u32[]{:S(2)}, u32[]{:S(2)}) collective-permute-start(bf16[256,1024]{1,0:T(8,128)(2,1)S(1)} %fusion.140), channel_id=1, source_target_pairs={{0,1},{1,0},{2,3},{3,2},{4,5},{5,4},{6,7},{7,6},{8,9},{9,8},{10,11... | collective-permute-start | bytes 1572872 | tf_op jit(solution)/shard_map/ppermute | solution.py:13
  783.6 22.9 %collective-permute-start.106 = (bf16[256,1024]{1,0:T(8,128)(2,1)S(1)}, bf16[256,1024]{1,0:T(8,128)(2,1)S(1)}, u32[]{:S(2)}, u32[]{:S(2)}) collective-permute-start(bf16[256,1024]{1,0:T(8,128)(2,1)S(1)} %fusion.138), channel_id=1, source_target_pairs={{0,1},{1,0},{2,3},{3,2},{4,5},{5,4},{6,7},{7,6},{8,9},{9,8},{10,11... | collective-permute-start | bytes 1572872 | tf_op jit(solution)/shard_map/ppermute | solution.py:13
  786.0 26.7 %collective-permute-start.150 = (bf16[4,256]{1,0:T(4,128)(2,1)S(1)}, bf16[4,256]{1,0:T(4,128)(2,1)S(1)}, u32[]{:S(2)}, u32[]{:S(2)}) collective-permute-start(bf16[4,256]{1,0:T(4,128)(2,1)S(1)} %get-tuple-element.121), channel_id=1, source_target_pairs={{0,16},{16,0},{1,17},{17,1},{2,18},{18,2},{3,19},{19,3},{4,20},{20... | collective-permute-start | bytes 6152 | tf_op jit(solution)/shard_map/ppermute | solution.py:13
  795.7 16.4 %collective-permute-start.149 = (bf16[1024]{0:T(1024)(128)(2,1)S(1)}, bf16[1024]{0:T(1024)(128)(2,1)S(1)}, u32[]{:S(2)}, u32[]{:S(2)}) collective-permute-start(bf16[1024]{0:T(1024)(128)(2,1)S(1)} %copy-done.484), channel_id=1, source_target_pairs={{0,16},{16,0},{1,17},{17,1},{2,18},{18,2},{3,19},{19,3},{4,20},{20... | collective-permute-start | bytes 6152 | tf_op jit(solution)/shard_map/ppermute | solution.py:13
  810.8 89.3 %collective-permute-start.139 = (f32[2,256,1024]{2,1,0:T(8,128)}, f32[2,256,1024]{2,1,0:T(8,128)}, u32[]{:S(2)}, u32[]{:S(2)}) collective-permute-start(f32[2,256,1024]{2,1,0:T(8,128)} %fusion.87), channel_id=1, source_target_pairs={{0,16},{16,0},{1,17},{17,1},{2,18},{18,2},{3,19},{19,3},{4,20},{20... | collective-permute-start | bytes 6291464 | tf_op jit(solution)/shard_map/ppermute | solution.py:13
  811.4 44.0 %collective-permute-start.148 = (bf16[4,1024]{1,0:T(4,128)(2,1)S(1)}, bf16[4,1024]{1,0:T(4,128)(2,1)S(1)}, u32[]{:S(2)}, u32[]{:S(2)}) collective-permute-start(bf16[4,1024]{1,0:T(4,128)(2,1)S(1)} %select_convert_fusion.5), channel_id=1, source_target_pairs={{0,16},{16,0},{1,17},{17,1},{2,18},{18,2},{3,19},{19,3},{4,20},{20... | collective-permute-start | bytes 24584 | tf_op jit(solution)/shard_map/ppermute | solution.py:13
  812.2 43.2 %collective-permute-start.144 = (bf16[1024,16]{0,1:T(8,128)(2,1)}, bf16[1024,16]{0,1:T(8,128)(2,1)S(1)}, u32[]{:S(2)}, u32[]{:S(2)}) collective-permute-start(bf16[1024,16]{0,1:T(8,128)(2,1)} %get-tuple-element.524), channel_id=1, source_target_pairs={{0,16},{16,0},{1,17},{17,1},{2,18},{18,2},{3,19},{19,3},{4,20},{20... | collective-permute-start | bytes 98312 | tf_op jit(solution)/shard_map/ppermute | solution.py:13
  (578 other events, 5594.5 us)
Sparse Core Ops, SparseCore 0:
  760.8 109.2 all-reduce.9
  875.5 212.9 all-reduce.11

commit v2 on v1

v2 whole, which is shorter than its diff:
```python
import functools

import jax
import jax.numpy as jnp
from jax import lax
from jax.experimental import pallas as pl
from jax.experimental.pallas import tpu as pltpu
from jax.sharding import PartitionSpec as P

EPS = 1e-05
F32 = jnp.float32
BF16 = jnp.bfloat16
LANES = 128
HALO = 8
VMEM = 24 * 1024 * 1024


def exchange(block, axis, bit):
    route = [(i, i ^ bit) for i in range(lax.axis_size(axis))]
    return lax.ppermute(block, axis, route)


def shifted(block, axis, distance):
    devices = range(lax.axis_size(axis))
    route = [(i - distance, i) for i in devices if i - distance in devices]
    return lax.ppermute(block, axis, route)


def low(value):
    return value.astype(BF16)


def wide(value):
    return value.astype(F32)


def matmul(left, right):
    return jnp.dot(left, right, preferred_element_type=F32)


def lead_dot(left, right):
    return lax.dot_general(left, right, (((0,), (0,)), ((), ())), preferred_element_type=F32)


def tail_dot(left, right):
    return lax.dot_general(left, right, (((1,), (1,)), ((), ())), preferred_element_type=F32)


def head_sum(part):
    bit = 1
    while bit < lax.axis_size("head"):
        part = low(part)
        part = wide(part) + wide(exchange(part, "head", bit))
        bit *= 2
    return part


def parts_of(value, count):
    terms = []
    for _ in range(count):
        term = low(value)
        terms.append(term)
        value = value - wide(term)
    return terms


def dot_parts(left, right, count, dot=matmul):
    return sum(dot(left, term) for term in parts_of(right, count))


def iota(shape, axis):
    return lax.broadcasted_iota(jnp.int32, shape, axis)


def lower_mask(length):
    return iota((length, length), 0) >= iota((length, length), 1)


def expand(values, pair):
    length = values.shape[0]
    early = iota((length, LANES), 1) < LANES // 2
    first = values[:, 2 * pair : 2 * pair + 1]
    second = values[:, 2 * pair + 1 : 2 * pair + 2]
    return jnp.where(early, first, second)


def head_matrix(inner, width):
    return jnp.where(iota((inner, LANES), 0) // width == iota((inner, LANES), 1), 1.0, 0.0).astype(BF16)


def head_sums(values, matrix):
    high, rest = parts_of(values, 2)
    return matmul(high, matrix) + matmul(rest, matrix)


def sigmoid(value):
    return 1.0 / (1.0 + jnp.exp(-value))


def softplus(value):
    tail = jnp.exp(-jnp.abs(value))
    shifted_one = 1.0 + tail
    gap = shifted_one - 1.0
    small = jnp.where(gap == 0.0, tail, jnp.log(shifted_one) * (tail / jnp.where(gap == 0.0, 1.0, gap)))
    return jnp.maximum(value, 0.0) + small


def conv_preact(joined_ref, before_ref, conv_ref, ext_ref):
    length, channels = joined_ref.shape[0], conv_ref.shape[1]
    ext_ref[0:HALO, :] = before_ref[...]
    ext_ref[HALO : HALO + length, :] = joined_ref[:, 0:channels]
    total = conv_ref[4:5, :]
    for tap in range(4):
        total = total + conv_ref[tap : tap + 1, :] * ext_ref[HALO - 3 + tap : HALO - 3 + tap + length, :]
    return total


def decays(joined_ref, head_ref, channels):
    length = joined_ref.shape[0]
    raw = joined_ref[:, channels : channels + LANES] + head_ref[0:1, :]
    step = softplus(raw)
    rate = -jnp.exp(head_ref[1:2, :])
    lower = jnp.where(lower_mask(length), 1.0, 0.0).astype(BF16)
    decay_sum = dot_parts(lower, rate * step, 3)
    return raw, step, rate, decay_sum


def pair_dots(early, mixing_a, mixing_b, values, dot):
    return jnp.where(early, dot(mixing_a, values), dot(mixing_b, values))


def local_kernel(joined_ref, before_ref, conv_ref, head_ref, y_ref, message_ref, read_ref, rise_ref, ext_ref, act_ref):
    length = joined_ref.shape[0]
    channels = conv_ref.shape[1]
    inner = y_ref.shape[1]
    state = read_ref.shape[1]
    pairs = inner // LANES
    preact = conv_preact(joined_ref, before_ref, conv_ref, ext_ref)
    act_ref[...] = preact * sigmoid(preact)
    write_low = low(act_ref[:, inner : inner + state])
    read_low = low(act_ref[:, inner + state : inner + 2 * state])
    read_ref[...] = read_low
    _, step, _, decay_sum = decays(joined_ref, head_ref, channels)
    rise_ref[...] = jnp.exp(decay_sum)
    keep_step = jnp.exp(decay_sum[length - 1 : length, :] - decay_sum) * step
    decay_rows = decay_sum.T
    step_rows = step.T
    gram = tail_dot(read_low, write_low)
    lower = lower_mask(length)
    early = iota((length, LANES), 1) < LANES // 2
    half = inner // 2
    for pair in range(pairs):
        lanes = slice(pair * LANES, (pair + 1) * LANES)
        signal = act_ref[:, lanes]
        signal_low = low(signal)
        mixings = []
        for head in (2 * pair, 2 * pair + 1):
            diff = decay_sum[:, head : head + 1] - decay_rows[head : head + 1, :]
            decay = jnp.exp(jnp.where(lower, diff, -1e30))
            mixings.append(low(gram * decay * step_rows[head : head + 1, :]))
        mixed = pair_dots(early, mixings[0], mixings[1], signal_low, matmul)
        y_ref[:, lanes] = mixed + conv_ref[5:6, lanes] * signal
        local = lead_dot(low(expand(keep_step, pair) * signal), write_low)
        place = pair * LANES
        if half % LANES == 0:
            side, row = place // half, place % half
            message_ref[side, row : row + LANES, :] = low(local)
    heads = 2 * pairs
    per = heads // 2
    for side in range(2):
        column = jnp.exp(decay_rows[side * per : side * per + 8, length - 1 : length])
        fade = jnp.broadcast_to(column, (8, state))
        high = wide(low(fade))
        message_ref[side, half : half + 16, :] = low(jnp.concatenate([high, fade - high], 0))


def output_kernel(y_ref, read_ref, rise_ref, start_ref, gate_ref, mix_ref, w_ref, ssd_ref, part_ref, mixed_ref):
    length, inner = y_ref.shape
    features = w_ref.shape[1]
    squares = jnp.zeros((length, 1), F32)
    for pair in range(inner // LANES):
        lanes = slice(pair * LANES, (pair + 1) * LANES)
        reach = tail_dot(read_ref[...], start_ref[lanes, :])
        ssd_out = y_ref[:, lanes] + expand(rise_ref[...], pair) * reach
        ssd_ref[:, lanes] = ssd_out
        gate = gate_ref[:, lanes]
        gated = ssd_out * (gate * sigmoid(gate))
        squares = squares + jnp.sum(gated * gated, 1, keepdims=True)
        mixed_ref[:, lanes] = low(gated * mix_ref[0:1, lanes])
    part_ref[:, 0:features] = low(matmul(mixed_ref[...], w_ref[...]))
    high = wide(low(squares))
    lane = iota((length, LANES), 1)
    tail = jnp.where(lane == 0, high, jnp.where(lane == 1, squares - high, 0.0))
    part_ref[:, features : features + LANES] = low(tail)


def gate_back_kernel(
    total_inner, grad_ref, w_ref, ssd_ref, gate_ref, scale_ref, branch_ref, mix_ref, rise_ref, read_ref,
    grad_y_ref, gate_low_ref, mixed_ref, start_ref, sums_ref,
):
    length, inner = ssd_ref.shape
    scale = scale_ref[:, 0:1]
    along = jnp.sum(wide(grad_ref[...]) * branch_ref[...], 1, keepdims=True) * (scale * scale / total_inner)
    half = inner // 2
    sums_ref[...] = jnp.zeros(sums_ref.shape, F32)
    for pair in range(inner // LANES):
        lanes = slice(pair * LANES, (pair + 1) * LANES)
        grad_mixed = tail_dot(grad_ref[...], w_ref[lanes, :])
        gain = mix_ref[0:1, lanes]
        gate = gate_ref[:, lanes]
        ssd_out = ssd_ref[:, lanes]
        sigma = sigmoid(gate)
        active = gate * sigma
        gated = ssd_out * active
        normal = gated * scale
        sums_ref[0:1, lanes] = jnp.sum(grad_mixed * normal, 0, keepdims=True)
        mixed_ref[:, lanes] = low(normal * gain)
        grad_gated = scale * (grad_mixed * gain) - gated * along
        grad_y = grad_gated * active
        grad_y_ref[:, lanes] = grad_y
        gate_low_ref[:, lanes] = low(grad_gated * ssd_out * (sigma * (1.0 + gate * (1.0 - sigma))))
        grad_reach = low(grad_y * expand(rise_ref[...], pair))
        grad_start = lead_dot(grad_reach, read_ref[...])
        place = pair * LANES
        if half % LANES == 0:
            side, row = place // half, place % half
            start_ref[side, row : row + LANES, :] = low(grad_start)


def scan_back_kernel(
    joined_ref, before_ref, conv_ref, head_ref, grad_y_ref, start_ref,
    signal_ref, keys_ref, sums_ref, row_ref,
    ext_ref, act_ref, step_ref, gram_ref, prod_ref,
):
    length, inner = grad_y_ref.shape
    channels = conv_ref.shape[1]
    state = start_ref.shape[1]
    pairs = inner // LANES
    preact = conv_preact(joined_ref, before_ref, conv_ref, ext_ref)
    act_ref[...] = preact * sigmoid(preact)
    write_low = low(act_ref[:, inner : inner + state])
    read_low = low(act_ref[:, inner + state : inner + 2 * state])
    _, step, _, decay_sum = decays(joined_ref, head_ref, channels)
    rise = jnp.exp(decay_sum)
    decay_rows = decay_sum.T
    step_rows = step.T
    gram = tail_dot(read_low, write_low)
    lower = lower_mask(length)
    early = iota((length, LANES), 1) < LANES // 2
    lane = iota((length, LANES), 1)
    step_ref[...] = jnp.zeros(step_ref.shape, F32)
    gram_ref[...] = jnp.zeros(gram_ref.shape, F32)
    columns = jnp.zeros((length, LANES), F32)
    grad_read = jnp.zeros((length, state), F32)
    row_ref[...] = jnp.zeros(row_ref.shape, F32)
    for pair in range(pairs):
        lanes = slice(pair * LANES, (pair + 1) * LANES)
        signal = act_ref[:, lanes]
        signal_low = low(signal)
        grad_y = grad_y_ref[:, lanes]
        grad_y_low = low(grad_y)
        mixings = []
        for head in (2 * pair, 2 * pair + 1):
            mine = early if head % 2 == 0 else jnp.logical_not(early)
            own = jnp.where(mine, grad_y, 0.0)
            grad_mixing = tail_dot(low(own), signal_low)
            diff = decay_sum[:, head : head + 1] - decay_rows[head : head + 1, :]
            decay = jnp.exp(jnp.where(lower, diff, -1e30))
            step_row = step_rows[head : head + 1, :]
            plain = gram * decay
            mixings.append(low(plain * step_row))
            gram_ref[...] += grad_mixing * decay * step_row
            weighed = grad_mixing * plain
            step_ref[head : head + 1, :] = jnp.sum(weighed, 0, keepdims=True)
            columns = jnp.where(lane == head, jnp.sum(weighed * step_row, 1, keepdims=True), columns)
        back = pair_dots(early, mixings[0], mixings[1], grad_y_low, lead_dot)
        signal_ref[:, lanes] = conv_ref[5:6, lanes] * grad_y + back
        row_ref[0:1, lanes] = jnp.sum(grad_y * signal, 0, keepdims=True)
        start = start_ref[lanes, :]
        reach = tail_dot(read_low, start)
        prod_ref[:, lanes] = grad_y * reach
        grad_read = grad_read + matmul(low(grad_y * expand(rise, pair)), start)
    gram_parts = parts_of(gram_ref[...], 2)
    keys_ref[:, 0:state] = sum(lead_dot(part, read_low) for part in gram_parts)
    keys_ref[:, state : 2 * state] = grad_read + sum(matmul(part, write_low) for part in gram_parts)
    grad_step = step_ref[...].T
    matrix = head_matrix(inner, LANES // 2)
    sums_ref[:, 0:LANES] = columns - step * grad_step + head_sums(prod_ref[...], matrix) * rise
    sums_ref[:, LANES : 2 * LANES] = grad_step


def state_back_kernel(
    joined_ref, before_ref, conv_ref, head_ref, signal_ref, keys_ref, sums_ref, local_ref, start_ref,
    pre_ref, raw_ref, conv_sums_ref, head_sums_ref,
    ext_ref, prod_ref,
):
    length, inner = signal_ref.shape
    channels = conv_ref.shape[1]
    state = start_ref.shape[1]
    preact = conv_preact(joined_ref, before_ref, conv_ref, ext_ref)
    raw, step, rate, decay_sum = decays(joined_ref, head_ref, channels)
    keep = jnp.exp(decay_sum[length - 1 : length, :] - decay_sum)
    tail = keep * step
    sigma = sigmoid(preact)
    active = preact * sigma
    slope = sigma * (1.0 + preact * (1.0 - sigma))
    write_low = low(active[:, inner : inner + state])
    grad_write = keys_ref[:, 0:state]
    conv_sums_ref[...] = jnp.zeros(conv_sums_ref.shape, F32)

    def finish(grad, lanes):
        grad_pre = grad * slope[:, lanes]
        pre_ref[:, lanes] = grad_pre
        for tap in range(4):
            rows = ext_ref[HALO - 3 + tap : HALO - 3 + tap + length, lanes]
            conv_sums_ref[tap : tap + 1, lanes] = jnp.sum(grad_pre * rows, 0, keepdims=True)
        conv_sums_ref[4:5, lanes] = jnp.sum(grad_pre, 0, keepdims=True)

    for pair in range(inner // LANES):
        lanes = slice(pair * LANES, (pair + 1) * LANES)
        signal = active[:, lanes]
        local = local_ref[lanes, :]
        spread = tail_dot(write_low, local)
        wide_tail = expand(tail, pair)
        prod_ref[:, lanes] = signal * spread
        grad_write = grad_write + matmul(low(wide_tail * signal), local)
        finish(signal_ref[:, lanes] + wide_tail * spread, lanes)
    finish(grad_write, slice(inner, inner + state))
    finish(keys_ref[:, state : 2 * state], slice(inner + state, inner + 2 * state))
    matrix = head_matrix(inner, LANES // 2)
    grad_tail = head_sums(prod_ref[...], matrix)
    grad_step = sums_ref[:, LANES : 2 * LANES] + grad_tail * keep
    tail_log = grad_tail * tail
    product = wide(local_ref[...]) * wide(start_ref[...])
    by_state = sum(lead_dot(matrix, part) for part in parts_of(product, 2))
    ones = jnp.ones((8, state), BF16)
    totals = sum(tail_dot(ones, part) for part in parts_of(by_state, 2))[0:1, :]
    fade = jnp.exp(decay_sum[length - 1 : length, :])
    last = iota((length, LANES), 0) == length - 1
    extra = jnp.sum(tail_log, 0, keepdims=True) + totals * fade
    grad_decay = sums_ref[:, 0:LANES] - tail_log + jnp.where(last, extra, 0.0)
    upper = jnp.where(iota((length, length), 1) >= iota((length, length), 0), 1.0, 0.0).astype(BF16)
    grad_log = dot_parts(upper, grad_decay, 3)
    grad_step = grad_step + grad_log * rate
    grad_raw = grad_step * sigmoid(raw)
    raw_ref[...] = low(grad_raw)
    head_sums_ref[...] = jnp.zeros(head_sums_ref.shape, F32)
    head_sums_ref[0:1, :] = jnp.sum(grad_raw, 0, keepdims=True)
    head_sums_ref[1:2, :] = jnp.sum(grad_log * step, 0, keepdims=True) * rate


def input_back_kernel(pre_ref, after_ref, conv_ref, raw_ref, gate_ref, w_ref, w_gate_ref, joined_ref, part_ref, ext_ref):
    length, channels = pre_ref.shape
    ext_ref[0:length, :] = pre_ref[...]
    ext_ref[length : length + HALO, :] = after_ref[...]
    total = jnp.zeros((length, channels), F32)
    for tap in range(4):
        total = total + conv_ref[tap : tap + 1, :] * ext_ref[3 - tap : 3 - tap + length, :]
    joined_ref[:, 0:channels] = low(total)
    joined_ref[:, channels : channels + LANES] = raw_ref[...]
    part_ref[...] = low(tail_dot(joined_ref[...], w_ref[...]) + tail_dot(gate_ref[...], w_gate_ref[...]))


def normalized(value, gain):
    return low(value * lax.rsqrt(jnp.mean(value * value, 1, keepdims=True) + EPS) * gain)


def merge_kernel(total_inner, part_ref, other_ref, entry_ref, gain_ref, out_ref, branch_ref, scale_ref, normed_ref):
    features = entry_ref.shape[1]
    total = wide(part_ref[...]) + wide(other_ref[...])
    squares = jnp.sum(total[:, features:], 1, keepdims=True)
    scale = lax.rsqrt(squares / total_inner + EPS)
    branch = scale * total[:, :features]
    out = low(wide(entry_ref[...]) + branch)
    out_ref[...] = out
    branch_ref[...] = branch
    scale_ref[...] = jnp.broadcast_to(scale, scale_ref.shape)
    normed_ref[...] = normalized(wide(out), gain_ref[0:1, :])


def entry_back_kernel(part_ref, other_ref, entry_ref, gain_ref, grad_ref, out_ref, low_ref, sums_ref):
    grad_normed = wide(part_ref[...]) + wide(other_ref[...])
    value = wide(entry_ref[...])
    inverse_rms = lax.rsqrt(jnp.mean(value * value, 1, keepdims=True) + EPS)
    sums_ref[...] = jnp.zeros(sums_ref.shape, F32)
    sums_ref[0:1, :] = jnp.sum(grad_normed * value * inverse_rms, 0, keepdims=True)
    scaled = grad_normed * gain_ref[0:1, :]
    mean = jnp.mean(scaled * value, 1, keepdims=True)
    out = wide(grad_ref[...]) + inverse_rms * scaled - value * (inverse_rms * inverse_rms * inverse_rms * mean)
    out_ref[...] = out
    low_ref[...] = low(out)


def product_kernel(
    section_ref, normed_a, normed_b, grad_a, grad_b, joined_a, joined_b, gate_a, gate_b, mixed_a, mixed_b,
    conv_a, conv_b, head_a, head_b, mix_a, mix_b, skip_a, skip_b, gain_a, gain_b, sent_ref, own_ref,
):
    pl.when(pl.program_id(0) == 0)(
        lambda: fill_products(
            normed_a, normed_b, grad_a, grad_b, joined_a, joined_b, gate_a, gate_b, mixed_a, mixed_b,
            conv_a, conv_b, head_a, head_b, mix_a, mix_b, skip_a, skip_b, gain_a, gain_b, sent_ref,
        )
    )
    pl.when(pl.program_id(0) == 1)(
        lambda: fill_products(
            normed_a, normed_b, grad_a, grad_b, joined_a, joined_b, gate_a, gate_b, mixed_a, mixed_b,
            conv_a, conv_b, head_a, head_b, mix_a, mix_b, skip_a, skip_b, gain_a, gain_b, own_ref,
        )
    )


def fill_products(
    normed_a, normed_b, grad_a, grad_b, joined_a, joined_b, gate_a, gate_b, mixed_a, mixed_b,
    conv_a, conv_b, head_a, head_b, mix_a, mix_b, skip_a, skip_b, gain_a, gain_b, out_ref,
):
    rows = normed_a.shape[1]
    wide_in, inner = joined_a.shape[1], gate_a.shape[1]
    channels = wide_in - LANES
    gate_at, out_at = wide_in, wide_in + inner
    both = lambda left_a, right_a, left_b, right_b: low(
        lead_dot(left_a[...], right_a[...]) + lead_dot(left_b[...], right_b[...])
    )
    out_ref[0:rows, 0:wide_in] = both(normed_a, joined_a, normed_b, joined_b)
    out_ref[0:rows, gate_at:out_at] = both(normed_a, gate_a, normed_b, gate_b)
    out_ref[0:rows, out_at : out_at + inner] = both(grad_a, mixed_a, grad_b, mixed_b)
    pad = lambda value: low(jnp.concatenate([value, jnp.zeros(value.shape, F32)], 0))
    last = slice(rows, rows + 16)
    out_ref[last, 0:channels] = pad(conv_a[...] + conv_b[...])
    out_ref[last, channels:wide_in] = pad(head_a[...] + head_b[...])
    place = iota((8, inner), 0)
    mixes = mix_a[0:1, :] + mix_b[0:1, :]
    skips = skip_a[0:1, :] + skip_b[0:1, :]
    out_ref[last, gate_at:out_at] = pad(jnp.where(place == 0, mixes, jnp.where(place == 1, skips, 0.0)))
    gains = jnp.zeros((8, inner), F32)
    for piece in range(gain_a.shape[1] // inner):
        lanes = slice(piece * inner, (piece + 1) * inner)
        gains = jnp.where(place == piece, gain_a[0:1, lanes] + gain_b[0:1, lanes], gains)
    out_ref[last, out_at : out_at + inner] = pad(gains)


def add_kernel(inner, channels, own_ref, other_ref, keys_ref, across_ref, out_ref):
    step = 48
    for at in range(0, own_ref.shape[0], step):
        rows = slice(at, at + step)
        total = wide(own_ref[rows, :]) + wide(other_ref[rows, :])
        out_ref[rows, :] = low(total)
        keys = wide(keys_ref[rows, :]) + wide(across_ref[rows, :])
        out_ref[rows, inner:channels] = low(total[:, inner:channels] + keys)


def unpack_kernel(inner, keys, section_ref, early_ref, late_ref, other_ref, x_ref, keys_ref, step_ref, gate_ref, out_ref):
    section = section_ref[0]
    mine = pl.program_id(0) == section
    own = jnp.where(section == 0, early_ref[...], late_ref[...])
    value = wide(jnp.where(mine, own, other_ref[...]))
    wide_in = inner + keys + LANES
    x_ref[...] = value[:, :inner]
    keys_ref[...] = value[:, inner : inner + keys]
    step_ref[...] = value[:, inner + keys : wide_in]
    gate_ref[...] = value[:, wide_in : wide_in + inner]
    out_ref[...] = value[:, wide_in + inner :].T


def call(kernel, outs, scratch, micros, *args):
    shapes = [jax.ShapeDtypeStruct(shape, dtype) for shape, dtype in outs]
    moved = sum(a.size * a.dtype.itemsize for a in args) + sum(s.size * s.dtype.itemsize for s in shapes)
    return pl.pallas_call(
        kernel,
        out_shape=shapes,
        in_specs=[pl.BlockSpec(memory_space=pltpu.VMEM)] * len(args),
        out_specs=[pl.BlockSpec(memory_space=pltpu.VMEM)] * len(shapes),
        scratch_shapes=[pltpu.VMEM(shape, dtype) for shape, dtype in scratch],
        compiler_params=pltpu.CompilerParams(vmem_limit_bytes=VMEM),
        cost_estimate=pl.CostEstimate(flops=int(micros * 1.1e9), bytes_accessed=moved, transcendentals=0),
    )(*args)


def pick(halves, index):
    return lax.dynamic_index_in_dim(halves, index, 0, False)


def faded(state, fade):
    per = fade.shape[0]
    rows, lanes = state.shape
    return (state.reshape(per, rows // per, lanes) * fade[:, None, :]).reshape(rows, lanes)


def fade_rows(fade):
    per = fade.shape[0]
    high = wide(low(fade))
    pad = lambda rows: jnp.pad(rows, ((0, 8 - per), (0, 0)))
    return low(jnp.concatenate([pad(high), pad(fade - high)], 0))


def read_fade(rows, per):
    return wide(rows[:per]) + wide(rows[8 : 8 + per])


def scan_states(message, per, fades, reverse):
    blocks = lax.axis_size("seq")
    half = message.shape[1] - (0 if reverse else 16)
    state = message.shape[2]
    if blocks != 8:
        local = message[:, :half].reshape(2 * half, state)
        if fades is None:
            fades = jnp.concatenate([read_fade(message[side, half:], per) for side in range(2)], 0)
        running = jnp.zeros((2 * half, state), F32)
        for _ in range(blocks - 1):
            running = shifted(faded(running, fades) + wide(local), "seq", -1 if reverse else 1)
        return low(running), fades
    side = lax.axis_index("seq") % 2
    even = side == 0
    mine = pick(message, side)
    other = exchange(pick(message, 1 - side), "seq", 1)
    first = jnp.where(even, mine, other)
    second = jnp.where(even, other, mine)
    if fades is None:
        fades = (read_fade(first[half:], per), read_fade(second[half:], per))
    first, second = wide(first[:half]), wide(second[:half])
    fade_first, fade_second = fades
    if reverse:
        total = faded(second, fade_first) + first
    else:
        total = faded(first, fade_second) + second
    sent = jnp.concatenate([low(total), fade_rows(fade_first * fade_second)], 0)
    sign = -1 if reverse else 1
    arrived = [shifted(sent, "seq", sign * 2 * hop) for hop in (1, 2, 3)]
    states = [wide(one[:half]) for one in arrived]
    factors = [read_fade(one[half:], per) for one in arrived]
    entering = states[0] + faded(states[1] + faded(states[2], factors[1]), factors[0])
    if reverse:
        for_second = entering
        for_first = second + faded(entering, fade_second)
    else:
        for_first = entering
        for_second = first + faded(entering, fade_first)
    for_first, for_second = low(for_first), low(for_second)
    kept = jnp.where(even, for_first, for_second)
    back = exchange(jnp.where(even, for_second, for_first), "seq", 1)
    return jnp.concatenate([jnp.where(even, kept, back), jnp.where(even, back, kept)], 0), fades


def layer_forward(entries, normed, weights, next_gain):
    count = len(entries)
    inner = weights["w_z"].shape[1]
    channels = weights["conv"].shape[1]
    features = weights["w_out"].shape[1]
    state = (channels - inner) // 2
    length = entries[0].shape[0]
    heads = 2 * inner // LANES
    joined = [matmul(one, weights["w_in"]) for one in normed]
    before = [shifted(one[length - HALO :, :channels], "seq", 1) for one in joined]
    gate = [matmul(one, weights["w_z"]) for one in normed]
    locals_ = [
        call(
            local_kernel,
            [
                ((length, inner), F32),
                ((2, inner // 2 + 16, state), BF16),
                ((length, state), BF16),
                ((length, LANES), F32),
            ],
            [((HALO + length, channels), F32), ((length, channels), F32)],
            3.2,
            joined[index], before[index], weights["conv"], weights["head"],
        )
        for index in range(count)
    ]
    scans = [scan_states(one[1], heads // 2, None, False) for one in locals_]
    finished = [
        call(
            output_kernel,
            [((length, inner), F32), ((length, features + LANES), BF16)],
            [((length, inner), BF16)],
            2.5,
            one[0], one[2], one[3], scan[0], gate[index], weights["mix"], weights["w_out"],
        )
        for index, (one, scan) in enumerate(zip(locals_, scans))
    ]
    outputs = []
    next_normed = []
    kept = []
    total_inner = inner * lax.axis_size("head")
    for index in range(count):
        ssd_out, part = finished[index]
        bit = 1
        while 2 * bit < lax.axis_size("head"):
            total = wide(part) + wide(exchange(part, "head", bit))
            squares = jnp.sum(total[:, features:], 1, keepdims=True)
            high = wide(low(squares))
            tail = jnp.pad(jnp.concatenate([high, squares - high], 1), ((0, 0), (0, LANES - 2)))
            part = low(jnp.concatenate([total[:, :features], tail], 1))
            bit *= 2
        out, branch, scale, later = call(
            functools.partial(merge_kernel, total_inner),
            [
                ((length, features), BF16),
                ((length, features), F32),
                ((length, LANES), F32),
                ((length, features), BF16),
            ],
            [],
            1.0,
            part, exchange(part, "head", bit), entries[index], next_gain,
        )
        outputs.append(out)
        next_normed.append(later)
        kept.append(
            dict(
                entry=entries[index], normed=normed[index],
                joined=joined[index], before=before[index], gate=gate[index],
                read=locals_[index][2], rise=locals_[index][3], start=scans[index][0],
                fades=scans[index][1], ssd_out=ssd_out, scale=scale, branch=branch,
            )
        )
    return outputs, next_normed, kept


def layer_backward(grads, lows, kept, weights):
    count = len(grads)
    inner = weights["w_z"].shape[1]
    channels = weights["conv"].shape[1]
    features = weights["w_out"].shape[1]
    state = (channels - inner) // 2
    length = grads[0].shape[0]
    heads = 2 * inner // LANES
    total_inner = inner * lax.axis_size("head")
    gates = []
    for grad_low, one in zip(lows, kept):
        gates.append(
            call(
                functools.partial(gate_back_kernel, total_inner),
                [
                    ((length, inner), F32),
                    ((length, inner), BF16),
                    ((length, inner), BF16),
                    ((2, inner // 2, state), BF16),
                    ((8, inner), F32),
                ],
                [],
                3.9,
                grad_low, weights["w_out"], one["ssd_out"], one["gate"], one["scale"],
                one["branch"], weights["mix"], one["rise"], one["read"],
            )
        )
    scans = [scan_states(gate[3], heads // 2, one["fades"], True)[0] for gate, one in zip(gates, kept)]
    mixes = [
        call(
            scan_back_kernel,
            [
                ((length, inner), F32),
                ((length, 2 * state), F32),
                ((length, 2 * LANES), F32),
                ((8, inner), F32),
            ],
            [
                ((HALO + length, channels), F32),
                ((length, channels), F32),
                ((LANES, length), F32),
                ((length, length), F32),
                ((length, inner), F32),
            ],
            6.8,
            one["joined"], one["before"], weights["conv"], weights["head"], gate[0], one["start"],
        )
        for gate, one in zip(gates, kept)
    ]
    states = [
        call(
            state_back_kernel,
            [
                ((length, channels), F32),
                ((length, LANES), BF16),
                ((8, channels), F32),
                ((8, LANES), F32),
            ],
            [((HALO + length, channels), F32), ((length, inner), F32)],
            4.1,
            one["joined"], one["before"], weights["conv"], weights["head"],
            mix[0], mix[1], mix[2], scan, one["start"],
        )
        for mix, scan, one in zip(mixes, scans, kept)
    ]
    after = [shifted(one[0][:HALO], "seq", -1) for one in states]
    inputs = [
        call(
            input_back_kernel,
            [((length, channels + LANES), BF16), ((length, features), BF16)],
            [((length + HALO, channels), F32)],
            2.0,
            one[0], rim, weights["conv"], one[1], gate[1], weights["w_in"], weights["w_z"],
        )
        for one, rim, gate in zip(states, after, gates)
    ]
    results = []
    for index in range(count):
        one = kept[index]
        part = inputs[index][1]
        bit = 1
        while 2 * bit < lax.axis_size("head"):
            part = low(wide(part) + wide(exchange(part, "head", bit)))
            bit *= 2
        results.append(
            call(
                entry_back_kernel,
                [((length, features), F32), ((length, features), BF16), ((8, features), F32)],
                [],
                1.2,
                part, exchange(part, "head", bit), one["entry"], weights["gain"], grads[index],
            )
        )
    pairs = (
        [one["normed"] for one in kept], lows, [one[0] for one in inputs], [one[1] for one in gates],
        [one[2] for one in gates], [one[2] for one in states], [one[3] for one in states],
        [one[4] for one in gates], [one[3] for one in mixes], [one[2] for one in results],
    )
    return results, reduced(pairs, inner, channels)


NAMES = (
    "norm_gain", "w_z", "w_x", "w_bc", "w_dt", "dt_bias", "a_log", "d_skip",
    "conv_x", "conv_bias_x", "conv_bc", "conv_bias_bc", "mix_gain", "w_out",
)


def packed(mine):
    inner = mine["w_z"].shape[1]
    lanes = lambda rows, width: jnp.pad(rows, ((0, 0), (0, width - rows.shape[1])))
    heads = mine["w_dt"].shape[1]
    w_in = jnp.concatenate([mine["w_x"], mine["w_bc"], lanes(mine["w_dt"], LANES)], 1)
    keys = mine["w_bc"].shape[1]
    bias = jnp.concatenate([mine["conv_bias_x"], mine["conv_bias_bc"]], 0)[None]
    skip = lanes(jnp.repeat(mine["d_skip"], inner // heads)[None], inner + keys)
    conv = jnp.concatenate([mine["conv_x"], mine["conv_bc"]], 1)
    rows = jnp.concatenate([conv, bias, skip, jnp.zeros((2, inner + keys), F32)], 0)
    head = lanes(jnp.stack([mine["dt_bias"], mine["a_log"]]), LANES)
    vectors = jnp.concatenate([lanes(head, LANES), jnp.zeros((6, LANES), F32)], 0)
    mix = jnp.pad(mine["mix_gain"][None], ((0, 7), (0, 0)))
    gain = jnp.pad(mine["norm_gain"][None], ((0, 7), (0, 0)))
    return dict(w_in=w_in, w_z=mine["w_z"], w_out=mine["w_out"], small=jnp.concatenate([rows, vectors, mix, gain], 1))


def both_layers(mine):
    first = lax.axis_index("section") == 0
    inner = mine["w_z"].shape[1]
    channels = inner + mine["w_bc"].shape[1]
    own = packed(mine)
    other = {name: exchange(own[name], "section", 1) for name in ("small", "w_in")}
    own["w_z"], own["w_out"], other["w_in"] = lax.optimization_barrier(
        (own["w_z"], own["w_out"], other["w_in"])
    )
    other.update({name: exchange(own[name], "section", 1) for name in ("w_z", "w_out")})

    def layer(flag):
        chosen = {name: jnp.where(flag, own[name], other[name]) for name in own}
        small = chosen.pop("small")
        chosen["conv"] = small[:, :channels]
        chosen["head"] = small[:, channels : channels + LANES]
        chosen["mix"] = small[:, channels + LANES : channels + LANES + inner]
        chosen["gain"] = small[:, channels + LANES + inner :]
        return chosen

    return layer(first), layer(~first)


def reduced(pairs, inner, channels):
    section = lax.axis_index("section")
    length, features = pairs[0][0].shape
    half = features // 2
    width = channels + LANES + 2 * inner
    whole = lambda array: pl.BlockSpec(array.shape, lambda i, side: (0, 0))
    split = pl.BlockSpec((length, half), lambda i, side: (0, (1 - side[0]) * (1 - i) + side[0] * i))
    flat = [array for pair in pairs for array in pair]
    given = pl.BlockSpec((half + 16, width), lambda i, side: (0, 0))
    shape = jax.ShapeDtypeStruct((half + 16, width), BF16)
    sent, own = pl.pallas_call(
        product_kernel,
        grid_spec=pltpu.PrefetchScalarGridSpec(
            num_scalar_prefetch=1,
            grid=(2,),
            in_specs=[split] * 4 + [whole(array) for array in flat[4:]],
            out_specs=[given, given],
        ),
        out_shape=[shape, shape],
        compiler_params=pltpu.CompilerParams(vmem_limit_bytes=2 * VMEM),
        cost_estimate=pl.CostEstimate(flops=8 * 10**9, bytes_accessed=1 << 24, transcendentals=0),
    )(jnp.full((1,), section, jnp.int32), *flat)
    other = exchange(sent, "section", 1)
    heads = lax.axis_size("head")
    if heads == 2:
        keys = exchange(own[:, inner:channels], "head", 1)
        route = [(i, i ^ 3) for i in range(4)]
        across = lax.ppermute(sent[:, inner:channels], ("section", "head"), route)
    else:
        mine = wide(own[:, inner:channels]) + wide(other[:, inner:channels])
        keys = low(head_sum(mine) - mine)
        across = jnp.zeros_like(keys)
    return call(
        functools.partial(add_kernel, inner, channels), [(own.shape, BF16)], [], 4.0, own, other, keys, across
    )[0]


def shards(hidden_in, order, cotangent, *params):
    mine = {name: param[0] for name, param in zip(NAMES, params)}
    layers = both_layers(mine)
    sections = lax.axis_size("section")
    section = lax.axis_index("section")
    first = section == 0
    count = order.shape[0] // sections
    base = section * count
    inner = mine["w_z"].shape[1]
    channels = inner + mine["w_bc"].shape[1]
    features = hidden_in.shape[2]
    entries = [pick(hidden_in, order[base + index]) for index in range(count)]
    gains = [weights["gain"] for weights in layers]
    normed = [normalized(wide(entry), gains[0][0:1]) for entry in entries]
    outputs = []
    kept = []
    for index, weights in enumerate(layers):
        entries, normed, one = layer_forward(entries, normed, weights, gains[1])
        outputs.append(jnp.stack(entries))
        kept.append(one)
    incoming = [pick(cotangent, base + index) for index in range(count)]
    results, late = layer_backward(incoming, incoming, kept[1], layers[1])
    late_grads = jnp.stack([one[0] for one in results])
    wides = [one[0] for one in results]
    lows = [one[1] for one in results]
    results, early = layer_backward(lows, lows, kept[0], layers[0])
    early_grads = jnp.stack([one[0] for one in results])
    early, late = lax.psum((early, late), "seq")

    def swapped(early, late):
        return exchange(jnp.where(first, late, early), "section", 1)

    def to_owner(early, late):
        own, sent = jnp.where(first, early, late), swapped(early, late)
        return jnp.concatenate([jnp.where(first, own, sent), jnp.where(first, sent, own)], 0)

    activations = to_owner(outputs[0], outputs[1])[None]
    grads = to_owner(early_grads, late_grads)[None]
    half = features // 2
    keys_width = channels - inner
    early, late, activations, grads = lax.optimization_barrier((early, late, activations, grads))
    other = swapped(early, late)
    block = 128
    steps = half // block
    width = early.shape[1]
    taken = pl.BlockSpec((block, width), lambda side, i: (i, 0))
    given = lambda lanes: pl.BlockSpec((block, lanes), lambda side, i: (side * steps + i, 0))
    shape = lambda rows, lanes: jax.ShapeDtypeStruct((rows, lanes), F32)
    w_x, w_bc, w_dt, w_z, w_out = pl.pallas_call(
        functools.partial(unpack_kernel, inner, keys_width),
        grid=(2, steps),
        out_shape=[
            shape(features, inner), shape(features, keys_width), shape(features, LANES),
            shape(features, inner), shape(inner, features),
        ],
        in_specs=[pl.BlockSpec(memory_space=pltpu.SMEM), taken, taken, taken],
        out_specs=[
            given(inner), given(keys_width), given(LANES), given(inner),
            pl.BlockSpec((inner, block), lambda side, i: (0, side * steps + i)),
        ],
        compiler_params=pltpu.CompilerParams(vmem_limit_bytes=VMEM),
    )(jnp.full((1,), section, jnp.int32), early, late, other)
    rows = wide(jnp.where(first, early[half : half + 8], late[half : half + 8]))
    heads = mine["w_dt"].shape[1]
    wide_in = channels + LANES
    mixes = rows[:, wide_in : wide_in + inner]
    gains = rows[: features // inner, wide_in + inner :].reshape(features)
    results = dict(
        norm_gain=gains,
        w_z=w_z,
        w_x=w_x,
        w_bc=w_bc,
        w_dt=w_dt[:, :heads],
        dt_bias=rows[0, channels : channels + heads],
        a_log=rows[1, channels : channels + heads],
        d_skip=jnp.sum(mixes[1].reshape(heads, -1), 1),
        conv_x=rows[:4, :inner],
        conv_bias_x=rows[4, :inner],
        conv_bc=rows[:4, inner:channels],
        conv_bias_bc=rows[4, inner:channels],
        mix_gain=mixes[0],
        w_out=w_out,
    )
    return (activations, grads) + tuple(results[name][None] for name in NAMES)


def solution(mesh):
    in_specs = (
        P(None, "seq", None),
        P(),
        P(None, "seq", None),
        P("section", None),
        P("section", None, "head"),
        P("section", None, "head"),
        P("section", None, None),
        P("section", None, "head"),
        P("section", "head"),
        P("section", "head"),
        P("section", "head"),
        P("section", None, "head"),
        P("section", "head"),
        P("section", None, None),
        P("section", None),
        P("section", "head"),
        P("section", "head", None),
    )
    out_specs = (
        P("section", None, "seq", None),
        P("section", None, "seq", None),
        P("section", None),
        P("section", None, "head"),
        P("section", None, "head"),
        P("section", None, None),
        P("section", None, "head"),
        P("section", "head"),
        P("section", "head"),
        P("section", "head"),
        P("section", None, "head"),
        P("section", "head"),
        P("section", None, None),
        P("section", None),
        P("section", "head"),
        P("section", "head", None),
    )
    return jax.shard_map(shards, mesh=mesh, in_specs=in_specs, out_specs=out_specs, check_vma=False)
```

time: 1120 us -> 657 us (0.59)
  other arithmetic: 182 us -> 21.9 us
  local copies, waits for them, and re-layouts: 185 us -> 28 us
  matrix products: 159 us -> 6.82 us
  Pallas kernels: 0 us -> 123 us
  starting transfers between devices: 221 us -> 120 us
  blocking collectives: 75.8 us -> 0 us
  waiting for transfers between devices: 257 us -> 326 us
    ppermute x146 -> x35, starting transfers between devices: 202 us -> 34.7 us  [exchange(): return lax.ppermute(block, axis, route)]
    dot_general x66 -> x0, matrix products: 129 us -> none  [the longest x32 48.1 us: tail_dot(): lax.dot_general(left, right, (((1,), (1,)), ((), ())), preferred_element_...]
    pallas_call x0 -> x37, Pallas kernels: none -> 123 us  [the longest x34 98.3 us: call(): pl.pallas_call(kernel, out_shape=shapes, in_specs=[pl.BlockSpec(memory_sp...]
    psum x2 -> x0, blocking collectives: 75.8 us -> none  [reduced(): return lax.psum(total, axes)]
    ppermute x8 -> x32, starting transfers between devices: 19.1 us -> 82.4 us  [shifted(): return lax.ppermute(block, axis, route)]
    psum x2 -> x1, waiting for transfers between devices: 183 us -> 237 us  [shards(): early, late = lax.psum((early, late), 'seq')]
    unnamed x1130 -> x176, local copies, waits for them, and re-layouts: 68.3 us -> 19.6 us
    reduce_sum x39 -> x2, other arithmetic: 48.3 us -> 0.92 us  [the longest x1 0.63 us: shards(): jnp.sum(mixes[1].reshape(heads, -1), 1)]
  transfers between devices with their start and end apart: 156 -> 70, of which waited for: 34 -> 30; matrix products, arithmetic and copies ran while one was open for 37% -> 5% of each run, Pallas kernels for 0% -> 17%
where the time goes in v2:
time: 657 us; the launch traced here: 647 us
  waiting for transfers between devices  326 us (50%)
  Pallas kernels  123 us (19%)
  starting transfers between devices  120 us (18%)
  local copies, waits for them, and re-layouts  28 us (4%)
  other arithmetic  21.9 us (3%)
  between operations  20.4 us (3%)
  matrix products  6.82 us (1%)
    psum x1, waiting for transfers between devices, shards(): early, late = lax.psum((early, late), 'seq')  237 us
    pallas_call x34, Pallas kernels, call(): pl.pallas_call(kernel, out_shape=shapes, in_specs=[pl.BlockSpec(memory_sp...  98.3 us
    ppermute x32, starting transfers between devices, shifted(): return lax.ppermute(block, axis, route)  82.4 us
    ppermute x35, waiting for transfers between devices, exchange(): return lax.ppermute(block, axis, route)  52.5 us
    ppermute x35, starting transfers between devices, exchange(): return lax.ppermute(block, axis, route)  34.7 us
    ppermute x32, waiting for transfers between devices, shifted(): return lax.ppermute(block, axis, route)  33.1 us
    unnamed x176, local copies, waits for them, and re-layouts  19.6 us
    pallas_call x2, Pallas kernels, reduced(): pl.pallas_call(product_kernel, grid_spec=pltpu.PrefetchScalarGridSpec(num...  15.3 us
  transfers between devices with their start and end apart: 70, of which 30 were waited for; matrix products, arithmetic and copies ran while one was open for 5% of the time, Pallas kernels for 17%

profile of v2, /device:TPU:0, one launch (start us, length us, event | category | flops | bytes accessed | tf_op | source)
XLA Modules:
  0.0 646.9 jit_solution(7654928471394044153)
XLA Ops:
  8.3 3.2 fusion.1
  20.1 2.5 broadcast_select_fusion.1
  23.6 4.8 collective-permute-start.2
  29.5 3.5 collective-permute-start.25
  33.0 3.1 shard_map.288
  37.7 3.2 shard_map.299
  41.6 4.4 collective-permute-start.6
  47.3 2.5 collective-permute-start.4
  50.0 2.2 collective-permute-done.5
  52.2 7.7 %collective-permute-start.29 = (bf16[528,128]{1,0:T(8,128)(2,1)S(1)}, bf16[528,128]{1,0:T(8,128)(2,1)S(1)}, u32[]{:S(2)}, u32[]{:S(2)}) collective-permute-start(bf16[528,128]{1,0:T(8,128)(2,1)S(1)} %pad_maximum_fusion.21), channel_id=1, source_target_pairs={{0,12},{2,14},{1,13},{3,15},{16,28},{18,30},{17,29},{19,31}} | collective-permute-start | bytes 405512 | tf_op jit(solution)/shard_map/ppermute | solution.py:26
  59.9 1.9 collective-permute-start.28
  61.8 2.1 collective-permute-start.27
  64.1 2.5 collective-permute-done.28
  69.4 3.3 collective-permute-done.7
  84.2 10.7 %collective-permute-done.10.other_ref = bf16[256,1152]{1,0:T(8,128)(2,1)S(1)} collective-permute-done((bf16[256,1152]{1,0:T(8,128)(2,1)S(1)}, bf16[256,1152]{1,0:T(8,128)(2,1)S(1)}, u32[]{:S(2)}, u32[]{:S(2)}) %collective-permute-start.10) | collective-permute-done | bytes 589856 | tf_op jit(solution)/shard_map/ppermute | solution.py:20
  96.4 2.5 collective-permute-start.11
  99.6 5.9 collective-permute-done.31.other_ref
  108.7 2.5 collective-permute-start.32
  111.2 3.1 shard_map.291
  114.4 5.2 collective-permute-start.12
  119.6 3.1 shard_map.302
  123.4 5.8 collective-permute-start.15
  130.5 2.5 collective-permute-start.13
  136.1 15.2 %collective-permute-start.34 = (bf16[528,128]{1,0:T(8,128)(2,1)S(1)}, bf16[528,128]{1,0:T(8,128)(2,1)S(1)}, u32[]{:S(2)}, u32[]{:S(2)}) collective-permute-start(bf16[528,128]{1,0:T(8,128)(2,1)S(1)} %pad_maximum_fusion.25), channel_id=1, source_target_pairs={{0,4},{2,6},{4,8},{6,10},{8,12},{10,14},{1,5},{3,7},{5,9},{7,11},{... | collective-permute-start | bytes 405512 | tf_op jit(solution)/shard_map/ppermute | solution.py:26
  153.8 2.7 collective-permute-done.16
  163.6 6.0 collective-permute-done.17.other_ref
  174.5 3.8 shard_map.294
  181.1 3.7 shard_map.305
  186.5 6.9 %shard_map.295 = (f32[256,1024]{1,0:T(8,128)S(1)}, f32[256,256]{1,0:T(8,128)S(1)}, f32[256,256]{1,0:T(8,128)S(1)}, f32[8,1024]{1,0:T(8,128)S(1)}) custom-call(f32[256,1408]{1,0:T(8,128)S(1)} %fusion.86.joined_ref, f32[8,1280]{1,0:T(8,128)S(1)} %collective-permute-done.11.before_ref, f32[8,1280]{1,0:T(8,128)S(1)} %slice.549.conv_ref, ...), custom_call_target="tpu_custom_call" | custom-call | flops 7480000000 | bytes 4444160 | tf_op jit(solution)/shard_map/pallas_call | solution.py:467
  194.8 6.7 %shard_map.306 = (f32[256,1024]{1,0:T(8,128)S(1)}, f32[256,256]{1,0:T(8,128)S(1)}, f32[256,256]{1,0:T(8,128)S(1)}, f32[8,1024]{1,0:T(8,128)S(1)}) custom-call(f32[256,1408]{1,0:T(8,128)S(1)} %fusion.90.joined_ref, f32[8,1280]{1,0:T(8,128)S(1)} %collective-permute-done.32.before_ref, f32[8,1280]{1,0:T(8,128)S(1)} %slice.549.conv_ref, ...), custom_call_target="tpu_custom_call" | custom-call | flops 7480000000 | bytes 4444160 | tf_op jit(solution)/shard_map/pallas_call | solution.py:467
  213.5 4.1 collective-permute-done.41
  219.3 4.1 shard_map.296
  224.8 4.5 collective-permute-done.23.after_ref
  229.3 2.0 shard_map.297
  232.9 4.1 shard_map.307
  238.5 4.8 collective-permute-done.44.after_ref
  243.3 2.0 shard_map.308
  246.9 3.8 shard_map.310
  250.8 2.1 collective-permute-start.46
  255.3 3.8 shard_map.314
  259.2 2.1 collective-permute-start.52
  261.3 6.9 %shard_map.311 = (f32[256,1024]{1,0:T(8,128)S(1)}, f32[256,256]{1,0:T(8,128)S(1)}, f32[256,256]{1,0:T(8,128)S(1)}, f32[8,1024]{1,0:T(8,128)S(1)}) custom-call(f32[256,1408]{1,0:T(8,128)S(1)} %fusion.84.joined_ref, f32[8,1280]{1,0:T(8,128)S(1)} %collective-permute-done.2.before_ref, f32[8,1280]{1,0:T(8,128)S(1)} %slice.531.conv_ref, ...), custom_call_target="tpu_custom_call" | custom-call | flops 7480000000 | bytes 4444160 | tf_op jit(solution)/shard_map/pallas_call | solution.py:467
  269.7 6.7 %shard_map.315 = (f32[256,1024]{1,0:T(8,128)S(1)}, f32[256,256]{1,0:T(8,128)S(1)}, f32[256,256]{1,0:T(8,128)S(1)}, f32[8,1024]{1,0:T(8,128)S(1)}) custom-call(f32[256,1408]{1,0:T(8,128)S(1)} %fusion.88.joined_ref, f32[8,1280]{1,0:T(8,128)S(1)} %collective-permute-done.25.before_ref, f32[8,1280]{1,0:T(8,128)S(1)} %slice.531.conv_ref, ...), custom_call_target="tpu_custom_call" | custom-call | flops 7480000000 | bytes 4444160 | tf_op jit(solution)/shard_map/pallas_call | solution.py:467
  284.3 2.4 collective-permute-done.47
  287.4 5.1 collective-permute-done.54
  293.3 4.1 shard_map.312
  298.8 4.1 shard_map.316
  304.4 2.0 shard_map.313
  309.5 2.0 shard_map.317
  313.3 7.6 %shard_map.322 = (bf16[528,3456]{1,0:T(8,128)(2,1)}, bf16[528,3456]{1,0:T(8,128)(2,1)}) custom-call(s32[1]{0:T(128)} %bitcast.section_ref, bf16[256,1024]{1,0:T(8,128)(2,1)S(1)} %get-tuple-element.148.normed_a, bf16[256,1024]{1,0:T(8,128)(2,1)S(1)} %get-tuple-element.173.normed_b, bf16[256,1024]{1,0:T(8,128)(2,1)S(1)} %get-tuple-element.321.grad_ref.grad_a, ...), custom_call_target="tpu_custom_call" | custom-call | flops 8000000000 | bytes 16777216 | tf_op jit(solution)/shard_map/pallas_call | solution.py:776
  326.5 7.7 %shard_map.320 = (bf16[528,3456]{1,0:T(8,128)(2,1)}, bf16[528,3456]{1,0:T(8,128)(2,1)}) custom-call(s32[1]{0:T(128)} %bitcast.section_ref, bf16[256,1024]{1,0:T(8,128)(2,1)S(1)} %get-tuple-element.377.normed_a, bf16[256,1024]{1,0:T(8,128)(2,1)S(1)} %get-tuple-element.376.normed_b, bf16[256,1024]{1,0:T(8,128)(2,1)S(1)} %copy-done.33, ...), custom_call_target="tpu_custom_call" | custom-call | flops 8000000000 | bytes 16777216 | tf_op jit(solution)/shard_map/pallas_call | solution.py:776
  335.3 1.9 collective-permute-start.65
  340.7 3.3 collective-permute-done.65.across_ref
  345.3 5.3 collective-permute-done.64.keys_ref
  350.6 3.0 shard_map.323
  355.6 6.0 collective-permute-done.61.keys_ref
  367.2 4.9 collective-permute-done.66
  374.6 2.5 maximum_bitcast_fusion
  377.2 237.1 %all-reduce.9.cloned.1.call-done = (bf16[528,3456]{1,0:T(8,128)(2,1)}, bf16[528,3456]{1,0:T(8,128)(2,1)}) async-done(((bf16[528,3456]{1,0:T(8,128)(2,1)}, bf16[528,3456]{1,0:T(8,128)(2,1)}), (bf16[528,3456]{1,0:T(8,128)(2,1)}, bf16[528,3456]{1,0:T(8,128)(2,1)})) %all-reduce.9.cloned.1.call-update) | async-done | bytes 7299088 | tf_op jit(solution)/shard_map/psum | solution.py:830
  614.3 4.2 broadcast_select_fusion
  623.0 2.3 collective-permute-done.68.other_ref
  625.2 2.0 copy-done
  627.3 2.0 copy-done.1
  629.3 9.6 %shard_map.324 = (f32[1024,1024]{1,0:T(8,128)}, f32[1024,256]{1,0:T(8,128)}, f32[1024,128]{1,0:T(8,128)S(1)}, f32[1024,1024]{1,0:T(8,128)}, f32[1024,1024]{1,0:T(8,128)}) custom-call(s32[1]{0:T(128)} %bitcast.section_ref, bf16[528,3456]{1,0:T(8,128)(2,1)S(1)} %copy-done, bf16[528,3456]{1,0:T(8,128)(2,1)S(1)} %copy-done.1, ...), custom_call_target="tpu_custom_call" | custom-call | tf_op jit(solution)/shard_map/pallas_call | solution.py:851
  (422 shorter events, 122.7 us)
Async XLA Ops:
  7.2 607.1 %all-reduce.9.cloned.1.call-start = ((), (), s32[]{:S(2)}) async-start(), calls=%async_computation | async-start | bytes 14598144 | tf_op jit(solution)/shard_map/psum | solution.py:830
  11.4 7.7 %collective-permute-start.1 = (bf16[1024,1408]{1,0:T(8,128)(2,1)}, bf16[1024,1408]{1,0:T(8,128)(2,1)}, u32[]{:S(2)}, u32[]{:S(2)}) collective-permute-start(bf16[1024,1408]{1,0:T(8,128)(2,1)} %fusion.1), channel_id=1, source_target_pairs={{0,16},{16,0},{1,17},{17,1},{2,18},{18,2},{3,19},{19,3},{4,20},{20... | collective-permute-start | bytes 8650760 | tf_op jit(solution)/shard_map/ppermute | solution.py:20
  12.2 6.4 collective-permute-start
  19.2 55.3 %collective-permute-start.8 = (bf16[1024,1024]{1,0:T(8,128)(2,1)S(1)}, bf16[1024,1024]{1,0:T(8,128)(2,1)S(1)}, u32[]{:S(2)}, u32[]{:S(2)}) collective-permute-start(bf16[1024,1024]{1,0:T(8,128)(2,1)S(1)} %bitcast.407), channel_id=1, source_target_pairs={{0,16},{16,0},{1,17},{17,1},{2,18},{18,2},{3,19},{19,3},{4,20},{20... | collective-permute-start | bytes 6291464 | tf_op jit(solution)/shard_map/ppermute | solution.py:20
  19.7 55.8 %collective-permute-start.9 = (bf16[1024,1024]{1,0:T(8,128)(2,1)S(1)}, bf16[1024,1024]{1,0:T(8,128)(2,1)S(1)}, u32[]{:S(2)}, u32[]{:S(2)}) collective-permute-start(bf16[1024,1024]{1,0:T(8,128)(2,1)S(1)} %bitcast.409), channel_id=1, source_target_pairs={{0,16},{16,0},{1,17},{17,1},{2,18},{18,2},{3,19},{19,3},{4,20},{20... | collective-permute-start | bytes 6291464 | tf_op jit(solution)/shard_map/ppermute | solution.py:20
  23.6 9.3 %collective-permute-start.2 = (f32[8,1280]{1,0:T(8,128)S(1)}, f32[8,1280]{1,0:T(8,128)S(1)}, u32[]{:S(2)}, u32[]{:S(2)}) collective-permute-start(f32[8,1280]{1,0:T(8,128)S(1)} %slice.530), channel_id=1, source_target_pairs={{0,2},{2,4},{4,6},{6,8},{8,10},{10,12},{12,14},{1,3},{3,5},{5,7},{... | collective-permute-start | bytes 122888 | tf_op jit(solution)/shard_map/ppermute | solution.py:26
  29.5 8.2 %collective-permute-start.25 = (f32[8,1280]{1,0:T(8,128)S(1)}, f32[8,1280]{1,0:T(8,128)S(1)}, u32[]{:S(2)}, u32[]{:S(2)}) collective-permute-start(f32[8,1280]{1,0:T(8,128)S(1)} %slice.572), channel_id=1, source_target_pairs={{0,2},{2,4},{4,6},{6,8},{8,10},{10,12},{12,14},{1,3},{3,5},{5,7},{... | collective-permute-start | bytes 122888 | tf_op jit(solution)/shard_map/ppermute | solution.py:26
  40.9 6.4 collective-permute-start.26
  41.6 20.2 %collective-permute-start.6 = (bf16[528,128]{1,0:T(8,128)(2,1)S(1)}, bf16[528,128]{1,0:T(8,128)(2,1)S(1)}, u32[]{:S(2)}, u32[]{:S(2)}) collective-permute-start(bf16[528,128]{1,0:T(8,128)(2,1)S(1)} %pad_maximum_fusion.13), channel_id=1, source_target_pairs={{0,12},{2,14},{1,13},{3,15},{16,28},{18,30},{17,29},{19,31}} | collective-permute-start | bytes 405512 | tf_op jit(solution)/shard_map/ppermute | solution.py:26
  46.0 6.1 collective-permute-start.5
  47.3 12.6 %collective-permute-start.4 = (bf16[528,128]{1,0:T(8,128)(2,1)S(1)}, bf16[528,128]{1,0:T(8,128)(2,1)S(1)}, u32[]{:S(2)}, u32[]{:S(2)}) collective-permute-start(bf16[528,128]{1,0:T(8,128)(2,1)S(1)} %pad_maximum_fusion.13), channel_id=1, source_target_pairs={{0,4},{2,6},{4,8},{6,10},{8,12},{10,14},{1,5},{3,7},{5,9},{7,11},{... | collective-permute-start | bytes 405512 | tf_op jit(solution)/shard_map/ppermute | solution.py:26
  52.2 16.5 %collective-permute-start.29 = (bf16[528,128]{1,0:T(8,128)(2,1)S(1)}, bf16[528,128]{1,0:T(8,128)(2,1)S(1)}, u32[]{:S(2)}, u32[]{:S(2)}) collective-permute-start(bf16[528,128]{1,0:T(8,128)(2,1)S(1)} %pad_maximum_fusion.21), channel_id=1, source_target_pairs={{0,12},{2,14},{1,13},{3,15},{16,28},{18,30},{17,29},{19,31}} | collective-permute-start | bytes 405512 | tf_op jit(solution)/shard_map/ppermute | solution.py:26
  59.9 6.7 %collective-permute-start.28 = (bf16[528,128]{1,0:T(8,128)(2,1)S(1)}, bf16[528,128]{1,0:T(8,128)(2,1)S(1)}, u32[]{:S(2)}, u32[]{:S(2)}) collective-permute-start(bf16[528,128]{1,0:T(8,128)(2,1)S(1)} %pad_maximum_fusion.21), channel_id=1, source_target_pairs={{0,8},{2,10},{4,12},{6,14},{1,9},{3,11},{5,13},{7,15},{16,24},{18,... | collective-permute-start | bytes 405512 | tf_op jit(solution)/shard_map/ppermute | solution.py:26
  61.8 6.8 %collective-permute-start.27 = (bf16[528,128]{1,0:T(8,128)(2,1)S(1)}, bf16[528,128]{1,0:T(8,128)(2,1)S(1)}, u32[]{:S(2)}, u32[]{:S(2)}) collective-permute-start(bf16[528,128]{1,0:T(8,128)(2,1)S(1)} %pad_maximum_fusion.21), channel_id=1, source_target_pairs={{0,4},{2,6},{4,8},{6,10},{8,12},{10,14},{1,5},{3,7},{5,9},{7,11},{... | collective-permute-start | bytes 405512 | tf_op jit(solution)/shard_map/ppermute | solution.py:26
  66.7 6.0 collective-permute-start.7
  78.6 16.3 %collective-permute-start.10 = (bf16[256,1152]{1,0:T(8,128)(2,1)S(1)}, bf16[256,1152]{1,0:T(8,128)(2,1)S(1)}, u32[]{:S(2)}, u32[]{:S(2)}) collective-permute-start(bf16[256,1152]{1,0:T(8,128)(2,1)S(1)} %get-tuple-element.147.part_ref), channel_id=1, source_target_pairs={{0,1},{1,0},{2,3},{3,2},{4,5},{5,4},{6,7},{7,6},{8,9},{9,8},{10,11... | collective-permute-start | bytes 1769480 | tf_op jit(solution)/shard_map/ppermute | solution.py:20
  83.7 21.8 %collective-permute-start.31 = (bf16[256,1152]{1,0:T(8,128)(2,1)S(1)}, bf16[256,1152]{1,0:T(8,128)(2,1)S(1)}, u32[]{:S(2)}, u32[]{:S(2)}) collective-permute-start(bf16[256,1152]{1,0:T(8,128)(2,1)S(1)} %get-tuple-element.172.part_ref), channel_id=1, source_target_pairs={{0,1},{1,0},{2,3},{3,2},{4,5},{5,4},{6,7},{7,6},{8,9},{9,8},{10,11... | collective-permute-start | bytes 1769480 | tf_op jit(solution)/shard_map/ppermute | solution.py:20
  96.4 14.8 %collective-permute-start.11 = (f32[8,1280]{1,0:T(8,128)S(1)}, f32[8,1280]{1,0:T(8,128)S(1)}, u32[]{:S(2)}, u32[]{:S(2)}) collective-permute-start(f32[8,1280]{1,0:T(8,128)S(1)} %slice.548), channel_id=1, source_target_pairs={{0,2},{2,4},{4,6},{6,8},{8,10},{10,12},{12,14},{1,3},{3,5},{5,7},{... | collective-permute-start | bytes 122888 | tf_op jit(solution)/shard_map/ppermute | solution.py:26
  108.7 10.9 %collective-permute-start.32 = (f32[8,1280]{1,0:T(8,128)S(1)}, f32[8,1280]{1,0:T(8,128)S(1)}, u32[]{:S(2)}, u32[]{:S(2)}) collective-permute-start(f32[8,1280]{1,0:T(8,128)S(1)} %slice.586), channel_id=1, source_target_pairs={{0,2},{2,4},{4,6},{6,8},{8,10},{10,12},{12,14},{1,3},{3,5},{5,7},{... | collective-permute-start | bytes 122888 | tf_op jit(solution)/shard_map/ppermute | solution.py:26
  114.4 8.9 %collective-permute-start.12 = (bf16[528,128]{1,0:T(8,128)(2,1)S(1)}, bf16[528,128]{1,0:T(8,128)(2,1)S(1)}, u32[]{:S(2)}, u32[]{:S(2)}) collective-permute-start(bf16[528,128]{1,0:T(8,128)(2,1)S(1)} %dynamic-slice_bitcast_fusion.6), channel_id=1, source_target_pairs={{0,2},{2,0},{4,6},{6,4},{8,10},{10,8},{12,14},{14,12},{1,3},{3,1},... | collective-permute-start | bytes 405512 | tf_op jit(solution)/shard_map/ppermute | solution.py:20
  122.7 10.3 %collective-permute-start.33 = (bf16[528,128]{1,0:T(8,128)(2,1)S(1)}, bf16[528,128]{1,0:T(8,128)(2,1)S(1)}, u32[]{:S(2)}, u32[]{:S(2)}) collective-permute-start(bf16[528,128]{1,0:T(8,128)(2,1)S(1)} %dynamic-slice_bitcast_fusion.4), channel_id=1, source_target_pairs={{0,2},{2,0},{4,6},{6,4},{8,10},{10,8},{12,14},{14,12},{1,3},{3,1},... | collective-permute-start | bytes 405512 | tf_op jit(solution)/shard_map/ppermute | solution.py:20
  123.4 28.0 %collective-permute-start.15 = (bf16[528,128]{1,0:T(8,128)(2,1)S(1)}, bf16[528,128]{1,0:T(8,128)(2,1)S(1)}, u32[]{:S(2)}, u32[]{:S(2)}) collective-permute-start(bf16[528,128]{1,0:T(8,128)(2,1)S(1)} %pad_maximum_fusion.17), channel_id=1, source_target_pairs={{0,12},{2,14},{1,13},{3,15},{16,28},{18,30},{17,29},{19,31}} | collective-permute-start | bytes 405512 | tf_op jit(solution)/shard_map/ppermute | solution.py:26
  129.2 6.9 %collective-permute-start.14 = (bf16[528,128]{1,0:T(8,128)(2,1)S(1)}, bf16[528,128]{1,0:T(8,128)(2,1)S(1)}, u32[]{:S(2)}, u32[]{:S(2)}) collective-permute-start(bf16[528,128]{1,0:T(8,128)(2,1)S(1)} %pad_maximum_fusion.17), channel_id=1, source_target_pairs={{0,8},{2,10},{4,12},{6,14},{1,9},{3,11},{5,13},{7,15},{16,24},{18,... | collective-permute-start | bytes 405512 | tf_op jit(solution)/shard_map/ppermute | solution.py:26
  130.5 20.8 %collective-permute-start.13 = (bf16[528,128]{1,0:T(8,128)(2,1)S(1)}, bf16[528,128]{1,0:T(8,128)(2,1)S(1)}, u32[]{:S(2)}, u32[]{:S(2)}) collective-permute-start(bf16[528,128]{1,0:T(8,128)(2,1)S(1)} %pad_maximum_fusion.17), channel_id=1, source_target_pairs={{0,4},{2,6},{4,8},{6,10},{8,12},{10,14},{1,5},{3,7},{5,9},{7,11},{... | collective-permute-start | bytes 405512 | tf_op jit(solution)/shard_map/ppermute | solution.py:26
  133.1 18.7 %collective-permute-start.36 = (bf16[528,128]{1,0:T(8,128)(2,1)S(1)}, bf16[528,128]{1,0:T(8,128)(2,1)S(1)}, u32[]{:S(2)}, u32[]{:S(2)}) collective-permute-start(bf16[528,128]{1,0:T(8,128)(2,1)S(1)} %pad_maximum_fusion.25), channel_id=1, source_target_pairs={{0,12},{2,14},{1,13},{3,15},{16,28},{18,30},{17,29},{19,31}} | collective-permute-start | bytes 405512 | tf_op jit(solution)/shard_map/ppermute | solution.py:26
  134.5 17.4 %collective-permute-start.35 = (bf16[528,128]{1,0:T(8,128)(2,1)S(1)}, bf16[528,128]{1,0:T(8,128)(2,1)S(1)}, u32[]{:S(2)}, u32[]{:S(2)}) collective-permute-start(bf16[528,128]{1,0:T(8,128)(2,1)S(1)} %pad_maximum_fusion.25), channel_id=1, source_target_pairs={{0,8},{2,10},{4,12},{6,14},{1,9},{3,11},{5,13},{7,15},{16,24},{18,... | collective-permute-start | bytes 405512 | tf_op jit(solution)/shard_map/ppermute | solution.py:26
  136.1 15.8 %collective-permute-start.34 = (bf16[528,128]{1,0:T(8,128)(2,1)S(1)}, bf16[528,128]{1,0:T(8,128)(2,1)S(1)}, u32[]{:S(2)}, u32[]{:S(2)}) collective-permute-start(bf16[528,128]{1,0:T(8,128)(2,1)S(1)} %pad_maximum_fusion.25), channel_id=1, source_target_pairs={{0,4},{2,6},{4,8},{6,10},{8,12},{10,14},{1,5},{3,7},{5,9},{7,11},{... | collective-permute-start | bytes 405512 | tf_op jit(solution)/shard_map/ppermute | solution.py:26
  152.0 8.0 %collective-permute-start.37 = (bf16[512,128]{1,0:T(8,128)(2,1)S(1)}, bf16[512,128]{1,0:T(8,128)(2,1)S(1)}, u32[]{:S(2)}, u32[]{:S(2)}) collective-permute-start(bf16[512,128]{1,0:T(8,128)(2,1)S(1)} %get-tuple-element.291), channel_id=1, source_target_pairs={{0,2},{2,0},{4,6},{6,4},{8,10},{10,8},{12,14},{14,12},{1,3},{3,1},... | collective-permute-start | bytes 393224 | tf_op jit(solution)/shard_map/ppermute | solution.py:20
  158.4 11.2 %collective-permute-start.17 = (bf16[256,1152]{1,0:T(8,128)(2,1)S(1)}, bf16[256,1152]{1,0:T(8,128)(2,1)S(1)}, u32[]{:S(2)}, u32[]{:S(2)}) collective-permute-start(bf16[256,1152]{1,0:T(8,128)(2,1)S(1)} %get-tuple-element.154.part_ref), channel_id=1, source_target_pairs={{0,1},{1,0},{2,3},{3,2},{4,5},{5,4},{6,7},{7,6},{8,9},{9,8},{10,11... | collective-permute-start | bytes 1769480 | tf_op jit(solution)/shard_map/ppermute | solution.py:20
  162.8 16.1 %collective-permute-start.38 = (bf16[256,1152]{1,0:T(8,128)(2,1)S(1)}, bf16[256,1152]{1,0:T(8,128)(2,1)S(1)}, u32[]{:S(2)}, u32[]{:S(2)}) collective-permute-start(bf16[256,1152]{1,0:T(8,128)(2,1)S(1)} %get-tuple-element.179.part_ref), channel_id=1, source_target_pairs={{0,1},{1,0},{2,3},{3,2},{4,5},{5,4},{6,7},{7,6},{8,9},{9,8},{10,11... | collective-permute-start | bytes 1769480 | tf_op jit(solution)/shard_map/ppermute | solution.py:20
  178.4 15.0 %collective-permute-start.18 = (bf16[512,128]{1,0:T(8,128)(2,1)S(1)}, bf16[512,128]{1,0:T(8,128)(2,1)S(1)}, u32[]{:S(2)}, u32[]{:S(2)}) collective-permute-start(bf16[512,128]{1,0:T(8,128)(2,1)S(1)} %dynamic-slice_bitcast_fusion.11), channel_id=1, source_target_pairs={{0,2},{2,0},{4,6},{6,4},{8,10},{10,8},{12,14},{14,12},{1,3},{3,1},... | collective-permute-start | bytes 393224 | tf_op jit(solution)/shard_map/ppermute | solution.py:20
  184.9 19.3 %collective-permute-start.39 = (bf16[512,128]{1,0:T(8,128)(2,1)S(1)}, bf16[512,128]{1,0:T(8,128)(2,1)S(1)}, u32[]{:S(2)}, u32[]{:S(2)}) collective-permute-start(bf16[512,128]{1,0:T(8,128)(2,1)S(1)} %dynamic-slice_bitcast_fusion.10), channel_id=1, source_target_pairs={{0,2},{2,0},{4,6},{6,4},{8,10},{10,8},{12,14},{14,12},{1,3},{3,1},... | collective-permute-start | bytes 393224 | tf_op jit(solution)/shard_map/ppermute | solution.py:20
  193.5 14.8 %collective-permute-start.20 = (bf16[528,128]{1,0:T(8,128)(2,1)S(1)}, bf16[528,128]{1,0:T(8,128)(2,1)S(1)}, u32[]{:S(2)}, u32[]{:S(2)}) collective-permute-start(bf16[528,128]{1,0:T(8,128)(2,1)S(1)} %pad_maximum_fusion.16), channel_id=1, source_target_pairs={{8,0},{10,2},{12,4},{14,6},{9,1},{11,3},{13,5},{15,7},{24,16},{26,... | collective-permute-start | bytes 405512 | tf_op jit(solution)/shard_map/ppermute | solution.py:26
  201.5 10.4 %collective-permute-start.21 = (bf16[528,128]{1,0:T(8,128)(2,1)S(1)}, bf16[528,128]{1,0:T(8,128)(2,1)S(1)}, u32[]{:S(2)}, u32[]{:S(2)}) collective-permute-start(bf16[528,128]{1,0:T(8,128)(2,1)S(1)} %pad_maximum_fusion.16), channel_id=1, source_target_pairs={{12,0},{14,2},{13,1},{15,3},{28,16},{30,18},{29,17},{31,19}} | collective-permute-start | bytes 405512 | tf_op jit(solution)/shard_map/ppermute | solution.py:26
  202.8 7.4 %collective-permute-start.19 = (bf16[528,128]{1,0:T(8,128)(2,1)S(1)}, bf16[528,128]{1,0:T(8,128)(2,1)S(1)}, u32[]{:S(2)}, u32[]{:S(2)}) collective-permute-start(bf16[528,128]{1,0:T(8,128)(2,1)S(1)} %pad_maximum_fusion.16), channel_id=1, source_target_pairs={{4,0},{6,2},{8,4},{10,6},{12,8},{14,10},{5,1},{7,3},{9,5},{11,7},{... | collective-permute-start | bytes 405512 | tf_op jit(solution)/shard_map/ppermute | solution.py:26
  204.2 13.4 %collective-permute-start.42 = (bf16[528,128]{1,0:T(8,128)(2,1)S(1)}, bf16[528,128]{1,0:T(8,128)(2,1)S(1)}, u32[]{:S(2)}, u32[]{:S(2)}) collective-permute-start(bf16[528,128]{1,0:T(8,128)(2,1)S(1)} %pad_maximum_fusion.24), channel_id=1, source_target_pairs={{12,0},{14,2},{13,1},{15,3},{28,16},{30,18},{29,17},{31,19}} | collective-permute-start | bytes 405512 | tf_op jit(solution)/shard_map/ppermute | solution.py:26
  205.5 12.1 %collective-permute-start.41 = (bf16[528,128]{1,0:T(8,128)(2,1)S(1)}, bf16[528,128]{1,0:T(8,128)(2,1)S(1)}, u32[]{:S(2)}, u32[]{:S(2)}) collective-permute-start(bf16[528,128]{1,0:T(8,128)(2,1)S(1)} %pad_maximum_fusion.24), channel_id=1, source_target_pairs={{8,0},{10,2},{12,4},{14,6},{9,1},{11,3},{13,5},{15,7},{24,16},{26,... | collective-permute-start | bytes 405512 | tf_op jit(solution)/shard_map/ppermute | solution.py:26
  208.4 9.2 %collective-permute-start.40 = (bf16[528,128]{1,0:T(8,128)(2,1)S(1)}, bf16[528,128]{1,0:T(8,128)(2,1)S(1)}, u32[]{:S(2)}, u32[]{:S(2)}) collective-permute-start(bf16[528,128]{1,0:T(8,128)(2,1)S(1)} %pad_maximum_fusion.24), channel_id=1, source_target_pairs={{4,0},{6,2},{8,4},{10,6},{12,8},{14,10},{5,1},{7,3},{9,5},{11,7},{... | collective-permute-start | bytes 405512 | tf_op jit(solution)/shard_map/ppermute | solution.py:26
  212.1 7.1 %collective-permute-start.22 = (bf16[512,128]{1,0:T(8,128)(2,1)S(1)}, bf16[512,128]{1,0:T(8,128)(2,1)S(1)}, u32[]{:S(2)}, u32[]{:S(2)}) collective-permute-start(bf16[512,128]{1,0:T(8,128)(2,1)S(1)} %get-tuple-element.297), channel_id=1, source_target_pairs={{0,2},{2,0},{4,6},{6,4},{8,10},{10,8},{12,14},{14,12},{1,3},{3,1},... | collective-permute-start | bytes 393224 | tf_op jit(solution)/shard_map/ppermute | solution.py:20
  217.8 6.9 %collective-permute-start.43 = (bf16[512,128]{1,0:T(8,128)(2,1)S(1)}, bf16[512,128]{1,0:T(8,128)(2,1)S(1)}, u32[]{:S(2)}, u32[]{:S(2)}) collective-permute-start(bf16[512,128]{1,0:T(8,128)(2,1)S(1)} %get-tuple-element.288), channel_id=1, source_target_pairs={{0,2},{2,0},{4,6},{6,4},{8,10},{10,8},{12,14},{14,12},{1,3},{3,1},... | collective-permute-start | bytes 393224 | tf_op jit(solution)/shard_map/ppermute | solution.py:20
  231.3 14.7 %collective-permute-start.24 = (bf16[256,1024]{1,0:T(8,128)(2,1)S(1)}, bf16[256,1024]{1,0:T(8,128)(2,1)S(1)}, u32[]{:S(2)}, u32[]{:S(2)}) collective-permute-start(bf16[256,1024]{1,0:T(8,128)(2,1)S(1)} %get-tuple-element.166.part_ref), channel_id=1, source_target_pairs={{0,1},{1,0},{2,3},{3,2},{4,5},{5,4},{6,7},{7,6},{8,9},{9,8},{10,11... | collective-permute-start | bytes 1572872 | tf_op jit(solution)/shard_map/ppermute | solution.py:20
  237.0 6.3 collective-permute-start.44
  245.4 9.2 %collective-permute-start.45 = (bf16[256,1024]{1,0:T(8,128)(2,1)S(1)}, bf16[256,1024]{1,0:T(8,128)(2,1)S(1)}, u32[]{:S(2)}, u32[]{:S(2)}) collective-permute-start(bf16[256,1024]{1,0:T(8,128)(2,1)S(1)} %get-tuple-element.191.part_ref), channel_id=1, source_target_pairs={{0,1},{1,0},{2,3},{3,2},{4,5},{5,4},{6,7},{7,6},{8,9},{9,8},{10,11... | collective-permute-start | bytes 1572872 | tf_op jit(solution)/shard_map/ppermute | solution.py:20
  250.8 17.5 %collective-permute-start.46 = (bf16[512,128]{1,0:T(8,128)(2,1)S(1)}, bf16[512,128]{1,0:T(8,128)(2,1)S(1)}, u32[]{:S(2)}, u32[]{:S(2)}) collective-permute-start(bf16[512,128]{1,0:T(8,128)(2,1)S(1)} %dynamic-slice_bitcast_fusion.9), channel_id=1, source_target_pairs={{0,2},{2,0},{4,6},{6,4},{8,10},{10,8},{12,14},{14,12},{1,3},{3,1},... | collective-permute-start | bytes 393224 | tf_op jit(solution)/shard_map/ppermute | solution.py:20
  259.2 19.8 %collective-permute-start.52 = (bf16[512,128]{1,0:T(8,128)(2,1)S(1)}, bf16[512,128]{1,0:T(8,128)(2,1)S(1)}, u32[]{:S(2)}, u32[]{:S(2)}) collective-permute-start(bf16[512,128]{1,0:T(8,128)(2,1)S(1)} %dynamic-slice_bitcast_fusion.8), channel_id=1, source_target_pairs={{0,2},{2,0},{4,6},{6,4},{8,10},{10,8},{12,14},{14,12},{1,3},{3,1},... | collective-permute-start | bytes 393224 | tf_op jit(solution)/shard_map/ppermute | solution.py:20
  268.4 14.2 %collective-permute-start.48 = (bf16[528,128]{1,0:T(8,128)(2,1)S(1)}, bf16[528,128]{1,0:T(8,128)(2,1)S(1)}, u32[]{:S(2)}, u32[]{:S(2)}) collective-permute-start(bf16[528,128]{1,0:T(8,128)(2,1)S(1)} %pad_maximum_fusion.12), channel_id=1, source_target_pairs={{8,0},{10,2},{12,4},{14,6},{9,1},{11,3},{13,5},{15,7},{24,16},{26,... | collective-permute-start | bytes 405512 | tf_op jit(solution)/shard_map/ppermute | solution.py:26
  276.4 10.3 %collective-permute-start.49 = (bf16[528,128]{1,0:T(8,128)(2,1)S(1)}, bf16[528,128]{1,0:T(8,128)(2,1)S(1)}, u32[]{:S(2)}, u32[]{:S(2)}) collective-permute-start(bf16[528,128]{1,0:T(8,128)(2,1)S(1)} %pad_maximum_fusion.12), channel_id=1, source_target_pairs={{12,0},{14,2},{13,1},{15,3},{28,16},{30,18},{29,17},{31,19}} | collective-permute-start | bytes 405512 | tf_op jit(solution)/shard_map/ppermute | solution.py:26
  277.7 9.0 %collective-permute-start.47 = (bf16[528,128]{1,0:T(8,128)(2,1)S(1)}, bf16[528,128]{1,0:T(8,128)(2,1)S(1)}, u32[]{:S(2)}, u32[]{:S(2)}) collective-permute-start(bf16[528,128]{1,0:T(8,128)(2,1)S(1)} %pad_maximum_fusion.12), channel_id=1, source_target_pairs={{4,0},{6,2},{8,4},{10,6},{12,8},{14,10},{5,1},{7,3},{9,5},{11,7},{... | collective-permute-start | bytes 405512 | tf_op jit(solution)/shard_map/ppermute | solution.py:26
  279.1 13.4 %collective-permute-start.55 = (bf16[528,128]{1,0:T(8,128)(2,1)S(1)}, bf16[528,128]{1,0:T(8,128)(2,1)S(1)}, u32[]{:S(2)}, u32[]{:S(2)}) collective-permute-start(bf16[528,128]{1,0:T(8,128)(2,1)S(1)} %pad_maximum_fusion.20), channel_id=1, source_target_pairs={{12,0},{14,2},{13,1},{15,3},{28,16},{30,18},{29,17},{31,19}} | collective-permute-start | bytes 405512 | tf_op jit(solution)/shard_map/ppermute | solution.py:26
  280.4 12.1 %collective-permute-start.54 = (bf16[528,128]{1,0:T(8,128)(2,1)S(1)}, bf16[528,128]{1,0:T(8,128)(2,1)S(1)}, u32[]{:S(2)}, u32[]{:S(2)}) collective-permute-start(bf16[528,128]{1,0:T(8,128)(2,1)S(1)} %pad_maximum_fusion.20), channel_id=1, source_target_pairs={{8,0},{10,2},{12,4},{14,6},{9,1},{11,3},{13,5},{15,7},{24,16},{26,... | collective-permute-start | bytes 405512 | tf_op jit(solution)/shard_map/ppermute | solution.py:26
  282.6 9.9 %collective-permute-start.53 = (bf16[528,128]{1,0:T(8,128)(2,1)S(1)}, bf16[528,128]{1,0:T(8,128)(2,1)S(1)}, u32[]{:S(2)}, u32[]{:S(2)}) collective-permute-start(bf16[528,128]{1,0:T(8,128)(2,1)S(1)} %pad_maximum_fusion.20), channel_id=1, source_target_pairs={{4,0},{6,2},{8,4},{10,6},{12,8},{14,10},{5,1},{7,3},{9,5},{11,7},{... | collective-permute-start | bytes 405512 | tf_op jit(solution)/shard_map/ppermute | solution.py:26
  286.9 6.4 collective-permute-start.50
  297.4 7.0 %collective-permute-start.51 = (f32[8,1280]{1,0:T(8,128)S(1)}, f32[8,1280]{1,0:T(8,128)S(1)}, u32[]{:S(2)}, u32[]{:S(2)}) collective-permute-start(f32[8,1280]{1,0:T(8,128)S(1)} %slice.503), channel_id=1, source_target_pairs={{2,0},{4,2},{6,4},{8,6},{10,8},{12,10},{14,12},{3,1},{5,3},{7,5},{... | collective-permute-start | bytes 122888 | tf_op jit(solution)/shard_map/ppermute | solution.py:26
  302.9 6.5 %collective-permute-start.57 = (f32[8,1280]{1,0:T(8,128)S(1)}, f32[8,1280]{1,0:T(8,128)S(1)}, u32[]{:S(2)}, u32[]{:S(2)}) collective-permute-start(f32[8,1280]{1,0:T(8,128)S(1)} %slice.511), channel_id=1, source_target_pairs={{2,0},{4,2},{6,4},{8,6},{10,8},{12,10},{14,12},{3,1},{5,3},{7,5},{... | collective-permute-start | bytes 122888 | tf_op jit(solution)/shard_map/ppermute | solution.py:26
  306.4 14.5 %collective-permute-start.58 = (bf16[256,1024]{1,0:T(8,128)(2,1)S(1)}, bf16[256,1024]{1,0:T(8,128)(2,1)S(1)}, u32[]{:S(2)}, u32[]{:S(2)}) collective-permute-start(bf16[256,1024]{1,0:T(8,128)(2,1)S(1)} %get-tuple-element.227.part_ref), channel_id=1, source_target_pairs={{0,1},{1,0},{2,3},{3,2},{4,5},{5,4},{6,7},{7,6},{8,9},{9,8},{10,11... | collective-permute-start | bytes 1572872 | tf_op jit(solution)/shard_map/ppermute | solution.py:20
  311.5 12.6 %collective-permute-start.59 = (bf16[256,1024]{1,0:T(8,128)(2,1)S(1)}, bf16[256,1024]{1,0:T(8,128)(2,1)S(1)}, u32[]{:S(2)}, u32[]{:S(2)}) collective-permute-start(bf16[256,1024]{1,0:T(8,128)(2,1)S(1)} %get-tuple-element.229.part_ref), channel_id=1, source_target_pairs={{0,1},{1,0},{2,3},{3,2},{4,5},{5,4},{6,7},{7,6},{8,9},{9,8},{10,11... | collective-permute-start | bytes 1572872 | tf_op jit(solution)/shard_map/ppermute | solution.py:20
  320.9 29.7 %collective-permute-start.63 = (bf16[528,3456]{1,0:T(8,128)(2,1)}, bf16[528,3456]{1,0:T(8,128)(2,1)}, u32[]{:S(2)}, u32[]{:S(2)}) collective-permute-start(bf16[528,3456]{1,0:T(8,128)(2,1)} %get-tuple-element.248), channel_id=1, source_target_pairs={{0,16},{16,0},{1,17},{17,1},{2,18},{18,2},{3,19},{19,3},{4,20},{20... | collective-permute-start | bytes 10948616 | tf_op jit(solution)/shard_map/ppermute | solution.py:20
  334.3 27.4 %collective-permute-start.60 = (bf16[528,3456]{1,0:T(8,128)(2,1)}, bf16[528,3456]{1,0:T(8,128)(2,1)S(1)}, u32[]{:S(2)}, u32[]{:S(2)}) collective-permute-start(bf16[528,3456]{1,0:T(8,128)(2,1)} %get-tuple-element.232), channel_id=1, source_target_pairs={{0,16},{16,0},{1,17},{17,1},{2,18},{18,2},{3,19},{19,3},{4,20},{20... | collective-permute-start | bytes 10948616 | tf_op jit(solution)/shard_map/ppermute | solution.py:20
  335.3 8.7 %collective-permute-start.65 = (bf16[528,256]{1,0:T(8,128)(2,1)S(1)}, bf16[528,256]{1,0:T(8,128)(2,1)S(1)}, u32[]{:S(2)}, u32[]{:S(2)}) collective-permute-start(bf16[528,256]{1,0:T(8,128)(2,1)S(1)} %slice.516), channel_id=1, source_target_pairs={{0,17},{1,16},{16,1},{17,0},{2,19},{3,18},{18,3},{19,2},{4,21},{5,... | collective-permute-start | bytes 811016 | tf_op jit(solution)/shard_map/ppermute | solution.py:793
  337.2 13.3 %collective-permute-start.64 = (bf16[528,256]{1,0:T(8,128)(2,1)S(1)}, bf16[528,256]{1,0:T(8,128)(2,1)S(1)}, u32[]{:S(2)}, u32[]{:S(2)}) collective-permute-start(bf16[528,256]{1,0:T(8,128)(2,1)S(1)} %slice.515), channel_id=1, source_target_pairs={{0,1},{1,0},{2,3},{3,2},{4,5},{5,4},{6,7},{7,6},{8,9},{9,8},{10,11... | collective-permute-start | bytes 811016 | tf_op jit(solution)/shard_map/ppermute | solution.py:20
  339.6 16.1 %collective-permute-start.62 = (bf16[528,256]{1,0:T(8,128)(2,1)S(1)}, bf16[528,256]{1,0:T(8,128)(2,1)S(1)}, u32[]{:S(2)}, u32[]{:S(2)}) collective-permute-start(bf16[528,256]{1,0:T(8,128)(2,1)S(1)} %slice.514), channel_id=1, source_target_pairs={{0,17},{1,16},{16,1},{17,0},{2,19},{3,18},{18,3},{19,2},{4,21},{5,... | collective-permute-start | bytes 811016 | tf_op jit(solution)/shard_map/ppermute | solution.py:793
  344.0 17.6 %collective-permute-start.61 = (bf16[528,256]{1,0:T(8,128)(2,1)S(1)}, bf16[528,256]{1,0:T(8,128)(2,1)S(1)}, u32[]{:S(2)}, u32[]{:S(2)}) collective-permute-start(bf16[528,256]{1,0:T(8,128)(2,1)S(1)} %slice.513), channel_id=1, source_target_pairs={{0,1},{1,0},{2,3},{3,2},{4,5},{5,4},{6,7},{7,6},{8,9},{9,8},{10,11... | collective-permute-start | bytes 811016 | tf_op jit(solution)/shard_map/ppermute | solution.py:20
  366.3 7.5 %collective-permute-start.67 = (f32[2,256,1024]{2,1,0:T(8,128)S(1)}, f32[2,256,1024]{2,1,0:T(8,128)S(1)}, u32[]{:S(2)}, u32[]{:S(2)}) collective-permute-start(f32[2,256,1024]{2,1,0:T(8,128)S(1)} %fusion.2), channel_id=1, source_target_pairs={{0,16},{16,0},{1,17},{17,1},{2,18},{18,2},{3,19},{19,3},{4,20},{20... | collective-permute-start | bytes 6291464 | tf_op jit(solution)/shard_map/ppermute | solution.py:20
  618.5 6.7 %collective-permute-start.68 = (bf16[528,3456]{1,0:T(8,128)(2,1)}, bf16[528,3456]{1,0:T(8,128)(2,1)}, u32[]{:S(2)}, u32[]{:S(2)}) collective-permute-start(bf16[528,3456]{1,0:T(8,128)(2,1)} %broadcast_select_fusion), channel_id=1, source_target_pairs={{0,16},{16,0},{1,17},{17,1},{2,18},{18,2},{3,19},{19,3},{4,20},{20... | collective-permute-start | bytes 10948616 | tf_op jit(solution)/shard_map/ppermute | solution.py:20
  (93 other events, 1018.2 us)
Sparse Core Ops, SparseCore 0:
  364.6 249.5 all-reduce.8

commit v3 on v2

--- a/solution.py
+++ b/solution.py
@@ -392,26 +392,8 @@
 
 
 def product_kernel(
-    section_ref, normed_a, normed_b, grad_a, grad_b, joined_a, joined_b, gate_a, gate_b, mixed_a, mixed_b,
-    conv_a, conv_b, head_a, head_b, mix_a, mix_b, skip_a, skip_b, gain_a, gain_b, sent_ref, own_ref,
-):
-    pl.when(pl.program_id(0) == 0)(
-        lambda: fill_products(
-            normed_a, normed_b, grad_a, grad_b, joined_a, joined_b, gate_a, gate_b, mixed_a, mixed_b,
-            conv_a, conv_b, head_a, head_b, mix_a, mix_b, skip_a, skip_b, gain_a, gain_b, sent_ref,
-        )
-    )
-    pl.when(pl.program_id(0) == 1)(
-        lambda: fill_products(
-            normed_a, normed_b, grad_a, grad_b, joined_a, joined_b, gate_a, gate_b, mixed_a, mixed_b,
-            conv_a, conv_b, head_a, head_b, mix_a, mix_b, skip_a, skip_b, gain_a, gain_b, own_ref,
-        )
-    )
-
-
-def fill_products(
-    normed_a, normed_b, grad_a, grad_b, joined_a, joined_b, gate_a, gate_b, mixed_a, mixed_b,
-    conv_a, conv_b, head_a, head_b, mix_a, mix_b, skip_a, skip_b, gain_a, gain_b, out_ref,
+    half_ref, normed_a, normed_b, grad_a, grad_b, joined_a, joined_b, gate_a, gate_b, mixed_a, mixed_b,
+    conv_a, conv_b, head_a, head_b, mix_a, mix_b, skip_a, skip_b, out_ref,
 ):
     rows = normed_a.shape[1]
     wide_in, inner = joined_a.shape[1], gate_a.shape[1]
@@ -431,34 +413,32 @@
     mixes = mix_a[0:1, :] + mix_b[0:1, :]
     skips = skip_a[0:1, :] + skip_b[0:1, :]
     out_ref[last, gate_at:out_at] = pad(jnp.where(place == 0, mixes, jnp.where(place == 1, skips, 0.0)))
-    gains = jnp.zeros((8, inner), F32)
-    for piece in range(gain_a.shape[1] // inner):
-        lanes = slice(piece * inner, (piece + 1) * inner)
-        gains = jnp.where(place == piece, gain_a[0:1, lanes] + gain_b[0:1, lanes], gains)
-    out_ref[last, out_at : out_at + inner] = pad(gains)
-
-
-def add_kernel(inner, channels, own_ref, other_ref, keys_ref, across_ref, out_ref):
+    out_ref[last, out_at : out_at + inner] = jnp.zeros((16, inner), BF16)
+
+
+def add_kernel(inner, channels, own_ref, other_ref, keys_ref, across_ref, gains_ref, out_ref, rest_ref):
     step = 48
+    half, cut = own_ref.shape[0] - 16, out_ref.shape[1]
     for at in range(0, own_ref.shape[0], step):
         rows = slice(at, at + step)
         total = wide(own_ref[rows, :]) + wide(other_ref[rows, :])
-        out_ref[rows, :] = low(total)
+        out_ref[rows, :] = low(total[:, :cut])
+        rest_ref[rows, :] = low(total[:, cut:])
         keys = wide(keys_ref[rows, :]) + wide(across_ref[rows, :])
         out_ref[rows, inner:channels] = low(total[:, inner:channels] + keys)
-
-
-def unpack_kernel(inner, keys, section_ref, early_ref, late_ref, other_ref, x_ref, keys_ref, step_ref, gate_ref, out_ref):
-    section = section_ref[0]
-    mine = pl.program_id(0) == section
-    own = jnp.where(section == 0, early_ref[...], late_ref[...])
-    value = wide(jnp.where(mine, own, other_ref[...]))
+    rest_ref[half : half + 16, :] = low(gains_ref[...])
+
+
+def unpack_kernel(inner, keys, section_ref, early_ref, early_rest_ref, late_ref, late_rest_ref, *refs):
+    x_ref, keys_ref, step_ref, gate_ref, out_ref = refs[-5:]
+    value = wide(jnp.where(section_ref[0] == 0, early_ref[...], late_ref[...]))
     wide_in = inner + keys + LANES
     x_ref[...] = value[:, :inner]
     keys_ref[...] = value[:, inner : inner + keys]
     step_ref[...] = value[:, inner + keys : wide_in]
     gate_ref[...] = value[:, wide_in : wide_in + inner]
-    out_ref[...] = value[:, wide_in + inner :].T
+    rest = jnp.where(section_ref[0] == 0, early_rest_ref[...], late_rest_ref[...])
+    out_ref[...] = wide(rest).T
 
 
 def call(kernel, outs, scratch, micros, *args):
@@ -494,6 +474,24 @@
 
 def read_fade(rows, per):
     return wide(rows[:per]) + wide(rows[8 : 8 + per])
+
+
+def tree_sum(part):
+    me = lax.axis_index("seq")
+    bit = 1
+    while bit < lax.axis_size("seq"):
+        half = part.shape[1] // 2
+        upper = (me & bit) != 0
+        left, right = part[:, :half], part[:, half:]
+        sent = jnp.where(upper, left, right)
+        part = low(wide(jnp.where(upper, right, left)) + wide(exchange(sent, "seq", bit)))
+        bit *= 2
+    while bit > 1:
+        bit //= 2
+        upper = (me & bit) != 0
+        other = exchange(part, "seq", bit)
+        part = jnp.concatenate([jnp.where(upper, other, part), jnp.where(upper, part, other)], 1)
+    return part
 
 
 def scan_states(message, per, fades, reverse):
@@ -540,7 +538,7 @@
     return jnp.concatenate([jnp.where(even, kept, back), jnp.where(even, back, kept)], 0), fades
 
 
-def layer_forward(entries, normed, weights, next_gain):
+def layer_forward(entries, normed, rims, weights, next_gain):
     count = len(entries)
     inner = weights["w_z"].shape[1]
     channels = weights["conv"].shape[1]
@@ -549,7 +547,11 @@
     length = entries[0].shape[0]
     heads = 2 * inner // LANES
     joined = [matmul(one, weights["w_in"]) for one in normed]
-    before = [shifted(one[length - HALO :, :channels], "seq", 1) for one in joined]
+    if rims is None:
+        before = [shifted(one[length - HALO :, :channels], "seq", 1) for one in joined]
+    else:
+        rim = matmul(rims, weights["w_in"])
+        before = [rim[i * HALO : (i + 1) * HALO, :channels] for i in range(count)]
     gate = [matmul(one, weights["w_z"]) for one in normed]
     locals_ = [
         call(
@@ -660,7 +662,7 @@
                 ((length, length), F32),
                 ((length, inner), F32),
             ],
-            6.8,
+            1.0,
             one["joined"], one["before"], weights["conv"], weights["head"], gate[0], one["start"],
         )
         for gate, one in zip(gates, kept)
@@ -712,9 +714,9 @@
     pairs = (
         [one["normed"] for one in kept], lows, [one[0] for one in inputs], [one[1] for one in gates],
         [one[2] for one in gates], [one[2] for one in states], [one[3] for one in states],
-        [one[4] for one in gates], [one[3] for one in mixes], [one[2] for one in results],
+        [one[4] for one in gates], [one[3] for one in mixes],
     )
-    return results, reduced(pairs, inner, channels)
+    return results, reduced(pairs, [one[2] for one in results], inner, channels)
 
 
 NAMES = (
@@ -740,11 +742,12 @@
     return dict(w_in=w_in, w_z=mine["w_z"], w_out=mine["w_out"], small=jnp.concatenate([rows, vectors, mix, gain], 1))
 
 
-def both_layers(mine):
+def both_layers(mine, hidden_in):
     first = lax.axis_index("section") == 0
     inner = mine["w_z"].shape[1]
     channels = inner + mine["w_bc"].shape[1]
     own = packed(mine)
+    own["w_in"], hidden_in = lax.optimization_barrier((own["w_in"], hidden_in))
     other = {name: exchange(own[name], "section", 1) for name in ("small", "w_in")}
     own["w_z"], own["w_out"], other["w_in"] = lax.optimization_barrier(
         (own["w_z"], own["w_out"], other["w_in"])
@@ -760,32 +763,38 @@
         chosen["gain"] = small[:, channels + LANES + inner :]
         return chosen
 
-    return layer(first), layer(~first)
-
-
-def reduced(pairs, inner, channels):
+    return layer(first), layer(~first), hidden_in
+
+
+def reduced(pairs, gains, inner, channels):
     section = lax.axis_index("section")
     length, features = pairs[0][0].shape
     half = features // 2
     width = channels + LANES + 2 * inner
     whole = lambda array: pl.BlockSpec(array.shape, lambda i, side: (0, 0))
-    split = pl.BlockSpec((length, half), lambda i, side: (0, (1 - side[0]) * (1 - i) + side[0] * i))
+    split = pl.BlockSpec((length, half), lambda i, side: (0, side[0]))
     flat = [array for pair in pairs for array in pair]
-    given = pl.BlockSpec((half + 16, width), lambda i, side: (0, 0))
-    shape = jax.ShapeDtypeStruct((half + 16, width), BF16)
-    sent, own = pl.pallas_call(
-        product_kernel,
-        grid_spec=pltpu.PrefetchScalarGridSpec(
-            num_scalar_prefetch=1,
-            grid=(2,),
-            in_specs=[split] * 4 + [whole(array) for array in flat[4:]],
-            out_specs=[given, given],
-        ),
-        out_shape=[shape, shape],
-        compiler_params=pltpu.CompilerParams(vmem_limit_bytes=2 * VMEM),
-        cost_estimate=pl.CostEstimate(flops=8 * 10**9, bytes_accessed=1 << 24, transcendentals=0),
-    )(jnp.full((1,), section, jnp.int32), *flat)
+
+    def products(which):
+        return pl.pallas_call(
+            product_kernel,
+            grid_spec=pltpu.PrefetchScalarGridSpec(
+                num_scalar_prefetch=1,
+                grid=(1,),
+                in_specs=[split] * 4 + [whole(array) for array in flat[4:]],
+                out_specs=pl.BlockSpec((half + 16, width), lambda i, side: (0, 0)),
+            ),
+            out_shape=jax.ShapeDtypeStruct((half + 16, width), BF16),
+            compiler_params=pltpu.CompilerParams(vmem_limit_bytes=2 * VMEM),
+            cost_estimate=pl.CostEstimate(flops=4 * 10**9, bytes_accessed=1 << 23, transcendentals=0),
+        )(jnp.full((1,), which, jnp.int32), *flat)
+
+    sent = products(1 - section)
+    gain_sum = gains[0] + gains[1]
+    gain_sum = gain_sum + exchange(gain_sum, "section", 1)
+    rows = jnp.pad(gain_sum[0].reshape(-1, inner), ((0, 16 - features // inner), (0, 0)))
     other = exchange(sent, "section", 1)
+    own = products(section)
     heads = lax.axis_size("head")
     if heads == 2:
         keys = exchange(own[:, inner:channels], "head", 1)
@@ -796,13 +805,14 @@
         keys = low(head_sum(mine) - mine)
         across = jnp.zeros_like(keys)
     return call(
-        functools.partial(add_kernel, inner, channels), [(own.shape, BF16)], [], 4.0, own, other, keys, across
-    )[0]
+        functools.partial(add_kernel, inner, channels), [((half + 16, width - inner), BF16), ((half + 16, inner), BF16)],
+        [], 3.0, own, other, keys, across, rows,
+    )
 
 
 def shards(hidden_in, order, cotangent, *params):
     mine = {name: param[0] for name, param in zip(NAMES, params)}
-    layers = both_layers(mine)
+    *layers, hidden_in = both_layers(mine, hidden_in)
     sections = lax.axis_size("section")
     section = lax.axis_index("section")
     first = section == 0
@@ -814,10 +824,12 @@
     entries = [pick(hidden_in, order[base + index]) for index in range(count)]
     gains = [weights["gain"] for weights in layers]
     normed = [normalized(wide(entry), gains[0][0:1]) for entry in entries]
+    rims = jnp.concatenate([entry[entry.shape[0] - HALO :] for entry in entries], 0)
+    rims = normalized(wide(shifted(rims, "seq", 1)), gains[0][0:1])
     outputs = []
     kept = []
     for index, weights in enumerate(layers):
-        entries, normed, one = layer_forward(entries, normed, weights, gains[1])
+        entries, normed, one = layer_forward(entries, normed, rims if index == 0 else None, weights, gains[1])
         outputs.append(jnp.stack(entries))
         kept.append(one)
     incoming = [pick(cotangent, base + index) for index in range(count)]
@@ -825,9 +837,25 @@
     late_grads = jnp.stack([one[0] for one in results])
     wides = [one[0] for one in results]
     lows = [one[1] for one in results]
-    results, early = layer_backward(lows, lows, kept[0], layers[0])
-    early_grads = jnp.stack([one[0] for one in results])
-    early, late = lax.psum((early, late), "seq")
+    late = lax.psum(late, "seq")
+
+    def first_layer():
+        results, early = layer_backward(lows, lows, kept[0], layers[0])
+        return jnp.stack([one[0] for one in results]), *early
+
+    def empty():
+        return jnp.zeros(late_grads.shape, F32), *(jnp.zeros(one.shape, BF16) for one in late)
+
+    early_grads, early, early_rest = lax.cond(order[0] >= 0, first_layer, empty)
+    early, late = lax.optimization_barrier((early, late))
+    early = lax.psum(early, "seq")
+    late, late_rest = late
+    if lax.axis_size("seq") * LANES <= inner:
+        early_rest = lax.cond(
+            order[0] >= 0, tree_sum, lambda part: jnp.zeros(part.shape, BF16), early_rest
+        )
+    else:
+        early_rest = lax.psum(early_rest, "seq")
 
     def swapped(early, late):
         return exchange(jnp.where(first, late, early), "section", 1)
@@ -839,34 +867,60 @@
     activations = to_owner(outputs[0], outputs[1])[None]
     grads = to_owner(early_grads, late_grads)[None]
     half = features // 2
+    keys_width = channels - inner
+    late_other = lax.ppermute(late, "section", [(0, 1)])
+    late_rest_other = lax.ppermute(late_rest, "section", [(0, 1)])
+    early_rest_other = lax.ppermute(early_rest, "section", [(1, 0)])
+    early, late_other, late_rest_other, early_rest_other, activations, grads = lax.optimization_barrier(
+        (early, late_other, late_rest_other, early_rest_other, activations, grads)
+    )
+    early_other = lax.ppermute(early, "section", [(1, 0)])
     keys_width = channels - inner
     early, late, activations, grads = lax.optimization_barrier((early, late, activations, grads))
     other = swapped(early, late)
     block = 128
     steps = half // block
     width = early.shape[1]
-    taken = pl.BlockSpec((block, width), lambda side, i: (i, 0))
-    given = lambda lanes: pl.BlockSpec((block, lanes), lambda side, i: (side * steps + i, 0))
+    place = lambda side, flag, i: (side[0] ^ flag) * steps + i
     shape = lambda rows, lanes: jax.ShapeDtypeStruct((rows, lanes), F32)
-    w_x, w_bc, w_dt, w_z, w_out = pl.pallas_call(
-        functools.partial(unpack_kernel, inner, keys_width),
-        grid=(2, steps),
-        out_shape=[
-            shape(features, inner), shape(features, keys_width), shape(features, LANES),
-            shape(features, inner), shape(inner, features),
-        ],
-        in_specs=[pl.BlockSpec(memory_space=pltpu.SMEM), taken, taken, taken],
-        out_specs=[
-            given(inner), given(keys_width), given(LANES), given(inner),
-            pl.BlockSpec((inner, block), lambda side, i: (0, side * steps + i)),
-        ],
-        compiler_params=pltpu.CompilerParams(vmem_limit_bytes=VMEM),
-    )(jnp.full((1,), section, jnp.int32), early, late, other)
+
+    def unpack(flag, parts, filled):
+        given = lambda lanes: pl.BlockSpec((block, lanes), lambda i, side: (place(side, flag, i), 0))
+        return pl.pallas_call(
+            functools.partial(unpack_kernel, inner, keys_width),
+            grid_spec=pltpu.PrefetchScalarGridSpec(
+                num_scalar_prefetch=1,
+                grid=(steps,),
+                in_specs=[
+                    pl.BlockSpec((block, width), lambda i, side: ((1 - side[0]) * i, 0)),
+                    pl.BlockSpec((block, inner), lambda i, side: ((1 - side[0]) * i, 0)),
+                    pl.BlockSpec((block, width), lambda i, side: (side[0] * i, 0)),
+                    pl.BlockSpec((block, inner), lambda i, side: (side[0] * i, 0)),
+                ]
+                + [pl.BlockSpec(memory_space=pl.ANY)] * len(filled),
+                out_specs=[
+                    given(inner), given(keys_width), given(LANES), given(inner),
+                    pl.BlockSpec((inner, block), lambda i, side: (0, place(side, flag, i))),
+                ],
+            ),
+            out_shape=[
+                shape(features, inner), shape(features, keys_width), shape(features, LANES),
+                shape(features, inner), shape(inner, features),
+            ],
+            input_output_aliases={5 + i: i for i in range(len(filled))},
+            compiler_params=pltpu.CompilerParams(vmem_limit_bytes=VMEM),
+            cost_estimate=pl.CostEstimate(flops=5 * 10**9, bytes_accessed=1 << 23, transcendentals=0),
+        )(jnp.full((1,), section, jnp.int32), *parts, *filled)
+
+    filled = unpack(0, (early, early_rest, late, late_rest), [])
+    others = (early_other, early_rest_other, late_other, late_rest_other)
+    w_x, w_bc, w_dt, w_z, w_out = unpack(1, others, filled)
     rows = wide(jnp.where(first, early[half : half + 8], late[half : half + 8]))
+    rest = wide(jnp.where(first, early_rest[half : half + 8], late_rest[half : half + 8]))
     heads = mine["w_dt"].shape[1]
     wide_in = channels + LANES
     mixes = rows[:, wide_in : wide_in + inner]
-    gains = rows[: features // inner, wide_in + inner :].reshape(features)
+    gains = rest[: features // inner].reshape(features)
     results = dict(
         norm_gain=gains,
         w_z=w_z,

time: 657 us -> 617 us (0.939)
  waiting for transfers between devices: 326 us -> 235 us
  other arithmetic: 21.9 us -> 41.6 us
  local copies, waits for them, and re-layouts: 28 us -> 38.8 us
  Pallas kernels: 123 us -> 132 us
  starting transfers between devices: 120 us -> 129 us
    psum x1 -> x2, waiting for transfers between devices: 237 us -> 36 us  [the longest x1 19.5 us: shards(): late = lax.psum(late, 'seq')]
    ppermute x35 -> x42, waiting for transfers between devices: 52.5 us -> 153 us  [exchange(): return lax.ppermute(block, axis, route)]
    cond x0 -> x126, local copies, waits for them, and re-layouts: none -> 12.1 us
    pallas_call x34, Pallas kernels: 98.3 us -> 108 us  [call(): pl.pallas_call(kernel, out_shape=shapes, in_specs=[pl.BlockSpec(memory_sp...]
    ppermute x0 -> x4, starting transfers between devices: none -> 8.96 us  [the longest x1 3.24 us: shards(): late_other = lax.ppermute(late, 'section', [(0, 1)])]
    ppermute x32 -> x31, waiting for transfers between devices: 33.1 us -> 41.4 us  [shifted(): return lax.ppermute(block, axis, route)]
    unnamed x176 -> x92, local copies, waits for them, and re-layouts: 19.6 us -> 13.7 us
    ppermute x35 -> x42, starting transfers between devices: 34.7 us -> 38.1 us  [exchange(): return lax.ppermute(block, axis, route)]
  transfers between devices with their start and end apart: 70 -> 81, of which waited for: 30 -> 35; matrix products, arithmetic and copies ran while one was open for 5% -> 9% of each run, Pallas kernels for 17% -> 19%
where the time goes in v3:
time: 617 us; the launch traced here: 606 us
  waiting for transfers between devices  235 us (38%)
  Pallas kernels  132 us (21%)
  starting transfers between devices  129 us (21%)
  other arithmetic  41.6 us (7%)
  local copies, waits for them, and re-layouts  38.8 us (6%)
  between operations  20.3 us (3%)
  matrix products  7.3 us (1%)
    ppermute x42, waiting for transfers between devices, exchange(): return lax.ppermute(block, axis, route)  153 us
    pallas_call x34, Pallas kernels, call(): pl.pallas_call(kernel, out_shape=shapes, in_specs=[pl.BlockSpec(memory_sp...  108 us
    ppermute x31, starting transfers between devices, shifted(): return lax.ppermute(block, axis, route)  79.7 us
    ppermute x31, waiting for transfers between devices, shifted(): return lax.ppermute(block, axis, route)  41.4 us
    ppermute x42, starting transfers between devices, exchange(): return lax.ppermute(block, axis, route)  38.1 us
    psum x1, waiting for transfers between devices, shards(): late = lax.psum(late, 'seq')  19.5 us
    psum x1, waiting for transfers between devices, shards(): early = lax.psum(early, 'seq')  16.5 us
    pallas_call x4, Pallas kernels, products(): pl.pallas_call(product_kernel, grid_spec=pltpu.PrefetchScalarGridSpec(num...  15.8 us
  transfers between devices with their start and end apart: 81, of which 35 were waited for; matrix products, arithmetic and copies ran while one was open for 9% of the time, Pallas kernels for 19%

profile of v3, /device:TPU:0, one launch (start us, length us, event | category | flops | bytes accessed | tf_op | source)
XLA Modules:
  0.0 605.7 jit_solution(14872580031974266771)
XLA Ops:
  8.3 3.0 fusion.14
  17.4 4.8 collective-permute-start.26
  26.1 3.6 broadcast_select_fusion.17
  32.4 3.2 shard_map.299
  37.2 3.1 shard_map.288
  41.5 4.6 collective-permute-start.51
  46.3 3.9 collective-permute-start.30
  51.5 9.8 %collective-permute-start.50 = (bf16[528,128]{1,0:T(8,128)(2,1)S(1)}, bf16[528,128]{1,0:T(8,128)(2,1)S(1)}, u32[]{:S(2)}, u32[]{:S(2)}) collective-permute-start(bf16[528,128]{1,0:T(8,128)(2,1)S(1)} %pad_maximum_fusion.26), channel_id=1, source_target_pairs={{0,4},{2,6},{4,8},{6,10},{8,12},{10,14},{1,5},{3,7},{5,9},{7,11},{... | collective-permute-start | bytes 405512 | tf_op jit(solution)/shard_map/ppermute | solution.py:26
  61.3 2.9 collective-permute-done.50
  64.3 7.2 %collective-permute-start.52 = (bf16[528,128]{1,0:T(8,128)(2,1)S(1)}, bf16[528,128]{1,0:T(8,128)(2,1)S(1)}, u32[]{:S(2)}, u32[]{:S(2)}) collective-permute-start(bf16[528,128]{1,0:T(8,128)(2,1)S(1)} %pad_maximum_fusion.26), channel_id=1, source_target_pairs={{0,12},{2,14},{1,13},{3,15},{16,28},{18,30},{17,29},{19,31}} | collective-permute-start | bytes 405512 | tf_op jit(solution)/shard_map/ppermute | solution.py:26
  90.0 2.6 shard_map.289
  93.1 10.9 %collective-permute-done.54.other_ref = bf16[256,1152]{1,0:T(8,128)(2,1)S(1)} collective-permute-done((bf16[256,1152]{1,0:T(8,128)(2,1)S(1)}, bf16[256,1152]{1,0:T(8,128)(2,1)S(1)}, u32[]{:S(2)}, u32[]{:S(2)}) %collective-permute-start.54) | collective-permute-done | bytes 589856 | tf_op jit(solution)/shard_map/ppermute | solution.py:20
  107.0 5.8 collective-permute-done.34.other_ref
  117.4 5.2 collective-permute-start.35
  122.7 3.2 shard_map.302
  126.6 3.2 shard_map.291
  131.3 7.2 %collective-permute-start.59 = (bf16[528,128]{1,0:T(8,128)(2,1)S(1)}, bf16[528,128]{1,0:T(8,128)(2,1)S(1)}, u32[]{:S(2)}, u32[]{:S(2)}) collective-permute-start(bf16[528,128]{1,0:T(8,128)(2,1)S(1)} %pad_maximum_fusion.22), channel_id=1, source_target_pairs={{0,12},{2,14},{1,13},{3,15},{16,28},{18,30},{17,29},{19,31}} | collective-permute-start | bytes 405512 | tf_op jit(solution)/shard_map/ppermute | solution.py:26
  145.0 4.3 collective-permute-start.37
  149.6 3.9 collective-permute-start.60
  162.3 5.9 collective-permute-done.61.other_ref
  170.3 3.8 shard_map.305
  178.4 3.8 shard_map.294
  182.6 6.8 %shard_map.306 = (f32[256,1024]{1,0:T(8,128)S(1)}, f32[256,256]{1,0:T(8,128)S(1)}, f32[256,256]{1,0:T(8,128)S(1)}, f32[8,1024]{1,0:T(8,128)S(1)}) custom-call(f32[256,1408]{1,0:T(8,128)S(1)} %fusion.99.joined_ref, f32[8,1280]{1,0:T(8,128)S(1)} %collective-permute-done.55.before_ref, f32[8,1280]{1,0:T(8,128)S(1)} %slice.617.conv_ref, ...), custom_call_target="tpu_custom_call" | custom-call | flops 1100000000 | bytes 4444160 | tf_op jit(solution)/shard_map/pallas_call | solution.py:447
  190.9 6.7 %shard_map.295 = (f32[256,1024]{1,0:T(8,128)S(1)}, f32[256,256]{1,0:T(8,128)S(1)}, f32[256,256]{1,0:T(8,128)S(1)}, f32[8,1024]{1,0:T(8,128)S(1)}) custom-call(f32[256,1408]{1,0:T(8,128)S(1)} %fusion.95.joined_ref, f32[8,1280]{1,0:T(8,128)S(1)} %collective-permute-done.35.before_ref, f32[8,1280]{1,0:T(8,128)S(1)} %slice.617.conv_ref, ...), custom_call_target="tpu_custom_call" | custom-call | flops 1100000000 | bytes 4444160 | tf_op jit(solution)/shard_map/pallas_call | solution.py:447
  206.4 10.1 %collective-permute-done.63 = bf16[528,128]{1,0:T(8,128)(2,1)S(1)} collective-permute-done((bf16[528,128]{1,0:T(8,128)(2,1)S(1)}, bf16[528,128]{1,0:T(8,128)(2,1)S(1)}, u32[]{:S(2)}, u32[]{:S(2)}) %collective-permute-start.63) | collective-permute-done | bytes 135200 | tf_op jit(solution)/shard_map/ppermute | solution.py:26
  217.0 5.6 collective-permute-done.44
  223.2 4.1 shard_map.307
  228.7 4.1 shard_map.296
  236.5 2.8 collective-permute-done.47.after_ref
  241.3 3.9 shard_map.311
  248.3 3.9 shard_map.310.own_ref
  254.9 5.1 collective-permute-done.68.other_ref
  261.4 9.8 %collective-permute-done.48.other_ref = bf16[256,1024]{1,0:T(8,128)(2,1)S(1)} collective-permute-done((bf16[256,1024]{1,0:T(8,128)(2,1)S(1)}, bf16[256,1024]{1,0:T(8,128)(2,1)S(1)}, u32[]{:S(2)}, u32[]{:S(2)}) %collective-permute-start.48) | collective-permute-done | bytes 524320 | tf_op jit(solution)/shard_map/ppermute | solution.py:20
  276.2 6.2 %collective-permute-done.70.keys_ref = bf16[528,256]{1,0:T(8,128)(2,1)S(1)} collective-permute-done((bf16[528,256]{1,0:T(8,128)(2,1)S(1)}, bf16[528,256]{1,0:T(8,128)(2,1)S(1)}, u32[]{:S(2)}, u32[]{:S(2)}) %collective-permute-start.70) | collective-permute-done | bytes 270368 | tf_op jit(solution)/shard_map/ppermute | solution.py:20
  286.6 136.3 %conditional.2 = (f32[2,256,1024]{2,1,0:T(8,128)}, bf16[528,2432]{1,0:T(8,128)(2,1)}, bf16[528,1024]{1,0:T(8,128)(2,1)}) conditional(s32[]{:T(128)} %bitcast.16, () %tuple.35, (bf16[256,1024]{1,0:T(8,128)(2,1)}, bf16[1024,1024]{1,0:T(8,128)(2,1)}, f32[256,1024]{1,0:T(8,128)}, f32[256,1024]{1,0:T(8,128)}, f32[256,128]{1,0:T(8,128)}, ...), branch_computations={%region_3.4_spmd, %region_4.5_spmd} | conditional | flops 38145560576 | bytes 287767296 | solution.py:849
  287.5 6.6 %branch_1_fun.18 = (f32[256,1024]{1,0:T(8,128)S(1)}, bf16[256,1024]{1,0:T(8,128)(2,1)S(1)}, bf16[256,1024]{1,0:T(8,128)(2,1)S(1)}, bf16[2,512,128]{2,1,0:T(8,128)(2,1)S(1)}, f32[8,1024]{1,0:T(8,128)S(1)}) custom-call(bf16[256,1024]{1,0:T(8,128)(2,1)} %get-tuple-element.107.grad_ref.grad_b, bf16[1024,1024]{1,0:T(8,128)(2,1)} %get-tuple-element.80.w_ref, ...), custom_call_target="tpu_custom_call" | custom-call | flops 4289999872 | bytes 8519680 | tf_op jit(solution)/shard_map/cond/branch_1_fun/pallas_call | solution.py:447
  297.3 2.9 collective-permute-start.13
  300.3 3.7 branch_1_fun.13
  309.9 8.2 %branch_1_fun.14 = (f32[256,1024]{1,0:T(8,128)S(1)}, f32[256,256]{1,0:T(8,128)S(1)}, f32[256,256]{1,0:T(8,128)S(1)}, f32[8,1024]{1,0:T(8,128)S(1)}) custom-call(f32[256,1408]{1,0:T(8,128)} %get-tuple-element.75.joined_ref, f32[8,1280]{1,0:T(8,128)} %get-tuple-element.76.before_ref, f32[8,1280]{1,0:T(8,128)} %get-tuple-element.77.conv_ref, ...), custom_call_target="tpu_custom_call" | custom-call | flops 1100000000 | bytes 4444160 | tf_op jit(solution)/shard_map/cond/branch_1_fun/pallas_call | solution.py:447
  322.7 7.3 %branch_1_fun.19 = (f32[256,1024]{1,0:T(8,128)S(1)}, f32[256,256]{1,0:T(8,128)S(1)}, f32[256,256]{1,0:T(8,128)S(1)}, f32[8,1024]{1,0:T(8,128)S(1)}) custom-call(f32[256,1408]{1,0:T(8,128)S(1)} %copy-done.60, f32[8,1280]{1,0:T(8,128)S(1)} %copy-done.75, f32[8,1280]{1,0:T(8,128)S(1)} %copy-done.80, f32[8,128]{1,0:T(8,128)} %copy-done.88, ...), custom_call_target="tpu_custom_call" | custom-call | flops 1100000000 | bytes 4444160 | tf_op jit(solution)/shard_map/cond/branch_1_fun/pallas_call | solution.py:447
  342.6 7.8 %collective-permute-done.7 = bf16[528,128]{1,0:T(8,128)(2,1)S(1)} collective-permute-done((bf16[528,128]{1,0:T(8,128)(2,1)}, bf16[528,128]{1,0:T(8,128)(2,1)S(1)}, u32[]{:S(2)}, u32[]{:S(2)}) %collective-permute-start.7) | collective-permute-done | bytes 135200 | tf_op jit(solution)/shard_map/cond/branch_1_fun/ppermute | solution.py:26
  352.7 4.0 collective-permute-done.15
  358.6 4.1 branch_1_fun.15
  366.5 4.1 branch_1_fun.20
  378.7 3.9 branch_1_fun.24
  386.5 3.9 branch_1_fun.23.own_ref
  393.1 4.4 collective-permute-done.12.other_ref
  398.9 9.7 %collective-permute-done.19.other_ref = bf16[256,1024]{1,0:T(8,128)(2,1)S(1)} collective-permute-done((bf16[256,1024]{1,0:T(8,128)(2,1)S(1)}, bf16[256,1024]{1,0:T(8,128)(2,1)S(1)}, u32[]{:S(2)}, u32[]{:S(2)}) %collective-permute-start.19) | collective-permute-done | bytes 524320 | tf_op jit(solution)/shard_map/cond/branch_1_fun/ppermute | solution.py:20
  413.7 6.2 %collective-permute-done.21.keys_ref = bf16[528,256]{1,0:T(8,128)(2,1)S(1)} collective-permute-done((bf16[528,256]{1,0:T(8,128)(2,1)S(1)}, bf16[528,256]{1,0:T(8,128)(2,1)S(1)}, u32[]{:S(2)}, u32[]{:S(2)}) %collective-permute-start.21) | collective-permute-done | bytes 270368 | tf_op jit(solution)/shard_map/cond/branch_1_fun/ppermute | solution.py:20
  419.9 2.9 branch_1_fun.25
  426.1 19.5 %all-reduce.14.cloned.1.call-done = (bf16[528,2432]{1,0:T(8,128)(2,1)}, bf16[528,1024]{1,0:T(8,128)(2,1)}) async-done(((bf16[528,2432]{1,0:T(8,128)(2,1)}, bf16[528,1024]{1,0:T(8,128)(2,1)}), (bf16[528,2432]{1,0:T(8,128)(2,1)}, bf16[528,1024]{1,0:T(8,128)(2,1)})) %all-reduce.14.cloned.1.call-update) | async-done | bytes 3649552 | tf_op jit(solution)/shard_map/psum | solution.py:840
  445.6 3.2 collective-permute-start.73
  451.2 94.1 %conditional.3 = (bf16[528,1024]{1,0:T(8,128)(2,1)}, bf16[8,1024]{1,0:T(8,128)(2,1)S(1)}) conditional(s32[]{:T(128)} %bitcast.16, () %tuple.40, bf16[528,1024]{1,0:T(8,128)(2,1)} %get-tuple-element.352), branch_computations={%region_8.9_spmd, %region_9.10_spmd} | conditional | flops 9224201 | bytes 25022852 | solution.py:854
  454.7 22.6 %collective-permute-done = bf16[528,512]{1,0:T(8,128)(2,1)} collective-permute-done((bf16[528,512]{1,0:T(8,128)(2,1)}, bf16[528,512]{1,0:T(8,128)(2,1)}, u32[]{:S(2)}, u32[]{:S(2)}) %collective-permute-start) | collective-permute-done | bytes 540704 | tf_op jit(solution)/shard_map/cond/branch_1_fun/ppermute | solution.py:20
  480.7 14.6 %collective-permute-done.1 = bf16[528,256]{1,0:T(8,128)(2,1)S(1)} collective-permute-done((bf16[528,256]{1,0:T(8,128)(2,1)}, bf16[528,256]{1,0:T(8,128)(2,1)S(1)}, u32[]{:S(2)}, u32[]{:S(2)}) %collective-permute-start.1) | collective-permute-done | bytes 270368 | tf_op jit(solution)/shard_map/cond/branch_1_fun/ppermute | solution.py:20
  498.5 9.7 %collective-permute-done.2 = bf16[528,128]{1,0:T(8,128)(2,1)S(1)} collective-permute-done((bf16[528,128]{1,0:T(8,128)(2,1)S(1)}, bf16[528,128]{1,0:T(8,128)(2,1)S(1)}, u32[]{:S(2)}, u32[]{:S(2)}) %collective-permute-start.2) | collective-permute-done | bytes 135200 | tf_op jit(solution)/shard_map/cond/branch_1_fun/ppermute | solution.py:20
  508.4 11.8 %collective-permute-done.3 = bf16[528,128]{1,0:T(8,128)(2,1)S(1)} collective-permute-done((bf16[528,128]{1,0:T(8,128)(2,1)S(1)}, bf16[528,128]{1,0:T(8,128)(2,1)S(1)}, u32[]{:S(2)}, u32[]{:S(2)}) %collective-permute-start.3) | collective-permute-done | bytes 135200 | tf_op jit(solution)/shard_map/cond/branch_1_fun/ppermute | solution.py:20
  520.4 10.9 %collective-permute-done.4 = bf16[528,256]{1,0:T(8,128)(2,1)S(1)} collective-permute-done((bf16[528,256]{1,0:T(8,128)(2,1)S(1)}, bf16[528,256]{1,0:T(8,128)(2,1)S(1)}, u32[]{:S(2)}, u32[]{:S(2)}) %collective-permute-start.4) | collective-permute-done | bytes 270368 | tf_op jit(solution)/shard_map/cond/branch_1_fun/ppermute | solution.py:20
  531.5 12.4 %collective-permute-done.5 = bf16[528,512]{1,0:T(8,128)(2,1)S(1)} collective-permute-done((bf16[528,512]{1,0:T(8,128)(2,1)S(1)}, bf16[528,512]{1,0:T(8,128)(2,1)S(1)}, u32[]{:S(2)}, u32[]{:S(2)}) %collective-permute-start.5) | collective-permute-done | bytes 540704 | tf_op jit(solution)/shard_map/cond/branch_1_fun/ppermute | solution.py:20
  546.6 3.2 collective-permute-start.74
  553.0 2.9 broadcast_select_fusion.24
  560.6 16.5 %all-reduce.12.cloned.1.call-done.early_ref = bf16[528,2432]{1,0:T(8,128)(2,1)} async-done(((bf16[528,2432]{1,0:T(8,128)(2,1)}), bf16[528,2432]{1,0:T(8,128)(2,1)}) %all-reduce.12.cloned.1.call-update) | async-done | bytes 2568208 | tf_op jit(solution)/shard_map/psum | solution.py:851
  588.8 4.7 shard_map.313
  593.6 4.2 shard_map.314
  (520 shorter events, 192.8 us)
Async XLA Ops:
  7.2 438.4 %all-reduce.14.cloned.1.call-start = ((), (), s32[]{:S(2)}) async-start(), calls=%async_computation.1 | async-start | bytes 7299072 | tf_op jit(solution)/shard_map/psum | solution.py:840
  11.3 14.8 %collective-permute-start.25 = (bf16[1024,1408]{1,0:T(8,128)(2,1)}, bf16[1024,1408]{1,0:T(8,128)(2,1)}, u32[]{:S(2)}, u32[]{:S(2)}) collective-permute-start(bf16[1024,1408]{1,0:T(8,128)(2,1)} %fusion.14), channel_id=1, source_target_pairs={{0,16},{16,0},{1,17},{17,1},{2,18},{18,2},{3,19},{19,3},{4,20},{20... | collective-permute-start | bytes 8650760 | tf_op jit(solution)/shard_map/ppermute | solution.py:20
  12.1 13.5 %collective-permute-start.24 = (f32[8,3456]{1,0:T(8,128)S(1)}, f32[8,3456]{1,0:T(8,128)S(1)}, u32[]{:S(2)}, u32[]{:S(2)}) collective-permute-start(f32[8,3456]{1,0:T(8,128)S(1)} %select_maximum_fusion), channel_id=1, source_target_pairs={{0,16},{16,0},{1,17},{17,1},{2,18},{18,2},{3,19},{19,3},{4,20},{20... | collective-permute-start | bytes 331784 | tf_op jit(solution)/shard_map/ppermute | solution.py:20
  17.4 8.0 %collective-permute-start.26 = (bf16[16,1024]{1,0:T(8,128)(2,1)S(1)}, bf16[16,1024]{1,0:T(8,128)(2,1)S(1)}, u32[]{:S(2)}, u32[]{:S(2)}) collective-permute-start(bf16[16,1024]{1,0:T(8,128)(2,1)S(1)} %pad_maximum_fusion.27), channel_id=1, source_target_pairs={{0,2},{2,4},{4,6},{6,8},{8,10},{10,12},{12,14},{1,3},{3,5},{5,7},{... | collective-permute-start | bytes 98312 | tf_op jit(solution)/shard_map/ppermute | solution.py:26
  40.9 42.2 %collective-permute-start.32 = (bf16[1024,1024]{1,0:T(8,128)(2,1)S(1)}, bf16[1024,1024]{1,0:T(8,128)(2,1)S(1)}, u32[]{:S(2)}, u32[]{:S(2)}) collective-permute-start(bf16[1024,1024]{1,0:T(8,128)(2,1)S(1)} %bitcast.401), channel_id=1, source_target_pairs={{0,16},{16,0},{1,17},{17,1},{2,18},{18,2},{3,19},{19,3},{4,20},{20... | collective-permute-start | bytes 6291464 | tf_op jit(solution)/shard_map/ppermute | solution.py:20
  40.9 43.2 %collective-permute-start.33 = (bf16[1024,1024]{1,0:T(8,128)(2,1)S(1)}, bf16[1024,1024]{1,0:T(8,128)(2,1)S(1)}, u32[]{:S(2)}, u32[]{:S(2)}) collective-permute-start(bf16[1024,1024]{1,0:T(8,128)(2,1)S(1)} %bitcast.403), channel_id=1, source_target_pairs={{0,16},{16,0},{1,17},{17,1},{2,18},{18,2},{3,19},{19,3},{4,20},{20... | collective-permute-start | bytes 6291464 | tf_op jit(solution)/shard_map/ppermute | solution.py:20
  41.5 10.0 %collective-permute-start.51 = (bf16[528,128]{1,0:T(8,128)(2,1)S(1)}, bf16[528,128]{1,0:T(8,128)(2,1)S(1)}, u32[]{:S(2)}, u32[]{:S(2)}) collective-permute-start(bf16[528,128]{1,0:T(8,128)(2,1)S(1)} %pad_maximum_fusion.26), channel_id=1, source_target_pairs={{0,8},{2,10},{4,12},{6,14},{1,9},{3,11},{5,13},{7,15},{16,24},{18,... | collective-permute-start | bytes 405512 | tf_op jit(solution)/shard_map/ppermute | solution.py:26
  46.3 31.6 %collective-permute-start.30 = (bf16[528,128]{1,0:T(8,128)(2,1)S(1)}, bf16[528,128]{1,0:T(8,128)(2,1)S(1)}, u32[]{:S(2)}, u32[]{:S(2)}) collective-permute-start(bf16[528,128]{1,0:T(8,128)(2,1)S(1)} %pad_maximum_fusion.25), channel_id=1, source_target_pairs={{0,12},{2,14},{1,13},{3,15},{16,28},{18,30},{17,29},{19,31}} | collective-permute-start | bytes 405512 | tf_op jit(solution)/shard_map/ppermute | solution.py:26
  50.2 25.4 %collective-permute-start.29 = (bf16[528,128]{1,0:T(8,128)(2,1)S(1)}, bf16[528,128]{1,0:T(8,128)(2,1)S(1)}, u32[]{:S(2)}, u32[]{:S(2)}) collective-permute-start(bf16[528,128]{1,0:T(8,128)(2,1)S(1)} %pad_maximum_fusion.25), channel_id=1, source_target_pairs={{0,8},{2,10},{4,12},{6,14},{1,9},{3,11},{5,13},{7,15},{16,24},{18,... | collective-permute-start | bytes 405512 | tf_op jit(solution)/shard_map/ppermute | solution.py:26
  51.5 12.7 %collective-permute-start.50 = (bf16[528,128]{1,0:T(8,128)(2,1)S(1)}, bf16[528,128]{1,0:T(8,128)(2,1)S(1)}, u32[]{:S(2)}, u32[]{:S(2)}) collective-permute-start(bf16[528,128]{1,0:T(8,128)(2,1)S(1)} %pad_maximum_fusion.26), channel_id=1, source_target_pairs={{0,4},{2,6},{4,8},{6,10},{8,12},{10,14},{1,5},{3,7},{5,9},{7,11},{... | collective-permute-start | bytes 405512 | tf_op jit(solution)/shard_map/ppermute | solution.py:26
  64.3 9.7 %collective-permute-start.52 = (bf16[528,128]{1,0:T(8,128)(2,1)S(1)}, bf16[528,128]{1,0:T(8,128)(2,1)S(1)}, u32[]{:S(2)}, u32[]{:S(2)}) collective-permute-start(bf16[528,128]{1,0:T(8,128)(2,1)S(1)} %pad_maximum_fusion.26), channel_id=1, source_target_pairs={{0,12},{2,14},{1,13},{3,15},{16,28},{18,30},{17,29},{19,31}} | collective-permute-start | bytes 405512 | tf_op jit(solution)/shard_map/ppermute | solution.py:26
  87.7 16.3 %collective-permute-start.54 = (bf16[256,1152]{1,0:T(8,128)(2,1)S(1)}, bf16[256,1152]{1,0:T(8,128)(2,1)S(1)}, u32[]{:S(2)}, u32[]{:S(2)}) collective-permute-start(bf16[256,1152]{1,0:T(8,128)(2,1)S(1)} %get-tuple-element.308.part_ref), channel_id=1, source_target_pairs={{0,1},{1,0},{2,3},{3,2},{4,5},{5,4},{6,7},{7,6},{8,9},{9,8},{10,11... | collective-permute-start | bytes 1769480 | tf_op jit(solution)/shard_map/ppermute | solution.py:20
  92.6 20.3 %collective-permute-start.34 = (bf16[256,1152]{1,0:T(8,128)(2,1)S(1)}, bf16[256,1152]{1,0:T(8,128)(2,1)S(1)}, u32[]{:S(2)}, u32[]{:S(2)}) collective-permute-start(bf16[256,1152]{1,0:T(8,128)(2,1)S(1)} %get-tuple-element.280.part_ref), channel_id=1, source_target_pairs={{0,1},{1,0},{2,3},{3,2},{4,5},{5,4},{6,7},{7,6},{8,9},{9,8},{10,11... | collective-permute-start | bytes 1769480 | tf_op jit(solution)/shard_map/ppermute | solution.py:20
  115.2 7.4 %collective-permute-start.55 = (f32[8,1280]{1,0:T(8,128)S(1)}, f32[8,1280]{1,0:T(8,128)S(1)}, u32[]{:S(2)}, u32[]{:S(2)}) collective-permute-start(f32[8,1280]{1,0:T(8,128)S(1)} %slice.654), channel_id=1, source_target_pairs={{0,2},{2,4},{4,6},{6,8},{8,10},{10,12},{12,14},{1,3},{3,5},{5,7},{... | collective-permute-start | bytes 122888 | tf_op jit(solution)/shard_map/ppermute | solution.py:26
  117.4 9.1 %collective-permute-start.35 = (f32[8,1280]{1,0:T(8,128)S(1)}, f32[8,1280]{1,0:T(8,128)S(1)}, u32[]{:S(2)}, u32[]{:S(2)}) collective-permute-start(f32[8,1280]{1,0:T(8,128)S(1)} %slice.616), channel_id=1, source_target_pairs={{0,2},{2,4},{4,6},{6,8},{8,10},{10,12},{12,14},{1,3},{3,5},{5,7},{... | collective-permute-start | bytes 122888 | tf_op jit(solution)/shard_map/ppermute | solution.py:26
  129.7 12.6 %collective-permute-start.36 = (bf16[528,128]{1,0:T(8,128)(2,1)S(1)}, bf16[528,128]{1,0:T(8,128)(2,1)S(1)}, u32[]{:S(2)}, u32[]{:S(2)}) collective-permute-start(bf16[528,128]{1,0:T(8,128)(2,1)S(1)} %dynamic-slice_bitcast_fusion.8), channel_id=1, source_target_pairs={{0,2},{2,0},{4,6},{6,4},{8,10},{10,8},{12,14},{14,12},{1,3},{3,1},... | collective-permute-start | bytes 405512 | tf_op jit(solution)/shard_map/ppermute | solution.py:20
  131.3 18.1 %collective-permute-start.59 = (bf16[528,128]{1,0:T(8,128)(2,1)S(1)}, bf16[528,128]{1,0:T(8,128)(2,1)S(1)}, u32[]{:S(2)}, u32[]{:S(2)}) collective-permute-start(bf16[528,128]{1,0:T(8,128)(2,1)S(1)} %pad_maximum_fusion.22), channel_id=1, source_target_pairs={{0,12},{2,14},{1,13},{3,15},{16,28},{18,30},{17,29},{19,31}} | collective-permute-start | bytes 405512 | tf_op jit(solution)/shard_map/ppermute | solution.py:26
  139.8 9.6 %collective-permute-start.57 = (bf16[528,128]{1,0:T(8,128)(2,1)S(1)}, bf16[528,128]{1,0:T(8,128)(2,1)S(1)}, u32[]{:S(2)}, u32[]{:S(2)}) collective-permute-start(bf16[528,128]{1,0:T(8,128)(2,1)S(1)} %pad_maximum_fusion.22), channel_id=1, source_target_pairs={{0,4},{2,6},{4,8},{6,10},{8,12},{10,14},{1,5},{3,7},{5,9},{7,11},{... | collective-permute-start | bytes 405512 | tf_op jit(solution)/shard_map/ppermute | solution.py:26
  142.4 11.1 %collective-permute-start.39 = (bf16[528,128]{1,0:T(8,128)(2,1)S(1)}, bf16[528,128]{1,0:T(8,128)(2,1)S(1)}, u32[]{:S(2)}, u32[]{:S(2)}) collective-permute-start(bf16[528,128]{1,0:T(8,128)(2,1)S(1)} %pad_maximum_fusion.18), channel_id=1, source_target_pairs={{0,12},{2,14},{1,13},{3,15},{16,28},{18,30},{17,29},{19,31}} | collective-permute-start | bytes 405512 | tf_op jit(solution)/shard_map/ppermute | solution.py:26
  143.7 9.8 %collective-permute-start.38 = (bf16[528,128]{1,0:T(8,128)(2,1)S(1)}, bf16[528,128]{1,0:T(8,128)(2,1)S(1)}, u32[]{:S(2)}, u32[]{:S(2)}) collective-permute-start(bf16[528,128]{1,0:T(8,128)(2,1)S(1)} %pad_maximum_fusion.18), channel_id=1, source_target_pairs={{0,8},{2,10},{4,12},{6,14},{1,9},{3,11},{5,13},{7,15},{16,24},{18,... | collective-permute-start | bytes 405512 | tf_op jit(solution)/shard_map/ppermute | solution.py:26
  145.0 8.5 %collective-permute-start.37 = (bf16[528,128]{1,0:T(8,128)(2,1)S(1)}, bf16[528,128]{1,0:T(8,128)(2,1)S(1)}, u32[]{:S(2)}, u32[]{:S(2)}) collective-permute-start(bf16[528,128]{1,0:T(8,128)(2,1)S(1)} %pad_maximum_fusion.18), channel_id=1, source_target_pairs={{0,4},{2,6},{4,8},{6,10},{8,12},{10,14},{1,5},{3,7},{5,9},{7,11},{... | collective-permute-start | bytes 405512 | tf_op jit(solution)/shard_map/ppermute | solution.py:26
  158.3 9.9 %collective-permute-start.61 = (bf16[256,1152]{1,0:T(8,128)(2,1)S(1)}, bf16[256,1152]{1,0:T(8,128)(2,1)S(1)}, u32[]{:S(2)}, u32[]{:S(2)}) collective-permute-start(bf16[256,1152]{1,0:T(8,128)(2,1)S(1)} %get-tuple-element.315.part_ref), channel_id=1, source_target_pairs={{0,1},{1,0},{2,3},{3,2},{4,5},{5,4},{6,7},{7,6},{8,9},{9,8},{10,11... | collective-permute-start | bytes 1769480 | tf_op jit(solution)/shard_map/ppermute | solution.py:20
  161.7 14.5 %collective-permute-start.41 = (bf16[256,1152]{1,0:T(8,128)(2,1)S(1)}, bf16[256,1152]{1,0:T(8,128)(2,1)S(1)}, u32[]{:S(2)}, u32[]{:S(2)}) collective-permute-start(bf16[256,1152]{1,0:T(8,128)(2,1)S(1)} %get-tuple-element.287.part_ref), channel_id=1, source_target_pairs={{0,1},{1,0},{2,3},{3,2},{4,5},{5,4},{6,7},{7,6},{8,9},{9,8},{10,11... | collective-permute-start | bytes 1769480 | tf_op jit(solution)/shard_map/ppermute | solution.py:20
  174.2 15.3 %collective-permute-start.62 = (bf16[512,128]{1,0:T(8,128)(2,1)S(1)}, bf16[512,128]{1,0:T(8,128)(2,1)S(1)}, u32[]{:S(2)}, u32[]{:S(2)}) collective-permute-start(bf16[512,128]{1,0:T(8,128)(2,1)S(1)} %dynamic-slice_bitcast_fusion.10), channel_id=1, source_target_pairs={{0,2},{2,0},{4,6},{6,4},{8,10},{10,8},{12,14},{14,12},{1,3},{3,1},... | collective-permute-start | bytes 393224 | tf_op jit(solution)/shard_map/ppermute | solution.py:20
  182.2 17.9 %collective-permute-start.42 = (bf16[512,128]{1,0:T(8,128)(2,1)S(1)}, bf16[512,128]{1,0:T(8,128)(2,1)S(1)}, u32[]{:S(2)}, u32[]{:S(2)}) collective-permute-start(bf16[512,128]{1,0:T(8,128)(2,1)S(1)} %dynamic-slice_bitcast_fusion.11), channel_id=1, source_target_pairs={{0,2},{2,0},{4,6},{6,4},{8,10},{10,8},{12,14},{14,12},{1,3},{3,1},... | collective-permute-start | bytes 393224 | tf_op jit(solution)/shard_map/ppermute | solution.py:20
  189.6 15.3 %collective-permute-start.64 = (bf16[528,128]{1,0:T(8,128)(2,1)S(1)}, bf16[528,128]{1,0:T(8,128)(2,1)S(1)}, u32[]{:S(2)}, u32[]{:S(2)}) collective-permute-start(bf16[528,128]{1,0:T(8,128)(2,1)S(1)} %pad_maximum_fusion.21), channel_id=1, source_target_pairs={{8,0},{10,2},{12,4},{14,6},{9,1},{11,3},{13,5},{15,7},{24,16},{26,... | collective-permute-start | bytes 405512 | tf_op jit(solution)/shard_map/ppermute | solution.py:26
  197.6 18.9 %collective-permute-start.65 = (bf16[528,128]{1,0:T(8,128)(2,1)S(1)}, bf16[528,128]{1,0:T(8,128)(2,1)S(1)}, u32[]{:S(2)}, u32[]{:S(2)}) collective-permute-start(bf16[528,128]{1,0:T(8,128)(2,1)S(1)} %pad_maximum_fusion.21), channel_id=1, source_target_pairs={{12,0},{14,2},{13,1},{15,3},{28,16},{30,18},{29,17},{31,19}} | collective-permute-start | bytes 405512 | tf_op jit(solution)/shard_map/ppermute | solution.py:26
  198.9 17.6 %collective-permute-start.63 = (bf16[528,128]{1,0:T(8,128)(2,1)S(1)}, bf16[528,128]{1,0:T(8,128)(2,1)S(1)}, u32[]{:S(2)}, u32[]{:S(2)}) collective-permute-start(bf16[528,128]{1,0:T(8,128)(2,1)S(1)} %pad_maximum_fusion.21), channel_id=1, source_target_pairs={{4,0},{6,2},{8,4},{10,6},{12,8},{14,10},{5,1},{7,3},{9,5},{11,7},{... | collective-permute-start | bytes 405512 | tf_op jit(solution)/shard_map/ppermute | solution.py:26
  200.3 22.3 %collective-permute-start.45 = (bf16[528,128]{1,0:T(8,128)(2,1)S(1)}, bf16[528,128]{1,0:T(8,128)(2,1)S(1)}, u32[]{:S(2)}, u32[]{:S(2)}) collective-permute-start(bf16[528,128]{1,0:T(8,128)(2,1)S(1)} %pad_maximum_fusion.17), channel_id=1, source_target_pairs={{12,0},{14,2},{13,1},{15,3},{28,16},{30,18},{29,17},{31,19}} | collective-permute-start | bytes 405512 | tf_op jit(solution)/shard_map/ppermute | solution.py:26
  201.6 21.0 %collective-permute-start.44 = (bf16[528,128]{1,0:T(8,128)(2,1)S(1)}, bf16[528,128]{1,0:T(8,128)(2,1)S(1)}, u32[]{:S(2)}, u32[]{:S(2)}) collective-permute-start(bf16[528,128]{1,0:T(8,128)(2,1)S(1)} %pad_maximum_fusion.17), channel_id=1, source_target_pairs={{8,0},{10,2},{12,4},{14,6},{9,1},{11,3},{13,5},{15,7},{24,16},{26,... | collective-permute-start | bytes 405512 | tf_op jit(solution)/shard_map/ppermute | solution.py:26
  204.8 17.7 %collective-permute-start.43 = (bf16[528,128]{1,0:T(8,128)(2,1)S(1)}, bf16[528,128]{1,0:T(8,128)(2,1)S(1)}, u32[]{:S(2)}, u32[]{:S(2)}) collective-permute-start(bf16[528,128]{1,0:T(8,128)(2,1)S(1)} %pad_maximum_fusion.17), channel_id=1, source_target_pairs={{4,0},{6,2},{8,4},{10,6},{12,8},{14,10},{5,1},{7,3},{9,5},{11,7},{... | collective-permute-start | bytes 405512 | tf_op jit(solution)/shard_map/ppermute | solution.py:26
  245.2 37.2 %collective-permute-start.69 = (bf16[528,3456]{1,0:T(8,128)(2,1)}, bf16[528,3456]{1,0:T(8,128)(2,1)S(1)}, u32[]{:S(2)}, u32[]{:S(2)}) collective-permute-start(bf16[528,3456]{1,0:T(8,128)(2,1)} %shard_map.311), channel_id=1, source_target_pairs={{0,16},{16,0},{1,17},{17,1},{2,18},{18,2},{3,19},{19,3},{4,20},{20... | collective-permute-start | bytes 10948616 | tf_op jit(solution)/shard_map/ppermute | solution.py:20
  245.2 14.7 %collective-permute-start.68 = (bf16[256,1024]{1,0:T(8,128)(2,1)S(1)}, bf16[256,1024]{1,0:T(8,128)(2,1)S(1)}, u32[]{:S(2)}, u32[]{:S(2)}) collective-permute-start(bf16[256,1024]{1,0:T(8,128)(2,1)S(1)} %get-tuple-element.327.part_ref), channel_id=1, source_target_pairs={{0,1},{1,0},{2,3},{3,2},{4,5},{5,4},{6,7},{7,6},{8,9},{9,8},{10,11... | collective-permute-start | bytes 1572872 | tf_op jit(solution)/shard_map/ppermute | solution.py:20
  246.8 24.4 %collective-permute-start.48 = (bf16[256,1024]{1,0:T(8,128)(2,1)S(1)}, bf16[256,1024]{1,0:T(8,128)(2,1)S(1)}, u32[]{:S(2)}, u32[]{:S(2)}) collective-permute-start(bf16[256,1024]{1,0:T(8,128)(2,1)S(1)} %get-tuple-element.299.part_ref), channel_id=1, source_target_pairs={{0,1},{1,0},{2,3},{3,2},{4,5},{5,4},{6,7},{7,6},{8,9},{9,8},{10,11... | collective-permute-start | bytes 1572872 | tf_op jit(solution)/shard_map/ppermute | solution.py:20
  253.2 23.0 %collective-permute-start.71 = (bf16[528,256]{1,0:T(8,128)(2,1)S(1)}, bf16[528,256]{1,0:T(8,128)(2,1)S(1)}, u32[]{:S(2)}, u32[]{:S(2)}) collective-permute-start(bf16[528,256]{1,0:T(8,128)(2,1)S(1)} %slice.676), channel_id=1, source_target_pairs={{0,17},{1,16},{16,1},{17,0},{2,19},{3,18},{18,3},{19,2},{4,21},{5,... | collective-permute-start | bytes 811016 | tf_op jit(solution)/shard_map/ppermute | solution.py:802
  254.4 28.1 %collective-permute-start.70 = (bf16[528,256]{1,0:T(8,128)(2,1)S(1)}, bf16[528,256]{1,0:T(8,128)(2,1)S(1)}, u32[]{:S(2)}, u32[]{:S(2)}) collective-permute-start(bf16[528,256]{1,0:T(8,128)(2,1)S(1)} %slice.675), channel_id=1, source_target_pairs={{0,1},{1,0},{2,3},{3,2},{4,5},{5,4},{6,7},{7,6},{8,9},{9,8},{10,11... | collective-permute-start | bytes 811016 | tf_op jit(solution)/shard_map/ppermute | solution.py:20
  285.9 291.3 %all-reduce.12.cloned.1.call-start = ((), (), s32[]{:S(2)}) async-start(), calls=%async_computation | async-start | bytes 5136384 | tf_op jit(solution)/shard_map/psum | solution.py:851
  297.3 38.0 %collective-permute-start.13 = (bf16[512,128]{1,0:T(8,128)(2,1)}, bf16[512,128]{1,0:T(8,128)(2,1)}, u32[]{:S(2)}, u32[]{:S(2)}) collective-permute-start(bf16[512,128]{1,0:T(8,128)(2,1)} %dynamic-slice_bitcast_fusion), channel_id=1, source_target_pairs={{0,2},{2,0},{4,6},{6,4},{8,10},{10,8},{12,14},{14,12},{1,3},{3,1},... | collective-permute-start | bytes 393224 | tf_op jit(solution)/shard_map/cond/branch_1_fun/ppermute | solution.py:20
  308.0 11.1 %collective-permute-start.6 = (bf16[512,128]{1,0:T(8,128)(2,1)}, bf16[512,128]{1,0:T(8,128)(2,1)}, u32[]{:S(2)}, u32[]{:S(2)}) collective-permute-start(bf16[512,128]{1,0:T(8,128)(2,1)} %dynamic-slice_bitcast_fusion.1), channel_id=1, source_target_pairs={{0,2},{2,0},{4,6},{6,4},{8,10},{10,8},{12,14},{14,12},{1,3},{3,1},... | collective-permute-start | bytes 393224 | tf_op jit(solution)/shard_map/cond/branch_1_fun/ppermute | solution.py:20
  320.9 19.7 %collective-permute-start.8 = (bf16[528,128]{1,0:T(8,128)(2,1)}, bf16[528,128]{1,0:T(8,128)(2,1)}, u32[]{:S(2)}, u32[]{:S(2)}) collective-permute-start(bf16[528,128]{1,0:T(8,128)(2,1)} %pad_maximum_fusion.3), channel_id=1, source_target_pairs={{8,0},{10,2},{12,4},{14,6},{9,1},{11,3},{13,5},{15,7},{24,16},{26,... | collective-permute-start | bytes 405512 | tf_op jit(solution)/shard_map/cond/branch_1_fun/ppermute | solution.py:26
  332.4 18.0 %collective-permute-start.9 = (bf16[528,128]{1,0:T(8,128)(2,1)}, bf16[528,128]{1,0:T(8,128)(2,1)S(1)}, u32[]{:S(2)}, u32[]{:S(2)}) collective-permute-start(bf16[528,128]{1,0:T(8,128)(2,1)} %pad_maximum_fusion.3), channel_id=1, source_target_pairs={{12,0},{14,2},{13,1},{15,3},{28,16},{30,18},{29,17},{31,19}} | collective-permute-start | bytes 405512 | tf_op jit(solution)/shard_map/cond/branch_1_fun/ppermute | solution.py:26
  334.0 16.4 %collective-permute-start.7 = (bf16[528,128]{1,0:T(8,128)(2,1)}, bf16[528,128]{1,0:T(8,128)(2,1)S(1)}, u32[]{:S(2)}, u32[]{:S(2)}) collective-permute-start(bf16[528,128]{1,0:T(8,128)(2,1)} %pad_maximum_fusion.3), channel_id=1, source_target_pairs={{4,0},{6,2},{8,4},{10,6},{12,8},{14,10},{5,1},{7,3},{9,5},{11,7},{... | collective-permute-start | bytes 405512 | tf_op jit(solution)/shard_map/cond/branch_1_fun/ppermute | solution.py:26
  337.0 19.7 %collective-permute-start.16 = (bf16[528,128]{1,0:T(8,128)(2,1)S(1)}, bf16[528,128]{1,0:T(8,128)(2,1)S(1)}, u32[]{:S(2)}, u32[]{:S(2)}) collective-permute-start(bf16[528,128]{1,0:T(8,128)(2,1)S(1)} %pad_maximum_fusion.4), channel_id=1, source_target_pairs={{12,0},{14,2},{13,1},{15,3},{28,16},{30,18},{29,17},{31,19}} | collective-permute-start | bytes 405512 | tf_op jit(solution)/shard_map/cond/branch_1_fun/ppermute | solution.py:26
  338.3 18.3 %collective-permute-start.15 = (bf16[528,128]{1,0:T(8,128)(2,1)S(1)}, bf16[528,128]{1,0:T(8,128)(2,1)S(1)}, u32[]{:S(2)}, u32[]{:S(2)}) collective-permute-start(bf16[528,128]{1,0:T(8,128)(2,1)S(1)} %pad_maximum_fusion.4), channel_id=1, source_target_pairs={{8,0},{10,2},{12,4},{14,6},{9,1},{11,3},{13,5},{15,7},{24,16},{26,... | collective-permute-start | bytes 405512 | tf_op jit(solution)/shard_map/cond/branch_1_fun/ppermute | solution.py:26
  340.6 16.0 %collective-permute-start.14 = (bf16[528,128]{1,0:T(8,128)(2,1)S(1)}, bf16[528,128]{1,0:T(8,128)(2,1)S(1)}, u32[]{:S(2)}, u32[]{:S(2)}) collective-permute-start(bf16[528,128]{1,0:T(8,128)(2,1)S(1)} %pad_maximum_fusion.4), channel_id=1, source_target_pairs={{4,0},{6,2},{8,4},{10,6},{12,8},{14,10},{5,1},{7,3},{9,5},{11,7},{... | collective-permute-start | bytes 405512 | tf_op jit(solution)/shard_map/cond/branch_1_fun/ppermute | solution.py:26
  357.8 8.6 %collective-permute-start.17 = (bf16[512,128]{1,0:T(8,128)(2,1)S(1)}, bf16[512,128]{1,0:T(8,128)(2,1)S(1)}, u32[]{:S(2)}, u32[]{:S(2)}) collective-permute-start(bf16[512,128]{1,0:T(8,128)(2,1)S(1)} %get-tuple-element.401), channel_id=1, source_target_pairs={{0,2},{2,0},{4,6},{6,4},{8,10},{10,8},{12,14},{14,12},{1,3},{3,1},... | collective-permute-start | bytes 393224 | tf_op jit(solution)/shard_map/cond/branch_1_fun/ppermute | solution.py:20
  362.8 9.2 %collective-permute-start.11 = (f32[8,1280]{1,0:T(8,128)S(1)}, f32[8,1280]{1,0:T(8,128)S(1)}, u32[]{:S(2)}, u32[]{:S(2)}) collective-permute-start(f32[8,1280]{1,0:T(8,128)S(1)} %slice.348), channel_id=1, source_target_pairs={{2,0},{4,2},{6,4},{8,6},{10,8},{12,10},{14,12},{3,1},{5,3},{7,5},{... | collective-permute-start | bytes 122888 | tf_op jit(solution)/shard_map/cond/branch_1_fun/ppermute | solution.py:26
  382.7 37.2 %collective-permute-start.20 = (bf16[528,3456]{1,0:T(8,128)(2,1)}, bf16[528,3456]{1,0:T(8,128)(2,1)S(1)}, u32[]{:S(2)}, u32[]{:S(2)}) collective-permute-start(bf16[528,3456]{1,0:T(8,128)(2,1)} %branch_1_fun.24), channel_id=1, source_target_pairs={{0,16},{16,0},{1,17},{17,1},{2,18},{18,2},{3,19},{19,3},{4,20},{20... | collective-permute-start | bytes 10948616 | tf_op jit(solution)/shard_map/cond/branch_1_fun/ppermute | solution.py:20
  382.7 14.7 %collective-permute-start.12 = (bf16[256,1024]{1,0:T(8,128)(2,1)S(1)}, bf16[256,1024]{1,0:T(8,128)(2,1)S(1)}, u32[]{:S(2)}, u32[]{:S(2)}) collective-permute-start(bf16[256,1024]{1,0:T(8,128)(2,1)S(1)} %get-tuple-element.101.part_ref), channel_id=1, source_target_pairs={{0,1},{1,0},{2,3},{3,2},{4,5},{5,4},{6,7},{7,6},{8,9},{9,8},{10,11... | collective-permute-start | bytes 1572872 | tf_op jit(solution)/shard_map/cond/branch_1_fun/ppermute | solution.py:20
  384.2 24.5 %collective-permute-start.19 = (bf16[256,1024]{1,0:T(8,128)(2,1)S(1)}, bf16[256,1024]{1,0:T(8,128)(2,1)S(1)}, u32[]{:S(2)}, u32[]{:S(2)}) collective-permute-start(bf16[256,1024]{1,0:T(8,128)(2,1)S(1)} %get-tuple-element.125.part_ref), channel_id=1, source_target_pairs={{0,1},{1,0},{2,3},{3,2},{4,5},{5,4},{6,7},{7,6},{8,9},{9,8},{10,11... | collective-permute-start | bytes 1572872 | tf_op jit(solution)/shard_map/cond/branch_1_fun/ppermute | solution.py:20
  391.4 22.3 %collective-permute-start.22 = (bf16[528,256]{1,0:T(8,128)(2,1)S(1)}, bf16[528,256]{1,0:T(8,128)(2,1)S(1)}, u32[]{:S(2)}, u32[]{:S(2)}) collective-permute-start(bf16[528,256]{1,0:T(8,128)(2,1)S(1)} %slice.588), channel_id=1, source_target_pairs={{0,17},{1,16},{16,1},{17,0},{2,19},{3,18},{18,3},{19,2},{4,21},{5,... | collective-permute-start | bytes 811016 | tf_op jit(solution)/shard_map/cond/branch_1_fun/ppermute | solution.py:802
  392.5 27.3 %collective-permute-start.21 = (bf16[528,256]{1,0:T(8,128)(2,1)S(1)}, bf16[528,256]{1,0:T(8,128)(2,1)S(1)}, u32[]{:S(2)}, u32[]{:S(2)}) collective-permute-start(bf16[528,256]{1,0:T(8,128)(2,1)S(1)} %slice.587), channel_id=1, source_target_pairs={{0,1},{1,0},{2,3},{3,2},{4,5},{5,4},{6,7},{7,6},{8,9},{9,8},{10,11... | collective-permute-start | bytes 811016 | tf_op jit(solution)/shard_map/cond/branch_1_fun/ppermute | solution.py:20
  424.6 128.4 %collective-permute-start.77 = (f32[2,256,1024]{2,1,0:T(8,128)}, f32[2,256,1024]{2,1,0:T(8,128)}, u32[]{:S(2)}, u32[]{:S(2)}) collective-permute-start(f32[2,256,1024]{2,1,0:T(8,128)} %fusion.15), channel_id=1, source_target_pairs={{0,16},{16,0},{1,17},{17,1},{2,18},{18,2},{3,19},{19,3},{4,20},{20... | collective-permute-start | bytes 6291464 | tf_op jit(solution)/shard_map/ppermute | solution.py:20
  445.6 131.5 %collective-permute-start.73 = (bf16[528,2432]{1,0:T(8,128)(2,1)}, bf16[528,2432]{1,0:T(8,128)(2,1)}, u32[]{:S(2)}, u32[]{:S(2)}) collective-permute-start(bf16[528,2432]{1,0:T(8,128)(2,1)} %get-tuple-element.369.late_ref), channel_id=1, source_target_pairs={{0,16},{1,17},{2,18},{3,19},{4,20},{5,21},{6,22},{7,23},{8,24},{9,... | collective-permute-start | bytes 7704584 | tf_op jit(solution)/shard_map/ppermute | solution.py:871
  451.2 98.6 %collective-permute-start.76 = (bf16[2,256,1024]{2,1,0:T(8,128)(2,1)}, bf16[2,256,1024]{2,1,0:T(8,128)(2,1)}, u32[]{:S(2)}, u32[]{:S(2)}) collective-permute-start(bf16[2,256,1024]{2,1,0:T(8,128)(2,1)} %broadcast_select_fusion.27), channel_id=1, source_target_pairs={{0,16},{16,0},{1,17},{17,1},{2,18},{18,2},{3,19},{19,3},{4,20},{20... | collective-permute-start | bytes 3145736 | tf_op jit(solution)/shard_map/ppermute | solution.py:20
  453.3 24.0 %collective-permute-start = (bf16[528,512]{1,0:T(8,128)(2,1)}, bf16[528,512]{1,0:T(8,128)(2,1)}, u32[]{:S(2)}, u32[]{:S(2)}) collective-permute-start(bf16[528,512]{1,0:T(8,128)(2,1)} %broadcast_select_fusion.10), channel_id=1, source_target_pairs={{0,2},{2,0},{4,6},{6,4},{8,10},{10,8},{12,14},{14,12},{1,3},{3,1},... | collective-permute-start | bytes 1622024 | tf_op jit(solution)/shard_map/cond/branch_1_fun/ppermute | solution.py:20
  480.5 14.8 %collective-permute-start.1 = (bf16[528,256]{1,0:T(8,128)(2,1)}, bf16[528,256]{1,0:T(8,128)(2,1)S(1)}, u32[]{:S(2)}, u32[]{:S(2)}) collective-permute-start(bf16[528,256]{1,0:T(8,128)(2,1)} %broadcast_select_fusion.13), channel_id=1, source_target_pairs={{0,4},{2,6},{4,0},{6,2},{8,12},{10,14},{12,8},{14,10},{1,5},{3,7},... | collective-permute-start | bytes 811016 | tf_op jit(solution)/shard_map/cond/branch_1_fun/ppermute | solution.py:20
  496.4 11.8 %collective-permute-start.2 = (bf16[528,128]{1,0:T(8,128)(2,1)S(1)}, bf16[528,128]{1,0:T(8,128)(2,1)S(1)}, u32[]{:S(2)}, u32[]{:S(2)}) collective-permute-start(bf16[528,128]{1,0:T(8,128)(2,1)S(1)} %broadcast_select_fusion.16), channel_id=1, source_target_pairs={{0,8},{2,10},{4,12},{6,14},{8,0},{10,2},{12,4},{14,6},{1,9},{3,11}... | collective-permute-start | bytes 405512 | tf_op jit(solution)/shard_map/cond/branch_1_fun/ppermute | solution.py:20
  508.3 11.9 %collective-permute-start.3 = (bf16[528,128]{1,0:T(8,128)(2,1)S(1)}, bf16[528,128]{1,0:T(8,128)(2,1)S(1)}, u32[]{:S(2)}, u32[]{:S(2)}) collective-permute-start(bf16[528,128]{1,0:T(8,128)(2,1)S(1)} %add_convert_fusion.2), channel_id=1, source_target_pairs={{0,8},{2,10},{4,12},{6,14},{8,0},{10,2},{12,4},{14,6},{1,9},{3,11}... | collective-permute-start | bytes 405512 | tf_op jit(solution)/shard_map/cond/branch_1_fun/ppermute | solution.py:20
  520.3 11.0 %collective-permute-start.4 = (bf16[528,256]{1,0:T(8,128)(2,1)S(1)}, bf16[528,256]{1,0:T(8,128)(2,1)S(1)}, u32[]{:S(2)}, u32[]{:S(2)}) collective-permute-start(bf16[528,256]{1,0:T(8,128)(2,1)S(1)} %pad_maximum_fusion.7), channel_id=1, source_target_pairs={{0,4},{2,6},{4,0},{6,2},{8,12},{10,14},{12,8},{14,10},{1,5},{3,7},... | collective-permute-start | bytes 811016 | tf_op jit(solution)/shard_map/cond/branch_1_fun/ppermute | solution.py:20
  531.5 12.5 %collective-permute-start.5 = (bf16[528,512]{1,0:T(8,128)(2,1)S(1)}, bf16[528,512]{1,0:T(8,128)(2,1)S(1)}, u32[]{:S(2)}, u32[]{:S(2)}) collective-permute-start(bf16[528,512]{1,0:T(8,128)(2,1)S(1)} %pad_maximum_fusion.6), channel_id=1, source_target_pairs={{0,2},{2,0},{4,6},{6,4},{8,10},{10,8},{12,14},{14,12},{1,3},{3,1},... | collective-permute-start | bytes 1622024 | tf_op jit(solution)/shard_map/cond/branch_1_fun/ppermute | solution.py:20
  545.3 13.2 %collective-permute-start.75 = (bf16[528,1024]{1,0:T(8,128)(2,1)}, bf16[528,1024]{1,0:T(8,128)(2,1)S(1)}, u32[]{:S(2)}, u32[]{:S(2)}) collective-permute-start(bf16[528,1024]{1,0:T(8,128)(2,1)} %get-tuple-element.353.early_rest_ref), channel_id=1, source_target_pairs={{16,0},{17,1},{18,2},{19,3},{20,4},{21,5},{22,6},{23,7},{24,8},{25... | collective-permute-start | bytes 3244040 | tf_op jit(solution)/shard_map/ppermute | solution.py:873
  546.6 12.9 %collective-permute-start.74 = (bf16[528,1024]{1,0:T(8,128)(2,1)}, bf16[528,1024]{1,0:T(8,128)(2,1)S(1)}, u32[]{:S(2)}, u32[]{:S(2)}) collective-permute-start(bf16[528,1024]{1,0:T(8,128)(2,1)} %get-tuple-element.351.late_rest_ref), channel_id=1, source_target_pairs={{0,16},{1,17},{2,18},{3,19},{4,20},{5,21},{6,22},{7,23},{8,24},{9,... | collective-permute-start | bytes 3244040 | tf_op jit(solution)/shard_map/ppermute | solution.py:872
  577.1 16.5 %collective-permute-start.78 = (bf16[528,2432]{1,0:T(8,128)(2,1)}, bf16[528,2432]{1,0:T(8,128)(2,1)S(1)}, u32[]{:S(2)}, u32[]{:S(2)}) collective-permute-start(bf16[528,2432]{1,0:T(8,128)(2,1)} %all-reduce.12.cloned.1.call-done.early_ref), channel_id=1, source_target_pairs={{16,0},{17,1},{18,2},{19,3},{20,4},{21,5},{22,6},{23,7},{24,8},{25... | collective-permute-start | bytes 7704584 | tf_op jit(solution)/shard_map/ppermute | solution.py:877
  (125 other events, 1438.4 us)
Sparse Core Ops, SparseCore 0:
  286.0 159.5 all-reduce.13
  449.8 127.2 all-reduce.11

commit v4 on v3

--- a/solution.py
+++ b/solution.py
@@ -416,7 +416,7 @@
     out_ref[last, out_at : out_at + inner] = jnp.zeros((16, inner), BF16)
 
 
-def add_kernel(inner, channels, own_ref, other_ref, keys_ref, across_ref, gains_ref, out_ref, rest_ref):
+def add_kernel(inner, channels, own_ref, other_ref, keys_ref, gains_ref, out_ref, rest_ref):
     step = 48
     half, cut = own_ref.shape[0] - 16, out_ref.shape[1]
     for at in range(0, own_ref.shape[0], step):
@@ -424,8 +424,7 @@
         total = wide(own_ref[rows, :]) + wide(other_ref[rows, :])
         out_ref[rows, :] = low(total[:, :cut])
         rest_ref[rows, :] = low(total[:, cut:])
-        keys = wide(keys_ref[rows, :]) + wide(across_ref[rows, :])
-        out_ref[rows, inner:channels] = low(total[:, inner:channels] + keys)
+        out_ref[rows, inner:channels] = keys_ref[rows, :]
     rest_ref[half : half + 16, :] = low(gains_ref[...])
 
 
@@ -795,18 +794,10 @@
     rows = jnp.pad(gain_sum[0].reshape(-1, inner), ((0, 16 - features // inner), (0, 0)))
     other = exchange(sent, "section", 1)
     own = products(section)
-    heads = lax.axis_size("head")
-    if heads == 2:
-        keys = exchange(own[:, inner:channels], "head", 1)
-        route = [(i, i ^ 3) for i in range(4)]
-        across = lax.ppermute(sent[:, inner:channels], ("section", "head"), route)
-    else:
-        mine = wide(own[:, inner:channels]) + wide(other[:, inner:channels])
-        keys = low(head_sum(mine) - mine)
-        across = jnp.zeros_like(keys)
+    keys = low(head_sum(wide(own[:, inner:channels]) + wide(other[:, inner:channels])))
     return call(
         functools.partial(add_kernel, inner, channels), [((half + 16, width - inner), BF16), ((half + 16, inner), BF16)],
-        [], 3.0, own, other, keys, across, rows,
+        [], 3.0, own, other, keys, rows,
     )
 
 

time: 617 us -> 616 us (level)
    unnamed x92 -> x98, local copies, waits for them, and re-layouts: 13.7 us -> 13.6 us
  transfers between devices with their start and end apart: 81 -> 79, of which waited for: 35 -> 33; matrix products, arithmetic and copies ran while one was open for 9% -> 8% of each run, Pallas kernels for 19% -> 19%
where the time goes in v4:
time: 616 us; the launch traced here: 605 us
  waiting for transfers between devices  238 us (39%)
  Pallas kernels  132 us (21%)
  starting transfers between devices  128 us (21%)
  other arithmetic  41.9 us (7%)
  local copies, waits for them, and re-layouts  34.9 us (6%)
  between operations  20.4 us (3%)
  matrix products  7.34 us (1%)
    ppermute x42, waiting for transfers between devices, exchange(): return lax.ppermute(block, axis, route)  154 us
    pallas_call x34, Pallas kernels, call(): pl.pallas_call(kernel, out_shape=shapes, in_specs=[pl.BlockSpec(memory_sp...  108 us
    ppermute x31, starting transfers between devices, shifted(): return lax.ppermute(block, axis, route)  79.8 us
    ppermute x31, waiting for transfers between devices, shifted(): return lax.ppermute(block, axis, route)  41.6 us
    ppermute x42, starting transfers between devices, exchange(): return lax.ppermute(block, axis, route)  39.7 us
    psum x1, waiting for transfers between devices, shards(): late = lax.psum(late, 'seq')  24.5 us
    psum x1, waiting for transfers between devices, shards(): early = lax.psum(early, 'seq')  18.4 us
    pallas_call x4, Pallas kernels, products(): pl.pallas_call(product_kernel, grid_spec=pltpu.PrefetchScalarGridSpec(num...  15.8 us
  transfers between devices with their start and end apart: 79, of which 33 were waited for; matrix products, arithmetic and copies ran while one was open for 8% of the time, Pallas kernels for 19%

profile of v4, /device:TPU:0, one launch (start us, length us, event | category | flops | bytes accessed | tf_op | source)
XLA Modules:
  0.0 604.8 jit_solution(2624450561189191483)
XLA Ops:
  8.3 3.0 fusion.14
  17.4 4.8 collective-permute-start.25
  26.1 3.6 broadcast_select_fusion.17
  32.4 3.2 shard_map.299
  37.2 3.1 shard_map.288
  41.6 4.6 collective-permute-start.50
  46.3 3.9 collective-permute-start.29
  51.6 9.8 %collective-permute-start.49 = (bf16[528,128]{1,0:T(8,128)(2,1)S(1)}, bf16[528,128]{1,0:T(8,128)(2,1)S(1)}, u32[]{:S(2)}, u32[]{:S(2)}) collective-permute-start(bf16[528,128]{1,0:T(8,128)(2,1)S(1)} %pad_maximum_fusion.26), channel_id=1, source_target_pairs={{0,4},{2,6},{4,8},{6,10},{8,12},{10,14},{1,5},{3,7},{5,9},{7,11},{... | collective-permute-start | bytes 405512 | tf_op jit(solution)/shard_map/ppermute | solution.py:26
  61.4 2.9 collective-permute-done.49
  64.3 7.2 %collective-permute-start.51 = (bf16[528,128]{1,0:T(8,128)(2,1)S(1)}, bf16[528,128]{1,0:T(8,128)(2,1)S(1)}, u32[]{:S(2)}, u32[]{:S(2)}) collective-permute-start(bf16[528,128]{1,0:T(8,128)(2,1)S(1)} %pad_maximum_fusion.26), channel_id=1, source_target_pairs={{0,12},{2,14},{1,13},{3,15},{16,28},{18,30},{17,29},{19,31}} | collective-permute-start | bytes 405512 | tf_op jit(solution)/shard_map/ppermute | solution.py:26
  93.1 10.8 %collective-permute-done.53.other_ref = bf16[256,1152]{1,0:T(8,128)(2,1)S(1)} collective-permute-done((bf16[256,1152]{1,0:T(8,128)(2,1)S(1)}, bf16[256,1152]{1,0:T(8,128)(2,1)S(1)}, u32[]{:S(2)}, u32[]{:S(2)}) %collective-permute-start.53) | collective-permute-done | bytes 589856 | tf_op jit(solution)/shard_map/ppermute | solution.py:20
  107.0 5.8 collective-permute-done.33.other_ref
  117.4 5.2 collective-permute-start.34
  122.7 3.1 shard_map.302
  126.5 3.1 shard_map.291
  131.3 7.2 %collective-permute-start.58 = (bf16[528,128]{1,0:T(8,128)(2,1)S(1)}, bf16[528,128]{1,0:T(8,128)(2,1)S(1)}, u32[]{:S(2)}, u32[]{:S(2)}) collective-permute-start(bf16[528,128]{1,0:T(8,128)(2,1)S(1)} %pad_maximum_fusion.22), channel_id=1, source_target_pairs={{0,12},{2,14},{1,13},{3,15},{16,28},{18,30},{17,29},{19,31}} | collective-permute-start | bytes 405512 | tf_op jit(solution)/shard_map/ppermute | solution.py:26
  145.0 4.3 collective-permute-start.36
  149.5 3.9 collective-permute-start.59
  162.2 5.9 collective-permute-done.60.other_ref
  170.3 3.8 shard_map.305
  178.3 3.9 shard_map.294
  182.6 6.8 %shard_map.306 = (f32[256,1024]{1,0:T(8,128)S(1)}, f32[256,256]{1,0:T(8,128)S(1)}, f32[256,256]{1,0:T(8,128)S(1)}, f32[8,1024]{1,0:T(8,128)S(1)}) custom-call(f32[256,1408]{1,0:T(8,128)S(1)} %fusion.99.joined_ref, f32[8,1280]{1,0:T(8,128)S(1)} %collective-permute-done.54.before_ref, f32[8,1280]{1,0:T(8,128)S(1)} %slice.617.conv_ref, ...), custom_call_target="tpu_custom_call" | custom-call | flops 1100000000 | bytes 4444160 | tf_op jit(solution)/shard_map/pallas_call | solution.py:446
  190.8 6.7 %shard_map.295 = (f32[256,1024]{1,0:T(8,128)S(1)}, f32[256,256]{1,0:T(8,128)S(1)}, f32[256,256]{1,0:T(8,128)S(1)}, f32[8,1024]{1,0:T(8,128)S(1)}) custom-call(f32[256,1408]{1,0:T(8,128)S(1)} %fusion.95.joined_ref, f32[8,1280]{1,0:T(8,128)S(1)} %collective-permute-done.34.before_ref, f32[8,1280]{1,0:T(8,128)S(1)} %slice.617.conv_ref, ...), custom_call_target="tpu_custom_call" | custom-call | flops 1100000000 | bytes 4444160 | tf_op jit(solution)/shard_map/pallas_call | solution.py:446
  206.3 10.1 %collective-permute-done.62 = bf16[528,128]{1,0:T(8,128)(2,1)S(1)} collective-permute-done((bf16[528,128]{1,0:T(8,128)(2,1)S(1)}, bf16[528,128]{1,0:T(8,128)(2,1)S(1)}, u32[]{:S(2)}, u32[]{:S(2)}) %collective-permute-start.62) | collective-permute-done | bytes 135200 | tf_op jit(solution)/shard_map/ppermute | solution.py:26
  216.9 5.6 collective-permute-done.43
  223.1 4.1 shard_map.307
  228.5 4.1 shard_map.296
  236.4 2.8 collective-permute-done.46.after_ref
  241.2 3.9 shard_map.311
  247.1 3.9 shard_map.310.own_ref
  251.1 8.8 %collective-permute-done.67.other_ref = bf16[256,1024]{1,0:T(8,128)(2,1)S(1)} collective-permute-done((bf16[256,1024]{1,0:T(8,128)(2,1)S(1)}, bf16[256,1024]{1,0:T(8,128)(2,1)S(1)}, u32[]{:S(2)}, u32[]{:S(2)}) %collective-permute-start.67) | collective-permute-done | bytes 524320 | tf_op jit(solution)/shard_map/ppermute | solution.py:20
  263.0 8.1 %collective-permute-done.47.other_ref = bf16[256,1024]{1,0:T(8,128)(2,1)S(1)} collective-permute-done((bf16[256,1024]{1,0:T(8,128)(2,1)S(1)}, bf16[256,1024]{1,0:T(8,128)(2,1)S(1)}, u32[]{:S(2)}, u32[]{:S(2)}) %collective-permute-start.47) | collective-permute-done | bytes 524320 | tf_op jit(solution)/shard_map/ppermute | solution.py:20
  273.8 2.7 collective-permute-done.69
  280.5 135.7 %conditional.2 = (f32[2,256,1024]{2,1,0:T(8,128)}, bf16[528,2432]{1,0:T(8,128)(2,1)}, bf16[528,1024]{1,0:T(8,128)(2,1)}) conditional(s32[]{:T(128)} %bitcast.16, () %tuple.35, (bf16[256,1024]{1,0:T(8,128)(2,1)}, bf16[1024,1024]{1,0:T(8,128)(2,1)}, f32[256,1024]{1,0:T(8,128)}, f32[256,1024]{1,0:T(8,128)}, f32[256,128]{1,0:T(8,128)}, ...), branch_computations={%region_3.4_spmd, %region_4.5_spmd} | conditional | flops 38146641920 | bytes 288266944 | solution.py:840
  280.8 6.6 %branch_1_fun.18 = (f32[256,1024]{1,0:T(8,128)S(1)}, bf16[256,1024]{1,0:T(8,128)(2,1)S(1)}, bf16[256,1024]{1,0:T(8,128)(2,1)S(1)}, bf16[2,512,128]{2,1,0:T(8,128)(2,1)S(1)}, f32[8,1024]{1,0:T(8,128)S(1)}) custom-call(bf16[256,1024]{1,0:T(8,128)(2,1)} %get-tuple-element.107.grad_ref.grad_b, bf16[1024,1024]{1,0:T(8,128)(2,1)} %get-tuple-element.80.w_ref, ...), custom_call_target="tpu_custom_call" | custom-call | flops 4289999872 | bytes 8519680 | tf_op jit(solution)/shard_map/cond/branch_1_fun/pallas_call | solution.py:446
  290.7 2.9 collective-permute-start.13
  293.7 3.7 branch_1_fun.13
  303.3 8.2 %branch_1_fun.14 = (f32[256,1024]{1,0:T(8,128)S(1)}, f32[256,256]{1,0:T(8,128)S(1)}, f32[256,256]{1,0:T(8,128)S(1)}, f32[8,1024]{1,0:T(8,128)S(1)}) custom-call(f32[256,1408]{1,0:T(8,128)} %get-tuple-element.75.joined_ref, f32[8,1280]{1,0:T(8,128)} %get-tuple-element.76.before_ref, f32[8,1280]{1,0:T(8,128)} %get-tuple-element.77.conv_ref, ...), custom_call_target="tpu_custom_call" | custom-call | flops 1100000000 | bytes 4444160 | tf_op jit(solution)/shard_map/cond/branch_1_fun/pallas_call | solution.py:446
  316.1 7.3 %branch_1_fun.19 = (f32[256,1024]{1,0:T(8,128)S(1)}, f32[256,256]{1,0:T(8,128)S(1)}, f32[256,256]{1,0:T(8,128)S(1)}, f32[8,1024]{1,0:T(8,128)S(1)}) custom-call(f32[256,1408]{1,0:T(8,128)S(1)} %copy-done.61, f32[8,1280]{1,0:T(8,128)S(1)} %copy-done.76, f32[8,1280]{1,0:T(8,128)S(1)} %copy-done.81, f32[8,128]{1,0:T(8,128)} %copy-done.89, ...), custom_call_target="tpu_custom_call" | custom-call | flops 1100000000 | bytes 4444160 | tf_op jit(solution)/shard_map/cond/branch_1_fun/pallas_call | solution.py:446
  333.0 3.5 collective-permute-done.8
  338.5 5.7 collective-permute-done.7
  346.9 3.9 collective-permute-done.15
  352.8 4.1 branch_1_fun.15
  360.8 4.1 branch_1_fun.20
  373.0 4.0 branch_1_fun.24
  379.7 3.9 branch_1_fun.23.own_ref
  383.7 8.0 %collective-permute-done.12.other_ref = bf16[256,1024]{1,0:T(8,128)(2,1)S(1)} collective-permute-done((bf16[256,1024]{1,0:T(8,128)(2,1)S(1)}, bf16[256,1024]{1,0:T(8,128)(2,1)S(1)}, u32[]{:S(2)}, u32[]{:S(2)}) %collective-permute-start.12) | collective-permute-done | bytes 524320 | tf_op jit(solution)/shard_map/cond/branch_1_fun/ppermute | solution.py:20
  393.2 9.3 %collective-permute-done.19.other_ref = bf16[256,1024]{1,0:T(8,128)(2,1)S(1)} collective-permute-done((bf16[256,1024]{1,0:T(8,128)(2,1)S(1)}, bf16[256,1024]{1,0:T(8,128)(2,1)S(1)}, u32[]{:S(2)}, u32[]{:S(2)}) %collective-permute-start.19) | collective-permute-done | bytes 524320 | tf_op jit(solution)/shard_map/cond/branch_1_fun/ppermute | solution.py:20
  408.0 5.2 collective-permute-done.21
  413.2 2.7 branch_1_fun.25
  418.6 24.5 %all-reduce.14.cloned.1.call-done = (bf16[528,2432]{1,0:T(8,128)(2,1)}, bf16[528,1024]{1,0:T(8,128)(2,1)}) async-done(((bf16[528,2432]{1,0:T(8,128)(2,1)}, bf16[528,1024]{1,0:T(8,128)(2,1)}), (bf16[528,2432]{1,0:T(8,128)(2,1)}, bf16[528,1024]{1,0:T(8,128)(2,1)})) %all-reduce.14.cloned.1.call-update) | async-done | bytes 3649552 | tf_op jit(solution)/shard_map/psum | solution.py:831
  443.1 3.2 collective-permute-start.71
  448.6 93.8 %conditional.3 = (bf16[528,1024]{1,0:T(8,128)(2,1)}, bf16[8,1024]{1,0:T(8,128)(2,1)S(1)}) conditional(s32[]{:T(128)} %bitcast.16, () %tuple.40, bf16[528,1024]{1,0:T(8,128)(2,1)} %get-tuple-element.352), branch_computations={%region_8.9_spmd, %region_9.10_spmd} | conditional | flops 9224201 | bytes 25022852 | solution.py:845
  452.2 22.7 %collective-permute-done = bf16[528,512]{1,0:T(8,128)(2,1)} collective-permute-done((bf16[528,512]{1,0:T(8,128)(2,1)}, bf16[528,512]{1,0:T(8,128)(2,1)}, u32[]{:S(2)}, u32[]{:S(2)}) %collective-permute-start) | collective-permute-done | bytes 540704 | tf_op jit(solution)/shard_map/cond/branch_1_fun/ppermute | solution.py:20
  478.1 14.7 %collective-permute-done.1 = bf16[528,256]{1,0:T(8,128)(2,1)S(1)} collective-permute-done((bf16[528,256]{1,0:T(8,128)(2,1)}, bf16[528,256]{1,0:T(8,128)(2,1)S(1)}, u32[]{:S(2)}, u32[]{:S(2)}) %collective-permute-start.1) | collective-permute-done | bytes 270368 | tf_op jit(solution)/shard_map/cond/branch_1_fun/ppermute | solution.py:20
  495.9 9.7 %collective-permute-done.2 = bf16[528,128]{1,0:T(8,128)(2,1)S(1)} collective-permute-done((bf16[528,128]{1,0:T(8,128)(2,1)S(1)}, bf16[528,128]{1,0:T(8,128)(2,1)S(1)}, u32[]{:S(2)}, u32[]{:S(2)}) %collective-permute-start.2) | collective-permute-done | bytes 135200 | tf_op jit(solution)/shard_map/cond/branch_1_fun/ppermute | solution.py:20
  505.8 11.9 %collective-permute-done.3 = bf16[528,128]{1,0:T(8,128)(2,1)S(1)} collective-permute-done((bf16[528,128]{1,0:T(8,128)(2,1)S(1)}, bf16[528,128]{1,0:T(8,128)(2,1)S(1)}, u32[]{:S(2)}, u32[]{:S(2)}) %collective-permute-start.3) | collective-permute-done | bytes 135200 | tf_op jit(solution)/shard_map/cond/branch_1_fun/ppermute | solution.py:20
  517.9 10.4 %collective-permute-done.4 = bf16[528,256]{1,0:T(8,128)(2,1)S(1)} collective-permute-done((bf16[528,256]{1,0:T(8,128)(2,1)S(1)}, bf16[528,256]{1,0:T(8,128)(2,1)S(1)}, u32[]{:S(2)}, u32[]{:S(2)}) %collective-permute-start.4) | collective-permute-done | bytes 270368 | tf_op jit(solution)/shard_map/cond/branch_1_fun/ppermute | solution.py:20
  528.5 12.5 %collective-permute-done.5 = bf16[528,512]{1,0:T(8,128)(2,1)S(1)} collective-permute-done((bf16[528,512]{1,0:T(8,128)(2,1)S(1)}, bf16[528,512]{1,0:T(8,128)(2,1)S(1)}, u32[]{:S(2)}, u32[]{:S(2)}) %collective-permute-start.5) | collective-permute-done | bytes 540704 | tf_op jit(solution)/shard_map/cond/branch_1_fun/ppermute | solution.py:20
  543.7 3.2 collective-permute-start.72
  550.2 2.9 broadcast_select_fusion.24
  557.8 18.4 %all-reduce.12.cloned.1.call-done.early_ref = bf16[528,2432]{1,0:T(8,128)(2,1)} async-done(((bf16[528,2432]{1,0:T(8,128)(2,1)}), bf16[528,2432]{1,0:T(8,128)(2,1)}) %all-reduce.12.cloned.1.call-update) | async-done | bytes 2568208 | tf_op jit(solution)/shard_map/psum | solution.py:842
  587.8 4.7 shard_map.313
  592.6 4.2 shard_map.314
  (520 shorter events, 186.1 us)
Async XLA Ops:
  7.2 435.9 %all-reduce.14.cloned.1.call-start = ((), (), s32[]{:S(2)}) async-start(), calls=%async_computation.1 | async-start | bytes 7299072 | tf_op jit(solution)/shard_map/psum | solution.py:831
  11.3 14.8 %collective-permute-start.24 = (bf16[1024,1408]{1,0:T(8,128)(2,1)}, bf16[1024,1408]{1,0:T(8,128)(2,1)}, u32[]{:S(2)}, u32[]{:S(2)}) collective-permute-start(bf16[1024,1408]{1,0:T(8,128)(2,1)} %fusion.14), channel_id=1, source_target_pairs={{0,16},{16,0},{1,17},{17,1},{2,18},{18,2},{3,19},{19,3},{4,20},{20... | collective-permute-start | bytes 8650760 | tf_op jit(solution)/shard_map/ppermute | solution.py:20
  12.1 13.5 %collective-permute-start.23 = (f32[8,3456]{1,0:T(8,128)S(1)}, f32[8,3456]{1,0:T(8,128)S(1)}, u32[]{:S(2)}, u32[]{:S(2)}) collective-permute-start(f32[8,3456]{1,0:T(8,128)S(1)} %select_maximum_fusion), channel_id=1, source_target_pairs={{0,16},{16,0},{1,17},{17,1},{2,18},{18,2},{3,19},{19,3},{4,20},{20... | collective-permute-start | bytes 331784 | tf_op jit(solution)/shard_map/ppermute | solution.py:20
  17.4 8.0 %collective-permute-start.25 = (bf16[16,1024]{1,0:T(8,128)(2,1)S(1)}, bf16[16,1024]{1,0:T(8,128)(2,1)S(1)}, u32[]{:S(2)}, u32[]{:S(2)}) collective-permute-start(bf16[16,1024]{1,0:T(8,128)(2,1)S(1)} %pad_maximum_fusion.27), channel_id=1, source_target_pairs={{0,2},{2,4},{4,6},{6,8},{8,10},{10,12},{12,14},{1,3},{3,5},{5,7},{... | collective-permute-start | bytes 98312 | tf_op jit(solution)/shard_map/ppermute | solution.py:26
  40.9 42.2 %collective-permute-start.31 = (bf16[1024,1024]{1,0:T(8,128)(2,1)S(1)}, bf16[1024,1024]{1,0:T(8,128)(2,1)S(1)}, u32[]{:S(2)}, u32[]{:S(2)}) collective-permute-start(bf16[1024,1024]{1,0:T(8,128)(2,1)S(1)} %bitcast.401), channel_id=1, source_target_pairs={{0,16},{16,0},{1,17},{17,1},{2,18},{18,2},{3,19},{19,3},{4,20},{20... | collective-permute-start | bytes 6291464 | tf_op jit(solution)/shard_map/ppermute | solution.py:20
  41.0 43.2 %collective-permute-start.32 = (bf16[1024,1024]{1,0:T(8,128)(2,1)S(1)}, bf16[1024,1024]{1,0:T(8,128)(2,1)S(1)}, u32[]{:S(2)}, u32[]{:S(2)}) collective-permute-start(bf16[1024,1024]{1,0:T(8,128)(2,1)S(1)} %bitcast.403), channel_id=1, source_target_pairs={{0,16},{16,0},{1,17},{17,1},{2,18},{18,2},{3,19},{19,3},{4,20},{20... | collective-permute-start | bytes 6291464 | tf_op jit(solution)/shard_map/ppermute | solution.py:20
  41.6 10.0 %collective-permute-start.50 = (bf16[528,128]{1,0:T(8,128)(2,1)S(1)}, bf16[528,128]{1,0:T(8,128)(2,1)S(1)}, u32[]{:S(2)}, u32[]{:S(2)}) collective-permute-start(bf16[528,128]{1,0:T(8,128)(2,1)S(1)} %pad_maximum_fusion.26), channel_id=1, source_target_pairs={{0,8},{2,10},{4,12},{6,14},{1,9},{3,11},{5,13},{7,15},{16,24},{18,... | collective-permute-start | bytes 405512 | tf_op jit(solution)/shard_map/ppermute | solution.py:26
  46.3 31.6 %collective-permute-start.29 = (bf16[528,128]{1,0:T(8,128)(2,1)S(1)}, bf16[528,128]{1,0:T(8,128)(2,1)S(1)}, u32[]{:S(2)}, u32[]{:S(2)}) collective-permute-start(bf16[528,128]{1,0:T(8,128)(2,1)S(1)} %pad_maximum_fusion.25), channel_id=1, source_target_pairs={{0,12},{2,14},{1,13},{3,15},{16,28},{18,30},{17,29},{19,31}} | collective-permute-start | bytes 405512 | tf_op jit(solution)/shard_map/ppermute | solution.py:26
  50.2 25.4 %collective-permute-start.28 = (bf16[528,128]{1,0:T(8,128)(2,1)S(1)}, bf16[528,128]{1,0:T(8,128)(2,1)S(1)}, u32[]{:S(2)}, u32[]{:S(2)}) collective-permute-start(bf16[528,128]{1,0:T(8,128)(2,1)S(1)} %pad_maximum_fusion.25), channel_id=1, source_target_pairs={{0,8},{2,10},{4,12},{6,14},{1,9},{3,11},{5,13},{7,15},{16,24},{18,... | collective-permute-start | bytes 405512 | tf_op jit(solution)/shard_map/ppermute | solution.py:26
  51.6 12.7 %collective-permute-start.49 = (bf16[528,128]{1,0:T(8,128)(2,1)S(1)}, bf16[528,128]{1,0:T(8,128)(2,1)S(1)}, u32[]{:S(2)}, u32[]{:S(2)}) collective-permute-start(bf16[528,128]{1,0:T(8,128)(2,1)S(1)} %pad_maximum_fusion.26), channel_id=1, source_target_pairs={{0,4},{2,6},{4,8},{6,10},{8,12},{10,14},{1,5},{3,7},{5,9},{7,11},{... | collective-permute-start | bytes 405512 | tf_op jit(solution)/shard_map/ppermute | solution.py:26
  64.3 9.7 %collective-permute-start.51 = (bf16[528,128]{1,0:T(8,128)(2,1)S(1)}, bf16[528,128]{1,0:T(8,128)(2,1)S(1)}, u32[]{:S(2)}, u32[]{:S(2)}) collective-permute-start(bf16[528,128]{1,0:T(8,128)(2,1)S(1)} %pad_maximum_fusion.26), channel_id=1, source_target_pairs={{0,12},{2,14},{1,13},{3,15},{16,28},{18,30},{17,29},{19,31}} | collective-permute-start | bytes 405512 | tf_op jit(solution)/shard_map/ppermute | solution.py:26
  87.7 16.3 %collective-permute-start.53 = (bf16[256,1152]{1,0:T(8,128)(2,1)S(1)}, bf16[256,1152]{1,0:T(8,128)(2,1)S(1)}, u32[]{:S(2)}, u32[]{:S(2)}) collective-permute-start(bf16[256,1152]{1,0:T(8,128)(2,1)S(1)} %get-tuple-element.308.part_ref), channel_id=1, source_target_pairs={{0,1},{1,0},{2,3},{3,2},{4,5},{5,4},{6,7},{7,6},{8,9},{9,8},{10,11... | collective-permute-start | bytes 1769480 | tf_op jit(solution)/shard_map/ppermute | solution.py:20
  92.6 20.2 %collective-permute-start.33 = (bf16[256,1152]{1,0:T(8,128)(2,1)S(1)}, bf16[256,1152]{1,0:T(8,128)(2,1)S(1)}, u32[]{:S(2)}, u32[]{:S(2)}) collective-permute-start(bf16[256,1152]{1,0:T(8,128)(2,1)S(1)} %get-tuple-element.280.part_ref), channel_id=1, source_target_pairs={{0,1},{1,0},{2,3},{3,2},{4,5},{5,4},{6,7},{7,6},{8,9},{9,8},{10,11... | collective-permute-start | bytes 1769480 | tf_op jit(solution)/shard_map/ppermute | solution.py:20
  115.2 7.5 %collective-permute-start.54 = (f32[8,1280]{1,0:T(8,128)S(1)}, f32[8,1280]{1,0:T(8,128)S(1)}, u32[]{:S(2)}, u32[]{:S(2)}) collective-permute-start(f32[8,1280]{1,0:T(8,128)S(1)} %slice.654), channel_id=1, source_target_pairs={{0,2},{2,4},{4,6},{6,8},{8,10},{10,12},{12,14},{1,3},{3,5},{5,7},{... | collective-permute-start | bytes 122888 | tf_op jit(solution)/shard_map/ppermute | solution.py:26
  117.4 9.1 %collective-permute-start.34 = (f32[8,1280]{1,0:T(8,128)S(1)}, f32[8,1280]{1,0:T(8,128)S(1)}, u32[]{:S(2)}, u32[]{:S(2)}) collective-permute-start(f32[8,1280]{1,0:T(8,128)S(1)} %slice.616), channel_id=1, source_target_pairs={{0,2},{2,4},{4,6},{6,8},{8,10},{10,12},{12,14},{1,3},{3,5},{5,7},{... | collective-permute-start | bytes 122888 | tf_op jit(solution)/shard_map/ppermute | solution.py:26
  129.7 12.6 %collective-permute-start.35 = (bf16[528,128]{1,0:T(8,128)(2,1)S(1)}, bf16[528,128]{1,0:T(8,128)(2,1)S(1)}, u32[]{:S(2)}, u32[]{:S(2)}) collective-permute-start(bf16[528,128]{1,0:T(8,128)(2,1)S(1)} %dynamic-slice_bitcast_fusion.8), channel_id=1, source_target_pairs={{0,2},{2,0},{4,6},{6,4},{8,10},{10,8},{12,14},{14,12},{1,3},{3,1},... | collective-permute-start | bytes 405512 | tf_op jit(solution)/shard_map/ppermute | solution.py:20
  131.3 18.1 %collective-permute-start.58 = (bf16[528,128]{1,0:T(8,128)(2,1)S(1)}, bf16[528,128]{1,0:T(8,128)(2,1)S(1)}, u32[]{:S(2)}, u32[]{:S(2)}) collective-permute-start(bf16[528,128]{1,0:T(8,128)(2,1)S(1)} %pad_maximum_fusion.22), channel_id=1, source_target_pairs={{0,12},{2,14},{1,13},{3,15},{16,28},{18,30},{17,29},{19,31}} | collective-permute-start | bytes 405512 | tf_op jit(solution)/shard_map/ppermute | solution.py:26
  139.8 9.5 %collective-permute-start.56 = (bf16[528,128]{1,0:T(8,128)(2,1)S(1)}, bf16[528,128]{1,0:T(8,128)(2,1)S(1)}, u32[]{:S(2)}, u32[]{:S(2)}) collective-permute-start(bf16[528,128]{1,0:T(8,128)(2,1)S(1)} %pad_maximum_fusion.22), channel_id=1, source_target_pairs={{0,4},{2,6},{4,8},{6,10},{8,12},{10,14},{1,5},{3,7},{5,9},{7,11},{... | collective-permute-start | bytes 405512 | tf_op jit(solution)/shard_map/ppermute | solution.py:26
  142.4 11.0 %collective-permute-start.38 = (bf16[528,128]{1,0:T(8,128)(2,1)S(1)}, bf16[528,128]{1,0:T(8,128)(2,1)S(1)}, u32[]{:S(2)}, u32[]{:S(2)}) collective-permute-start(bf16[528,128]{1,0:T(8,128)(2,1)S(1)} %pad_maximum_fusion.18), channel_id=1, source_target_pairs={{0,12},{2,14},{1,13},{3,15},{16,28},{18,30},{17,29},{19,31}} | collective-permute-start | bytes 405512 | tf_op jit(solution)/shard_map/ppermute | solution.py:26
  143.7 9.7 %collective-permute-start.37 = (bf16[528,128]{1,0:T(8,128)(2,1)S(1)}, bf16[528,128]{1,0:T(8,128)(2,1)S(1)}, u32[]{:S(2)}, u32[]{:S(2)}) collective-permute-start(bf16[528,128]{1,0:T(8,128)(2,1)S(1)} %pad_maximum_fusion.18), channel_id=1, source_target_pairs={{0,8},{2,10},{4,12},{6,14},{1,9},{3,11},{5,13},{7,15},{16,24},{18,... | collective-permute-start | bytes 405512 | tf_op jit(solution)/shard_map/ppermute | solution.py:26
  145.0 8.4 %collective-permute-start.36 = (bf16[528,128]{1,0:T(8,128)(2,1)S(1)}, bf16[528,128]{1,0:T(8,128)(2,1)S(1)}, u32[]{:S(2)}, u32[]{:S(2)}) collective-permute-start(bf16[528,128]{1,0:T(8,128)(2,1)S(1)} %pad_maximum_fusion.18), channel_id=1, source_target_pairs={{0,4},{2,6},{4,8},{6,10},{8,12},{10,14},{1,5},{3,7},{5,9},{7,11},{... | collective-permute-start | bytes 405512 | tf_op jit(solution)/shard_map/ppermute | solution.py:26
  158.2 9.9 %collective-permute-start.60 = (bf16[256,1152]{1,0:T(8,128)(2,1)S(1)}, bf16[256,1152]{1,0:T(8,128)(2,1)S(1)}, u32[]{:S(2)}, u32[]{:S(2)}) collective-permute-start(bf16[256,1152]{1,0:T(8,128)(2,1)S(1)} %get-tuple-element.315.part_ref), channel_id=1, source_target_pairs={{0,1},{1,0},{2,3},{3,2},{4,5},{5,4},{6,7},{7,6},{8,9},{9,8},{10,11... | collective-permute-start | bytes 1769480 | tf_op jit(solution)/shard_map/ppermute | solution.py:20
  161.7 14.5 %collective-permute-start.40 = (bf16[256,1152]{1,0:T(8,128)(2,1)S(1)}, bf16[256,1152]{1,0:T(8,128)(2,1)S(1)}, u32[]{:S(2)}, u32[]{:S(2)}) collective-permute-start(bf16[256,1152]{1,0:T(8,128)(2,1)S(1)} %get-tuple-element.287.part_ref), channel_id=1, source_target_pairs={{0,1},{1,0},{2,3},{3,2},{4,5},{5,4},{6,7},{7,6},{8,9},{9,8},{10,11... | collective-permute-start | bytes 1769480 | tf_op jit(solution)/shard_map/ppermute | solution.py:20
  174.1 15.3 %collective-permute-start.61 = (bf16[512,128]{1,0:T(8,128)(2,1)S(1)}, bf16[512,128]{1,0:T(8,128)(2,1)S(1)}, u32[]{:S(2)}, u32[]{:S(2)}) collective-permute-start(bf16[512,128]{1,0:T(8,128)(2,1)S(1)} %dynamic-slice_bitcast_fusion.10), channel_id=1, source_target_pairs={{0,2},{2,0},{4,6},{6,4},{8,10},{10,8},{12,14},{14,12},{1,3},{3,1},... | collective-permute-start | bytes 393224 | tf_op jit(solution)/shard_map/ppermute | solution.py:20
  182.2 17.9 %collective-permute-start.41 = (bf16[512,128]{1,0:T(8,128)(2,1)S(1)}, bf16[512,128]{1,0:T(8,128)(2,1)S(1)}, u32[]{:S(2)}, u32[]{:S(2)}) collective-permute-start(bf16[512,128]{1,0:T(8,128)(2,1)S(1)} %dynamic-slice_bitcast_fusion.11), channel_id=1, source_target_pairs={{0,2},{2,0},{4,6},{6,4},{8,10},{10,8},{12,14},{14,12},{1,3},{3,1},... | collective-permute-start | bytes 393224 | tf_op jit(solution)/shard_map/ppermute | solution.py:20
  189.5 15.2 %collective-permute-start.63 = (bf16[528,128]{1,0:T(8,128)(2,1)S(1)}, bf16[528,128]{1,0:T(8,128)(2,1)S(1)}, u32[]{:S(2)}, u32[]{:S(2)}) collective-permute-start(bf16[528,128]{1,0:T(8,128)(2,1)S(1)} %pad_maximum_fusion.21), channel_id=1, source_target_pairs={{8,0},{10,2},{12,4},{14,6},{9,1},{11,3},{13,5},{15,7},{24,16},{26,... | collective-permute-start | bytes 405512 | tf_op jit(solution)/shard_map/ppermute | solution.py:26
  197.5 18.8 %collective-permute-start.64 = (bf16[528,128]{1,0:T(8,128)(2,1)S(1)}, bf16[528,128]{1,0:T(8,128)(2,1)S(1)}, u32[]{:S(2)}, u32[]{:S(2)}) collective-permute-start(bf16[528,128]{1,0:T(8,128)(2,1)S(1)} %pad_maximum_fusion.21), channel_id=1, source_target_pairs={{12,0},{14,2},{13,1},{15,3},{28,16},{30,18},{29,17},{31,19}} | collective-permute-start | bytes 405512 | tf_op jit(solution)/shard_map/ppermute | solution.py:26
  198.8 17.5 %collective-permute-start.62 = (bf16[528,128]{1,0:T(8,128)(2,1)S(1)}, bf16[528,128]{1,0:T(8,128)(2,1)S(1)}, u32[]{:S(2)}, u32[]{:S(2)}) collective-permute-start(bf16[528,128]{1,0:T(8,128)(2,1)S(1)} %pad_maximum_fusion.21), channel_id=1, source_target_pairs={{4,0},{6,2},{8,4},{10,6},{12,8},{14,10},{5,1},{7,3},{9,5},{11,7},{... | collective-permute-start | bytes 405512 | tf_op jit(solution)/shard_map/ppermute | solution.py:26
  200.2 22.3 %collective-permute-start.44 = (bf16[528,128]{1,0:T(8,128)(2,1)S(1)}, bf16[528,128]{1,0:T(8,128)(2,1)S(1)}, u32[]{:S(2)}, u32[]{:S(2)}) collective-permute-start(bf16[528,128]{1,0:T(8,128)(2,1)S(1)} %pad_maximum_fusion.17), channel_id=1, source_target_pairs={{12,0},{14,2},{13,1},{15,3},{28,16},{30,18},{29,17},{31,19}} | collective-permute-start | bytes 405512 | tf_op jit(solution)/shard_map/ppermute | solution.py:26
  201.5 21.0 %collective-permute-start.43 = (bf16[528,128]{1,0:T(8,128)(2,1)S(1)}, bf16[528,128]{1,0:T(8,128)(2,1)S(1)}, u32[]{:S(2)}, u32[]{:S(2)}) collective-permute-start(bf16[528,128]{1,0:T(8,128)(2,1)S(1)} %pad_maximum_fusion.17), channel_id=1, source_target_pairs={{8,0},{10,2},{12,4},{14,6},{9,1},{11,3},{13,5},{15,7},{24,16},{26,... | collective-permute-start | bytes 405512 | tf_op jit(solution)/shard_map/ppermute | solution.py:26
  204.7 17.7 %collective-permute-start.42 = (bf16[528,128]{1,0:T(8,128)(2,1)S(1)}, bf16[528,128]{1,0:T(8,128)(2,1)S(1)}, u32[]{:S(2)}, u32[]{:S(2)}) collective-permute-start(bf16[528,128]{1,0:T(8,128)(2,1)S(1)} %pad_maximum_fusion.17), channel_id=1, source_target_pairs={{4,0},{6,2},{8,4},{10,6},{12,8},{14,10},{5,1},{7,3},{9,5},{11,7},{... | collective-permute-start | bytes 405512 | tf_op jit(solution)/shard_map/ppermute | solution.py:26
  227.2 7.2 %collective-permute-start.66 = (f32[8,1280]{1,0:T(8,128)S(1)}, f32[8,1280]{1,0:T(8,128)S(1)}, u32[]{:S(2)}, u32[]{:S(2)}) collective-permute-start(f32[8,1280]{1,0:T(8,128)S(1)} %slice.555), channel_id=1, source_target_pairs={{2,0},{4,2},{6,4},{8,6},{10,8},{12,10},{14,12},{3,1},{5,3},{7,5},{... | collective-permute-start | bytes 122888 | tf_op jit(solution)/shard_map/ppermute | solution.py:26
  245.1 16.2 %collective-permute-start.68 = (bf16[528,3456]{1,0:T(8,128)(2,1)}, bf16[528,3456]{1,0:T(8,128)(2,1)S(1)}, u32[]{:S(2)}, u32[]{:S(2)}) collective-permute-start(bf16[528,3456]{1,0:T(8,128)(2,1)} %shard_map.311), channel_id=1, source_target_pairs={{0,16},{16,0},{1,17},{17,1},{2,18},{18,2},{3,19},{19,3},{4,20},{20... | collective-permute-start | bytes 10948616 | tf_op jit(solution)/shard_map/ppermute | solution.py:20
  245.1 14.7 %collective-permute-start.67 = (bf16[256,1024]{1,0:T(8,128)(2,1)S(1)}, bf16[256,1024]{1,0:T(8,128)(2,1)S(1)}, u32[]{:S(2)}, u32[]{:S(2)}) collective-permute-start(bf16[256,1024]{1,0:T(8,128)(2,1)S(1)} %get-tuple-element.327.part_ref), channel_id=1, source_target_pairs={{0,1},{1,0},{2,3},{3,2},{4,5},{5,4},{6,7},{7,6},{8,9},{9,8},{10,11... | collective-permute-start | bytes 1572872 | tf_op jit(solution)/shard_map/ppermute | solution.py:20
  246.6 24.4 %collective-permute-start.47 = (bf16[256,1024]{1,0:T(8,128)(2,1)S(1)}, bf16[256,1024]{1,0:T(8,128)(2,1)S(1)}, u32[]{:S(2)}, u32[]{:S(2)}) collective-permute-start(bf16[256,1024]{1,0:T(8,128)(2,1)S(1)} %get-tuple-element.299.part_ref), channel_id=1, source_target_pairs={{0,1},{1,0},{2,3},{3,2},{4,5},{5,4},{6,7},{7,6},{8,9},{9,8},{10,11... | collective-permute-start | bytes 1572872 | tf_op jit(solution)/shard_map/ppermute | solution.py:20
  261.4 15.1 %collective-permute-start.69 = (bf16[528,256]{1,0:T(8,128)(2,1)S(1)}, bf16[528,256]{1,0:T(8,128)(2,1)S(1)}, u32[]{:S(2)}, u32[]{:S(2)}) collective-permute-start(bf16[528,256]{1,0:T(8,128)(2,1)S(1)} %add_convert_fusion.6), channel_id=1, source_target_pairs={{0,1},{1,0},{2,3},{3,2},{4,5},{5,4},{6,7},{7,6},{8,9},{9,8},{10,11... | collective-permute-start | bytes 811016 | tf_op jit(solution)/shard_map/ppermute | solution.py:20
  279.8 296.3 %all-reduce.12.cloned.1.call-start = ((), (), s32[]{:S(2)}) async-start(), calls=%async_computation | async-start | bytes 5136384 | tf_op jit(solution)/shard_map/psum | solution.py:842
  290.7 38.0 %collective-permute-start.13 = (bf16[512,128]{1,0:T(8,128)(2,1)}, bf16[512,128]{1,0:T(8,128)(2,1)}, u32[]{:S(2)}, u32[]{:S(2)}) collective-permute-start(bf16[512,128]{1,0:T(8,128)(2,1)} %dynamic-slice_bitcast_fusion), channel_id=1, source_target_pairs={{0,2},{2,0},{4,6},{6,4},{8,10},{10,8},{12,14},{14,12},{1,3},{3,1},... | collective-permute-start | bytes 393224 | tf_op jit(solution)/shard_map/cond/branch_1_fun/ppermute | solution.py:20
  301.4 11.1 %collective-permute-start.6 = (bf16[512,128]{1,0:T(8,128)(2,1)}, bf16[512,128]{1,0:T(8,128)(2,1)}, u32[]{:S(2)}, u32[]{:S(2)}) collective-permute-start(bf16[512,128]{1,0:T(8,128)(2,1)} %dynamic-slice_bitcast_fusion.1), channel_id=1, source_target_pairs={{0,2},{2,0},{4,6},{6,4},{8,10},{10,8},{12,14},{14,12},{1,3},{3,1},... | collective-permute-start | bytes 393224 | tf_op jit(solution)/shard_map/cond/branch_1_fun/ppermute | solution.py:20
  314.3 22.2 %collective-permute-start.8 = (bf16[528,128]{1,0:T(8,128)(2,1)}, bf16[528,128]{1,0:T(8,128)(2,1)}, u32[]{:S(2)}, u32[]{:S(2)}) collective-permute-start(bf16[528,128]{1,0:T(8,128)(2,1)} %pad_maximum_fusion.3), channel_id=1, source_target_pairs={{8,0},{10,2},{12,4},{14,6},{9,1},{11,3},{13,5},{15,7},{24,16},{26,... | collective-permute-start | bytes 405512 | tf_op jit(solution)/shard_map/cond/branch_1_fun/ppermute | solution.py:26
  325.9 18.3 %collective-permute-start.9 = (bf16[528,128]{1,0:T(8,128)(2,1)}, bf16[528,128]{1,0:T(8,128)(2,1)S(1)}, u32[]{:S(2)}, u32[]{:S(2)}) collective-permute-start(bf16[528,128]{1,0:T(8,128)(2,1)} %pad_maximum_fusion.3), channel_id=1, source_target_pairs={{12,0},{14,2},{13,1},{15,3},{28,16},{30,18},{29,17},{31,19}} | collective-permute-start | bytes 405512 | tf_op jit(solution)/shard_map/cond/branch_1_fun/ppermute | solution.py:26
  327.4 16.8 %collective-permute-start.7 = (bf16[528,128]{1,0:T(8,128)(2,1)}, bf16[528,128]{1,0:T(8,128)(2,1)S(1)}, u32[]{:S(2)}, u32[]{:S(2)}) collective-permute-start(bf16[528,128]{1,0:T(8,128)(2,1)} %pad_maximum_fusion.3), channel_id=1, source_target_pairs={{4,0},{6,2},{8,4},{10,6},{12,8},{14,10},{5,1},{7,3},{9,5},{11,7},{... | collective-permute-start | bytes 405512 | tf_op jit(solution)/shard_map/cond/branch_1_fun/ppermute | solution.py:26
  330.4 20.4 %collective-permute-start.16 = (bf16[528,128]{1,0:T(8,128)(2,1)S(1)}, bf16[528,128]{1,0:T(8,128)(2,1)S(1)}, u32[]{:S(2)}, u32[]{:S(2)}) collective-permute-start(bf16[528,128]{1,0:T(8,128)(2,1)S(1)} %pad_maximum_fusion.4), channel_id=1, source_target_pairs={{12,0},{14,2},{13,1},{15,3},{28,16},{30,18},{29,17},{31,19}} | collective-permute-start | bytes 405512 | tf_op jit(solution)/shard_map/cond/branch_1_fun/ppermute | solution.py:26
  331.7 19.1 %collective-permute-start.15 = (bf16[528,128]{1,0:T(8,128)(2,1)S(1)}, bf16[528,128]{1,0:T(8,128)(2,1)S(1)}, u32[]{:S(2)}, u32[]{:S(2)}) collective-permute-start(bf16[528,128]{1,0:T(8,128)(2,1)S(1)} %pad_maximum_fusion.4), channel_id=1, source_target_pairs={{8,0},{10,2},{12,4},{14,6},{9,1},{11,3},{13,5},{15,7},{24,16},{26,... | collective-permute-start | bytes 405512 | tf_op jit(solution)/shard_map/cond/branch_1_fun/ppermute | solution.py:26
  336.5 14.3 %collective-permute-start.14 = (bf16[528,128]{1,0:T(8,128)(2,1)S(1)}, bf16[528,128]{1,0:T(8,128)(2,1)S(1)}, u32[]{:S(2)}, u32[]{:S(2)}) collective-permute-start(bf16[528,128]{1,0:T(8,128)(2,1)S(1)} %pad_maximum_fusion.4), channel_id=1, source_target_pairs={{4,0},{6,2},{8,4},{10,6},{12,8},{14,10},{5,1},{7,3},{9,5},{11,7},{... | collective-permute-start | bytes 405512 | tf_op jit(solution)/shard_map/cond/branch_1_fun/ppermute | solution.py:26
  345.4 7.2 %collective-permute-start.10 = (bf16[512,128]{1,0:T(8,128)(2,1)S(1)}, bf16[512,128]{1,0:T(8,128)(2,1)S(1)}, u32[]{:S(2)}, u32[]{:S(2)}) collective-permute-start(bf16[512,128]{1,0:T(8,128)(2,1)S(1)} %get-tuple-element.398), channel_id=1, source_target_pairs={{0,2},{2,0},{4,6},{6,4},{8,10},{10,8},{12,14},{14,12},{1,3},{3,1},... | collective-permute-start | bytes 393224 | tf_op jit(solution)/shard_map/cond/branch_1_fun/ppermute | solution.py:20
  351.9 8.7 %collective-permute-start.17 = (bf16[512,128]{1,0:T(8,128)(2,1)S(1)}, bf16[512,128]{1,0:T(8,128)(2,1)S(1)}, u32[]{:S(2)}, u32[]{:S(2)}) collective-permute-start(bf16[512,128]{1,0:T(8,128)(2,1)S(1)} %get-tuple-element.401), channel_id=1, source_target_pairs={{0,2},{2,0},{4,6},{6,4},{8,10},{10,8},{12,14},{14,12},{1,3},{3,1},... | collective-permute-start | bytes 393224 | tf_op jit(solution)/shard_map/cond/branch_1_fun/ppermute | solution.py:20
  356.9 9.3 %collective-permute-start.11 = (f32[8,1280]{1,0:T(8,128)S(1)}, f32[8,1280]{1,0:T(8,128)S(1)}, u32[]{:S(2)}, u32[]{:S(2)}) collective-permute-start(f32[8,1280]{1,0:T(8,128)S(1)} %slice.348), channel_id=1, source_target_pairs={{2,0},{4,2},{6,4},{8,6},{10,8},{12,10},{14,12},{3,1},{5,3},{7,5},{... | collective-permute-start | bytes 122888 | tf_op jit(solution)/shard_map/cond/branch_1_fun/ppermute | solution.py:26
  376.9 27.1 %collective-permute-start.20 = (bf16[528,3456]{1,0:T(8,128)(2,1)}, bf16[528,3456]{1,0:T(8,128)(2,1)S(1)}, u32[]{:S(2)}, u32[]{:S(2)}) collective-permute-start(bf16[528,3456]{1,0:T(8,128)(2,1)} %branch_1_fun.24), channel_id=1, source_target_pairs={{0,16},{16,0},{1,17},{17,1},{2,18},{18,2},{3,19},{19,3},{4,20},{20... | collective-permute-start | bytes 10948616 | tf_op jit(solution)/shard_map/cond/branch_1_fun/ppermute | solution.py:20
  376.9 14.7 %collective-permute-start.12 = (bf16[256,1024]{1,0:T(8,128)(2,1)S(1)}, bf16[256,1024]{1,0:T(8,128)(2,1)S(1)}, u32[]{:S(2)}, u32[]{:S(2)}) collective-permute-start(bf16[256,1024]{1,0:T(8,128)(2,1)S(1)} %get-tuple-element.101.part_ref), channel_id=1, source_target_pairs={{0,1},{1,0},{2,3},{3,2},{4,5},{5,4},{6,7},{7,6},{8,9},{9,8},{10,11... | collective-permute-start | bytes 1572872 | tf_op jit(solution)/shard_map/cond/branch_1_fun/ppermute | solution.py:20
  378.4 24.1 %collective-permute-start.19 = (bf16[256,1024]{1,0:T(8,128)(2,1)S(1)}, bf16[256,1024]{1,0:T(8,128)(2,1)S(1)}, u32[]{:S(2)}, u32[]{:S(2)}) collective-permute-start(bf16[256,1024]{1,0:T(8,128)(2,1)S(1)} %get-tuple-element.125.part_ref), channel_id=1, source_target_pairs={{0,1},{1,0},{2,3},{3,2},{4,5},{5,4},{6,7},{7,6},{8,9},{9,8},{10,11... | collective-permute-start | bytes 1572872 | tf_op jit(solution)/shard_map/cond/branch_1_fun/ppermute | solution.py:20
  404.8 8.3 %collective-permute-start.21 = (bf16[528,256]{1,0:T(8,128)(2,1)S(1)}, bf16[528,256]{1,0:T(8,128)(2,1)S(1)}, u32[]{:S(2)}, u32[]{:S(2)}) collective-permute-start(bf16[528,256]{1,0:T(8,128)(2,1)S(1)} %add_convert_fusion.1), channel_id=1, source_target_pairs={{0,1},{1,0},{2,3},{3,2},{4,5},{5,4},{6,7},{7,6},{8,9},{9,8},{10,11... | collective-permute-start | bytes 811016 | tf_op jit(solution)/shard_map/cond/branch_1_fun/ppermute | solution.py:20
  417.9 132.3 %collective-permute-start.75 = (f32[2,256,1024]{2,1,0:T(8,128)}, f32[2,256,1024]{2,1,0:T(8,128)}, u32[]{:S(2)}, u32[]{:S(2)}) collective-permute-start(f32[2,256,1024]{2,1,0:T(8,128)} %fusion.15), channel_id=1, source_target_pairs={{0,16},{16,0},{1,17},{17,1},{2,18},{18,2},{3,19},{19,3},{4,20},{20... | collective-permute-start | bytes 6291464 | tf_op jit(solution)/shard_map/ppermute | solution.py:20
  443.1 133.0 %collective-permute-start.71 = (bf16[528,2432]{1,0:T(8,128)(2,1)}, bf16[528,2432]{1,0:T(8,128)(2,1)}, u32[]{:S(2)}, u32[]{:S(2)}) collective-permute-start(bf16[528,2432]{1,0:T(8,128)(2,1)} %get-tuple-element.369.late_ref), channel_id=1, source_target_pairs={{0,16},{1,17},{2,18},{3,19},{4,20},{5,21},{6,22},{7,23},{8,24},{9,... | collective-permute-start | bytes 7704584 | tf_op jit(solution)/shard_map/ppermute | solution.py:862
  448.6 98.2 %collective-permute-start.74 = (bf16[2,256,1024]{2,1,0:T(8,128)(2,1)}, bf16[2,256,1024]{2,1,0:T(8,128)(2,1)}, u32[]{:S(2)}, u32[]{:S(2)}) collective-permute-start(bf16[2,256,1024]{2,1,0:T(8,128)(2,1)} %broadcast_select_fusion.27), channel_id=1, source_target_pairs={{0,16},{16,0},{1,17},{17,1},{2,18},{18,2},{3,19},{19,3},{4,20},{20... | collective-permute-start | bytes 3145736 | tf_op jit(solution)/shard_map/ppermute | solution.py:20
  450.7 24.1 %collective-permute-start = (bf16[528,512]{1,0:T(8,128)(2,1)}, bf16[528,512]{1,0:T(8,128)(2,1)}, u32[]{:S(2)}, u32[]{:S(2)}) collective-permute-start(bf16[528,512]{1,0:T(8,128)(2,1)} %broadcast_select_fusion.10), channel_id=1, source_target_pairs={{0,2},{2,0},{4,6},{6,4},{8,10},{10,8},{12,14},{14,12},{1,3},{3,1},... | collective-permute-start | bytes 1622024 | tf_op jit(solution)/shard_map/cond/branch_1_fun/ppermute | solution.py:20
  478.0 14.8 %collective-permute-start.1 = (bf16[528,256]{1,0:T(8,128)(2,1)}, bf16[528,256]{1,0:T(8,128)(2,1)S(1)}, u32[]{:S(2)}, u32[]{:S(2)}) collective-permute-start(bf16[528,256]{1,0:T(8,128)(2,1)} %broadcast_select_fusion.13), channel_id=1, source_target_pairs={{0,4},{2,6},{4,0},{6,2},{8,12},{10,14},{12,8},{14,10},{1,5},{3,7},... | collective-permute-start | bytes 811016 | tf_op jit(solution)/shard_map/cond/branch_1_fun/ppermute | solution.py:20
  493.9 11.7 %collective-permute-start.2 = (bf16[528,128]{1,0:T(8,128)(2,1)S(1)}, bf16[528,128]{1,0:T(8,128)(2,1)S(1)}, u32[]{:S(2)}, u32[]{:S(2)}) collective-permute-start(bf16[528,128]{1,0:T(8,128)(2,1)S(1)} %broadcast_select_fusion.16), channel_id=1, source_target_pairs={{0,8},{2,10},{4,12},{6,14},{8,0},{10,2},{12,4},{14,6},{1,9},{3,11}... | collective-permute-start | bytes 405512 | tf_op jit(solution)/shard_map/cond/branch_1_fun/ppermute | solution.py:20
  505.7 12.0 %collective-permute-start.3 = (bf16[528,128]{1,0:T(8,128)(2,1)S(1)}, bf16[528,128]{1,0:T(8,128)(2,1)S(1)}, u32[]{:S(2)}, u32[]{:S(2)}) collective-permute-start(bf16[528,128]{1,0:T(8,128)(2,1)S(1)} %add_convert_fusion.4), channel_id=1, source_target_pairs={{0,8},{2,10},{4,12},{6,14},{8,0},{10,2},{12,4},{14,6},{1,9},{3,11}... | collective-permute-start | bytes 405512 | tf_op jit(solution)/shard_map/cond/branch_1_fun/ppermute | solution.py:20
  517.8 10.5 %collective-permute-start.4 = (bf16[528,256]{1,0:T(8,128)(2,1)S(1)}, bf16[528,256]{1,0:T(8,128)(2,1)S(1)}, u32[]{:S(2)}, u32[]{:S(2)}) collective-permute-start(bf16[528,256]{1,0:T(8,128)(2,1)S(1)} %pad_maximum_fusion.7), channel_id=1, source_target_pairs={{0,4},{2,6},{4,0},{6,2},{8,12},{10,14},{12,8},{14,10},{1,5},{3,7},... | collective-permute-start | bytes 811016 | tf_op jit(solution)/shard_map/cond/branch_1_fun/ppermute | solution.py:20
  528.5 12.6 %collective-permute-start.5 = (bf16[528,512]{1,0:T(8,128)(2,1)S(1)}, bf16[528,512]{1,0:T(8,128)(2,1)S(1)}, u32[]{:S(2)}, u32[]{:S(2)}) collective-permute-start(bf16[528,512]{1,0:T(8,128)(2,1)S(1)} %pad_maximum_fusion.6), channel_id=1, source_target_pairs={{0,2},{2,0},{4,6},{6,4},{8,10},{10,8},{12,14},{14,12},{1,3},{3,1},... | collective-permute-start | bytes 1622024 | tf_op jit(solution)/shard_map/cond/branch_1_fun/ppermute | solution.py:20
  542.4 13.3 %collective-permute-start.73 = (bf16[528,1024]{1,0:T(8,128)(2,1)}, bf16[528,1024]{1,0:T(8,128)(2,1)S(1)}, u32[]{:S(2)}, u32[]{:S(2)}) collective-permute-start(bf16[528,1024]{1,0:T(8,128)(2,1)} %get-tuple-element.353.early_rest_ref), channel_id=1, source_target_pairs={{16,0},{17,1},{18,2},{19,3},{20,4},{21,5},{22,6},{23,7},{24,8},{25... | collective-permute-start | bytes 3244040 | tf_op jit(solution)/shard_map/ppermute | solution.py:864
  543.7 13.0 %collective-permute-start.72 = (bf16[528,1024]{1,0:T(8,128)(2,1)}, bf16[528,1024]{1,0:T(8,128)(2,1)S(1)}, u32[]{:S(2)}, u32[]{:S(2)}) collective-permute-start(bf16[528,1024]{1,0:T(8,128)(2,1)} %get-tuple-element.351.late_rest_ref), channel_id=1, source_target_pairs={{0,16},{1,17},{2,18},{3,19},{4,20},{5,21},{6,22},{7,23},{8,24},{9,... | collective-permute-start | bytes 3244040 | tf_op jit(solution)/shard_map/ppermute | solution.py:863
  576.1 16.5 %collective-permute-start.76 = (bf16[528,2432]{1,0:T(8,128)(2,1)}, bf16[528,2432]{1,0:T(8,128)(2,1)S(1)}, u32[]{:S(2)}, u32[]{:S(2)}) collective-permute-start(bf16[528,2432]{1,0:T(8,128)(2,1)} %all-reduce.12.cloned.1.call-done.early_ref), channel_id=1, source_target_pairs={{16,0},{17,1},{18,2},{19,3},{20,4},{21,5},{22,6},{23,7},{24,8},{25... | collective-permute-start | bytes 7704584 | tf_op jit(solution)/shard_map/ppermute | solution.py:868
  (125 other events, 1441.9 us)
Sparse Core Ops, SparseCore 0:
  279.9 163.1 all-reduce.13
  447.3 128.7 all-reduce.11
